TPU v7x, 256 devices: a whole 4x4x8 slice. The times are simulated.
256 devices in a mesh: gx: 32 (over z_hi, x, core), gz: 8 (over y, z_lo).
Axes of the slice: x: 4, y: 4, z: 8 (z_hi: 4, z_lo: 2; z = z_hi * 2 + z_lo), core: 2. Of those that a mesh axis runs over, the one named last changes fastest.
Arguments:
- velocity: float32 [2048, 16, 1024], P('gx', None, 'gz'), may hold values from -6 to 6
- stress_xz: float32 [2, 2048, 16, 1024], P(None, 'gx', None, 'gz'), may hold values from -6 to 6
- stress_y: float32 [2048, 15, 1024], P('gx', None, 'gz'), may hold values from -6 to 6
- rigidity: float32 [2048, 16, 1024], P('gx', None, 'gz'), may hold values from 0.5 to 2
- buoyancy: float32 [2048, 16, 1024], P('gx', None, 'gz'), may hold values from 0.5 to 2
- sigma_star: float32 [2048, 1024], P('gx', 'gz'), may hold values from 1 to 3
- sigma_zero: float32 [2048, 1024], P('gx', 'gz'), may hold values from 1 to 3
- friction: float32 [2048, 1024], P('gx', 'gz'), may hold values from 0.3 to 0.8
- history: bfloat16 [2, 64, 2048, 1024], P(None, None, 'gx', 'gz'), may hold values from -6 to 6
- kernel: bfloat16 [2, 5, 64, 4096], replicated, may hold values from -0.09375 to 0.09375
- cone: int32 [2, 32, 5, 2], replicated, may hold values from 0 to 64, as said below
Outputs:
- new_velocity: float32 [2048, 16, 1024], P('gx', None, 'gz')
- new_stress_xz: float32 [2, 2048, 16, 1024], P(None, 'gx', None, 'gz')
- new_stress_y: float32 [2048, 15, 1024], P('gx', None, 'gz')
- new_state: float32 [2048, 1024], P('gx', 'gz')
- boundary_traction: float32 [2, 2048, 1024], P(None, 'gx', 'gz')
Inputs may be any that keep to these rules, and one draw needn't show every extreme that they name: cone[s, b, o] holds (first lag, end of lags) for source block b - (o - 2); a pair outside the light cone or whose source lies outside the blocks holds (0, 0); offset 0 always holds (0, 64); offsets -1 and 1 with a source inside the blocks always hold first lag 0; otherwise first lag < end of lags.
All inputs are finite; a program needn't handle non-finite values.
Results may differ from a plain program's by a relative error of at most 0.0022.
Values may be sent and summed in bfloat16 or wider, within the bound.
No kernel may reach another device: no remote copies, remote signals or barrier semaphores. Data moves between devices by JAX's collectives and lax.ppermute only.
A program may use at most 128 MiB of HBM per device.

v0:
```python
import jax
import jax.numpy as jnp
from jax import lax
from jax.sharding import PartitionSpec as P

courant = 0.25
bimaterial = 0.5
slip_ref = 0.2
decay_rate = 0.5
impedance = 0.5


def passed_along(value, axis, steps):
    count = lax.axis_size(axis)
    initial, last = (max(0, -steps), min(count, count - steps))
    return lax.ppermute(value, axis, [(source, source + steps) for source in range(initial, last)])


def padded_2(array, sides, width):
    for axis, dim in sides:
        size, length = (lax.axis_size(axis), array.shape[dim])
        up = [(i, (i + 1) % size) for i in range(size - 1)]
        down = [(j, i) for i, j in up]
        last = lax.slice_in_dim(array, length - width, length, axis=dim)
        initial = lax.slice_in_dim(array, 0, width, axis=dim)
        before = lax.ppermute(last, axis, up)
        after = lax.ppermute(initial, axis, down)
        array = jnp.concatenate([before, array, after], axis=dim)
    return array


def block_term(kernel, surface, index, source_history, first, last):
    lag_index = jnp.arange(source_history.shape[0], dtype=jnp.int32)

    def compute(unused):
        keep = ((lag_index >= first) & (lag_index < last)).astype(jnp.bfloat16)
        masked = source_history * keep[:, None, None]
        flat = masked.reshape(-1, source_history.shape[2])
        return jnp.dot(kernel[surface, index], flat, preferred_element_type=jnp.float32)

    def nothing(unused):
        return jnp.zeros((source_history.shape[1], source_history.shape[2]), jnp.float32)

    return lax.cond(last > first, compute, nothing, 0)


def target_terms(kernel, cone, remotes):
    block = lax.axis_index("gx")
    own_rows = lax.dynamic_index_in_dim(cone, block, 1, keepdims=False)
    totals = []
    for surface in range(2):
        total = jnp.zeros((remotes[0].shape[2], remotes[0].shape[3]), jnp.float32)
        for index in range(len(remotes)):
            total = total + block_term(
                kernel,
                surface,
                index,
                remotes[index][surface],
                own_rows[surface, index, 0],
                own_rows[surface, index, 1],
            )
        totals.append(total)
    return jnp.stack(totals)


def fetch_history(source, offset):
    return passed_along(source, "gx", offset)


def fetch_newest(source, offset):
    return passed_along(source, "gx", offset)


def advance(
    velocity,
    stress_xz,
    stress_y,
    rigidity,
    buoyancy,
    sigma_star,
    sigma_zero,
    friction,
    traction_history,
):
    padded = padded_2(velocity.astype(jnp.bfloat16), (("gx", 0), ("gz", 2)), 1).astype(
        velocity.dtype
    )
    along_x = padded[2:, :, 1:-1] - padded[:-2, :, 1:-1]
    along_z = padded[1:-1, :, 2:] - padded[1:-1, :, :-2]
    stress_x = stress_xz[0] + courant * 0.5 * rigidity * along_x
    stress_z = stress_xz[1] + courant * 0.5 * rigidity * along_z
    face_rigidity = 0.5 * (rigidity[:, 1:] + rigidity[:, :-1])
    trial = stress_y + courant * face_rigidity * (velocity[:, 1:] - velocity[:, :-1])
    fault = velocity.shape[1] // 2 - 1
    slip_rate = velocity[:, fault + 1] - velocity[:, fault]
    normal = sigma_zero + bimaterial * jnp.tanh(stress_x[:, fault + 1] - stress_x[:, fault])
    state = normal + (sigma_star - normal) * jnp.exp(-(jnp.abs(slip_rate) + slip_ref) * decay_rate)
    strength = friction * state
    stress_y_new = trial.at[:, fault].set(jnp.clip(trial[:, fault], -strength, strength))
    bottom = traction_history[0] + impedance * velocity[:, 0]
    top = traction_history[1] - impedance * velocity[:, -1]
    stacked = jnp.stack([stress_x, stress_z])
    spread = padded_2(stacked, (("gx", 1), ("gz", 3)), 1)
    divergence = 0.5 * (spread[0, 2:, :, 1:-1] - spread[0, :-2, :, 1:-1]) + 0.5 * (
        spread[1, 1:-1, :, 2:] - spread[1, 1:-1, :, :-2]
    )
    faces = jnp.concatenate([bottom[:, None], stress_y_new, top[:, None]], axis=1)
    velocity_new = velocity + courant * buoyancy * (divergence + faces[:, 1:] - faces[:, :-1])
    return (velocity_new, stacked, stress_y_new, state, jnp.stack([bottom, top]))


def local(
    velocity,
    stress_xz,
    stress_y,
    rigidity,
    buoyancy,
    sigma_star,
    sigma_zero,
    friction,
    history,
    kernel,
    cone,
):
    count = kernel.shape[1]
    reach = (count - 1) // 2
    remotes = [
        history if index == reach else fetch_history(history, index - reach)
        for index in range(count)
    ]
    traction_one = target_terms(kernel, cone, remotes)
    velocity_one, stress_one, face_one, state_one, bounds_one = advance(
        velocity,
        stress_xz,
        stress_y,
        rigidity,
        buoyancy,
        sigma_star,
        sigma_zero,
        friction,
        traction_one,
    )
    newest = jnp.stack([velocity_one[:, 0], velocity_one[:, -1]]).astype(jnp.bfloat16)
    history_next = jnp.concatenate([newest[:, None], history[:, :-1]], axis=1)
    remotes_next = []
    for index in range(count):
        if index == reach:
            remotes_next.append(history_next)
        else:
            fresh = fetch_newest(newest, index - reach)
            remotes_next.append(jnp.concatenate([fresh[:, None], remotes[index][:, :-1]], axis=1))
    traction_two = target_terms(kernel, cone, remotes_next)
    return advance(
        velocity_one,
        stress_one,
        face_one,
        rigidity,
        buoyancy,
        state_one,
        sigma_zero,
        friction,
        traction_two,
    )


def solution(mesh):
    in_specs = (
        P("gx", None, "gz"),
        P(None, "gx", None, "gz"),
        P("gx", None, "gz"),
        P("gx", None, "gz"),
        P("gx", None, "gz"),
        P("gx", "gz"),
        P("gx", "gz"),
        P("gx", "gz"),
        P(None, None, "gx", "gz"),
        P(),
        P(),
    )
    out_specs = (
        P("gx", None, "gz"),
        P(None, "gx", None, "gz"),
        P("gx", None, "gz"),
        P("gx", "gz"),
        P(None, "gx", "gz"),
    )
    return jax.shard_map(local, mesh=mesh, in_specs=in_specs, out_specs=out_specs, check_vma=False)
```

profile of v0, /device:TPU:86, one launch (start us, length us, event | category | flops | bytes accessed | tf_op | source)
XLA Modules:
  0.0 400.3 jit_solution(7583275244964858752)
XLA Ops:
  2.0 1.9 collective-permute-start
  3.9 3.6 collective-permute-start.1
  7.6 1.9 collective-permute-start.9
  9.5 4.7 %collective-permute-start.10 = (bf16[2,64,64,128]{3,2,1,0:T(8,128)(2,1)}, bf16[2,64,64,128]{3,2,1,0:T(8,128)(2,1)}, u32[]{:S(2)}, u32[]{:S(2)}) collective-permute-start(bf16[2,64,64,128]{3,2,1,0:T(8,128)(2,1)} %param.63), channel_id=1, source_target_pairs={{0,8},{8,16},{16,24},{24,32},{32,40},{40,48},{48,56},{56,64},{64,7... | collective-permute-start | bytes 6291464 | tf_op jit(solution)/shard_map/ppermute | solution.py:16
  14.2 8.2 %collective-permute-start.11 = (bf16[2,64,64,128]{3,2,1,0:T(8,128)(2,1)}, bf16[2,64,64,128]{3,2,1,0:T(8,128)(2,1)}, u32[]{:S(2)}, u32[]{:S(2)}) collective-permute-start(bf16[2,64,64,128]{3,2,1,0:T(8,128)(2,1)} %param.63), channel_id=1, source_target_pairs={{0,16},{8,24},{16,32},{24,40},{32,48},{40,56},{48,64},{56,72},{64,... | collective-permute-start | bytes 6291464 | tf_op jit(solution)/shard_map/ppermute | solution.py:16
  22.7 3.1 collective-permute-start.2
  25.8 3.8 collective-permute-start.3
  29.7 51.6 %collective-permute-done.2 = bf16[66,16,1]{2,0,1:T(8,128)(2,1)S(1)} collective-permute-done((bf16[66,16,1]{2,0,1:T(8,128)(2,1)S(1)}, bf16[66,16,1]{2,0,1:T(8,128)(2,1)S(1)}, u32[]{:S(2)}, u32[]{:S(2)}) %collective-permute-start.2) | collective-permute-done | bytes 2144 | tf_op jit(solution)/shard_map/ppermute | solution.py:26
  81.3 1.9 collective-permute-start.8
  83.2 4.4 %collective-permute-done.3 = bf16[66,16,1]{2,0,1:T(8,128)(2,1)S(1)} collective-permute-done((bf16[66,16,1]{2,0,1:T(8,128)(2,1)S(1)}, bf16[66,16,1]{2,0,1:T(8,128)(2,1)S(1)}, u32[]{:S(2)}, u32[]{:S(2)}) %collective-permute-start.3) | collective-permute-done | bytes 2144 | tf_op jit(solution)/shard_map/ppermute | solution.py:27
  88.1 1.7 fusion.64
  90.4 1.9 collective-permute-start.4
  92.6 81.2 %collective-permute-done.4 = f32[2,1,16,128]{3,2,1,0:T(8,128)S(1)} collective-permute-done((f32[2,1,16,128]{3,2,1,0:T(8,128)S(1)}, f32[2,1,16,128]{3,2,1,0:T(8,128)S(1)}, u32[]{:S(2)}, u32[]{:S(2)}) %collective-permute-start.4) | collective-permute-done | bytes 16416 | tf_op jit(solution)/shard_map/ppermute | solution.py:27
  173.8 25.5 %collective-permute-start.5 = (f32[2,1,16,128]{3,2,1,0:T(8,128)S(1)}, f32[2,1,16,128]{3,2,1,0:T(8,128)S(1)}, u32[]{:S(2)}, u32[]{:S(2)}) collective-permute-start(f32[2,1,16,128]{3,2,1,0:T(8,128)S(1)} %get-tuple-element.500), channel_id=1, source_target_pairs={{0,8},{8,16},{16,24},{24,32},{32,40},{40,48},{48,56},{56,64},{64,7... | collective-permute-start | bytes 49160 | tf_op jit(solution)/shard_map/ppermute | solution.py:26
  200.8 3.0 slice.533
  216.9 4.1 %conditional.22 = (f32[64,128]{1,0:T(8,128)S(1)}) conditional(s32[]{:T(128)} %convert_element_type.124, () %tuple.140, (bf16[2,64,64,128]{3,2,1,0:T(8,128)(2,1)}, s32[]{:T(128)}, s32[64]{0:T(128)S(1)}, s32[]{:T(128)}, s32[64]{0:T(128)S(1)}, /*index=5*/bf16[2,5,64,4096]{3,2,1,0:T(8,128)(2,1)}) %tuple.141), branch_computations={%region_4.5_spmd, %region_5.6_spmd} | conditional | flops 67633408 | bytes 3703568 | solution.py:44
  221.0 4.0 %conditional.27 = (f32[64,128]{1,0:T(8,128)S(1)}) conditional(s32[]{:T(128)} %convert_element_type.129, () %tuple.150, (bf16[2,64,64,128]{3,2,1,0:T(8,128)(2,1)}, s32[]{:T(128)}, s32[64]{0:T(128)S(1)}, s32[]{:T(128)}, s32[64]{0:T(128)S(1)}, /*index=5*/bf16[2,5,64,4096]{3,2,1,0:T(8,128)(2,1)}) %tuple.151), branch_computations={%region_14.15_spmd, %region_15.16_spmd} | conditional | flops 67633408 | bytes 3703568 | solution.py:44
  225.1 1.7 fusion.106
  226.8 1.7 copy.115
  228.5 2.1 collective-permute-start.6
  230.6 2.0 fusion.68
  232.6 1.7 copy.117
  234.3 3.9 collective-permute-start.7
  239.6 1.5 copy.116
  241.1 1.6 copy.118
  242.7 4.0 %conditional.21 = (f32[64,128]{1,0:T(8,128)S(1)}) conditional(s32[]{:T(128)} %convert_element_type.123, () %tuple.138, (bf16[2,64,64,128]{3,2,1,0:T(8,128)(2,1)}, s32[]{:T(128)}, s32[64]{0:T(128)S(1)}, s32[]{:T(128)}, s32[64]{0:T(128)S(1)}, /*index=5*/bf16[2,5,64,4096]{3,2,1,0:T(8,128)(2,1)}) %tuple.139), branch_computations={%region_2.3_spmd, %region_3.4_spmd} | conditional | flops 67633408 | bytes 3703568 | solution.py:44
  246.8 4.1 %conditional.23 = (f32[64,128]{1,0:T(8,128)S(1)}) conditional(s32[]{:T(128)} %convert_element_type.125, () %tuple.142, (bf16[2,64,64,128]{3,2,1,0:T(8,128)(2,1)}, s32[]{:T(128)}, s32[64]{0:T(128)S(1)}, s32[]{:T(128)}, s32[64]{0:T(128)S(1)}, /*index=5*/bf16[2,5,64,4096]{3,2,1,0:T(8,128)(2,1)}) %tuple.143), branch_computations={%region_6.7_spmd, %region_7.8_spmd} | conditional | flops 67633408 | bytes 3703568 | solution.py:44
  250.9 4.1 %conditional.24 = (f32[64,128]{1,0:T(8,128)S(1)}) conditional(s32[]{:T(128)} %convert_element_type.126, () %tuple.144, (bf16[2,64,64,128]{3,2,1,0:T(8,128)(2,1)}, s32[]{:T(128)}, s32[64]{0:T(128)S(1)}, s32[]{:T(128)}, s32[64]{0:T(128)S(1)}, /*index=5*/bf16[2,5,64,4096]{3,2,1,0:T(8,128)(2,1)}) %tuple.145), branch_computations={%region_8.9_spmd, %region_9.10_spmd} | conditional | flops 67633408 | bytes 3703568 | solution.py:44
  255.1 4.1 %conditional.26 = (f32[64,128]{1,0:T(8,128)S(1)}) conditional(s32[]{:T(128)} %convert_element_type.128, () %tuple.148, (bf16[2,64,64,128]{3,2,1,0:T(8,128)(2,1)}, s32[]{:T(128)}, s32[64]{0:T(128)S(1)}, s32[]{:T(128)}, s32[64]{0:T(128)S(1)}, /*index=5*/bf16[2,5,64,4096]{3,2,1,0:T(8,128)(2,1)}) %tuple.149), branch_computations={%region_12.13_spmd, %region_13.14_spmd} | conditional | flops 67633408 | bytes 3703568 | solution.py:44
  259.2 4.1 %conditional.28 = (f32[64,128]{1,0:T(8,128)S(1)}) conditional(s32[]{:T(128)} %convert_element_type.130, () %tuple.152, (bf16[2,64,64,128]{3,2,1,0:T(8,128)(2,1)}, s32[]{:T(128)}, s32[64]{0:T(128)S(1)}, s32[]{:T(128)}, s32[64]{0:T(128)S(1)}, /*index=5*/bf16[2,5,64,4096]{3,2,1,0:T(8,128)(2,1)}) %tuple.153), branch_computations={%region_16.17_spmd, %region_17.18_spmd} | conditional | flops 67633408 | bytes 3703568 | solution.py:44
  263.3 4.1 %conditional.20 = (f32[64,128]{1,0:T(8,128)S(1)}) conditional(s32[]{:T(128)} %convert_element_type.122, () %tuple.136, (bf16[2,64,64,128]{3,2,1,0:T(8,128)(2,1)}, s32[]{:T(128)}, s32[64]{0:T(128)S(1)}, s32[]{:T(128)}, s32[64]{0:T(128)S(1)}, /*index=5*/bf16[2,5,64,4096]{3,2,1,0:T(8,128)(2,1)}) %tuple.137), branch_computations={%region_0.1_spmd, %region_1.2_spmd} | conditional | flops 67633408 | bytes 3703568 | solution.py:44
  269.0 2.0 fusion.102
  272.4 1.9 collective-permute-start.20
  274.3 1.9 collective-permute-start.21
  276.2 2.4 collective-permute-start.22
  278.7 7.8 %collective-permute-start.12 = (bf16[1,16,128]{2,1,0:T(8,128)(2,1)S(1)}, bf16[1,16,128]{2,1,0:T(8,128)(2,1)S(1)}, u32[]{:S(2)}, u32[]{:S(2)}) collective-permute-start(bf16[1,16,128]{2,1,0:T(8,128)(2,1)S(1)} %get-tuple-element.520), channel_id=1, source_target_pairs={{0,8},{8,16},{16,24},{24,32},{32,40},{40,48},{48,56},{56,64},{64,7... | collective-permute-start | bytes 12296 | tf_op jit(solution)/shard_map/ppermute | solution.py:26
  286.5 2.1 collective-permute-start.13
  291.2 2.7 collective-permute-start.14
  293.9 4.1 %collective-permute-start.15 = (bf16[66,16,1]{2,1,0:T(8,128)(2,1)S(1)}, bf16[66,16,1]{2,1,0:T(8,128)(2,1)}, u32[]{:S(2)}, u32[]{:S(2)}) collective-permute-start(bf16[66,16,1]{2,1,0:T(8,128)(2,1)S(1)} %get-tuple-element.519), channel_id=1, source_target_pairs={{1,0},{2,1},{3,2},{4,3},{5,4},{6,5},{7,6},{9,8},{10,9},{11,10},{12... | collective-permute-start | bytes 6344 | tf_op jit(solution)/shard_map/ppermute | solution.py:27
  299.7 4.0 %conditional.37 = (f32[64,128]{1,0:T(8,128)S(1)}) conditional(s32[]{:T(128)} %convert_element_type.129, () %tuple.170, (bf16[2,64,64,128]{3,2,1,0:T(8,128)(2,1)}, s32[]{:T(128)}, s32[64]{0:T(128)S(1)}, s32[]{:T(128)}, s32[64]{0:T(128)S(1)}, /*index=5*/bf16[2,5,64,4096]{3,2,1,0:T(8,128)(2,1)}) %tuple.171), branch_computations={%region_34.35_spmd, %region_35.36_spmd} | conditional | flops 67633408 | bytes 3703568 | solution.py:44
  303.8 4.1 %conditional.32 = (f32[64,128]{1,0:T(8,128)S(1)}) conditional(s32[]{:T(128)} %convert_element_type.124, () %tuple.160, (bf16[2,64,64,128]{3,2,1,0:T(8,128)(2,1)}, s32[]{:T(128)}, s32[64]{0:T(128)S(1)}, s32[]{:T(128)}, s32[64]{0:T(128)S(1)}, /*index=5*/bf16[2,5,64,4096]{3,2,1,0:T(8,128)(2,1)}) %tuple.161), branch_computations={%region_24.25_spmd, %region_25.26_spmd} | conditional | flops 67633408 | bytes 3703568 | solution.py:44
  307.9 3.0 slice.602
  310.9 3.1 slice.603
  314.0 3.0 slice.604
  317.1 3.2 slice.605
  322.7 3.0 collective-permute-start.16
  325.8 6.7 %collective-permute-start.17 = (f32[2,1,16,128]{3,2,1,0:T(8,128)S(1)}, f32[2,1,16,128]{3,2,1,0:T(8,128)S(1)}, u32[]{:S(2)}, u32[]{:S(2)}) collective-permute-start(f32[2,1,16,128]{3,2,1,0:T(8,128)S(1)} %get-tuple-element.498), channel_id=1, source_target_pairs={{0,8},{8,16},{16,24},{24,32},{32,40},{40,48},{48,56},{56,64},{64,7... | collective-permute-start | bytes 49160 | tf_op jit(solution)/shard_map/ppermute | solution.py:26
  334.7 1.7 copy.134
  336.4 2.2 collective-permute-start.18
  339.1 3.6 collective-permute-start.19
  344.9 14.3 %collective-permute-start.23 = (bf16[2,64,128]{2,1,0:T(8,128)(2,1)}, bf16[2,64,128]{2,1,0:T(8,128)(2,1)S(1)}, u32[]{:S(2)}, u32[]{:S(2)}) collective-permute-start(bf16[2,64,128]{2,1,0:T(8,128)(2,1)} %pad_maximum_fusion.33), channel_id=1, source_target_pairs={{0,16},{8,24},{16,32},{24,40},{32,48},{40,56},{48,64},{56,72},{64,... | collective-permute-start | bytes 98312 | tf_op jit(solution)/shard_map/ppermute | solution.py:16
  359.8 1.6 copy.137
  361.4 3.2 pad_maximum_fusion
  364.6 2.5 pad_maximum_fusion.1
  367.1 2.4 pad_maximum_fusion.3
  369.6 1.5 pad_maximum_fusion.4
  371.1 4.1 %conditional.36 = (f32[64,128]{1,0:T(8,128)S(1)}) conditional(s32[]{:T(128)} %convert_element_type.128, () %tuple.168, (bf16[2,64,64,128]{3,2,1,0:T(8,128)(2,1)}, s32[]{:T(128)}, s32[64]{0:T(128)S(1)}, s32[]{:T(128)}, s32[64]{0:T(128)S(1)}, /*index=5*/bf16[2,5,64,4096]{3,2,1,0:T(8,128)(2,1)}) %tuple.169), branch_computations={%region_32.33_spmd, %region_33.34_spmd} | conditional | flops 67633408 | bytes 3703568 | solution.py:44
  375.2 4.1 %conditional.38 = (f32[64,128]{1,0:T(8,128)S(1)}) conditional(s32[]{:T(128)} %convert_element_type.130, () %tuple.172, (bf16[2,64,64,128]{3,2,1,0:T(8,128)(2,1)}, s32[]{:T(128)}, s32[64]{0:T(128)S(1)}, s32[]{:T(128)}, s32[64]{0:T(128)S(1)}, /*index=5*/bf16[2,5,64,4096]{3,2,1,0:T(8,128)(2,1)}) %tuple.173), branch_computations={%region_36.37_spmd, %region_37.38_spmd} | conditional | flops 67633408 | bytes 3703568 | solution.py:44
  379.3 4.1 %conditional.31 = (f32[64,128]{1,0:T(8,128)S(1)}) conditional(s32[]{:T(128)} %convert_element_type.123, () %tuple.158, (bf16[2,64,64,128]{3,2,1,0:T(8,128)(2,1)}, s32[]{:T(128)}, s32[64]{0:T(128)S(1)}, s32[]{:T(128)}, s32[64]{0:T(128)S(1)}, /*index=5*/bf16[2,5,64,4096]{3,2,1,0:T(8,128)(2,1)}) %tuple.159), branch_computations={%region_22.23_spmd, %region_23.24_spmd} | conditional | flops 67633408 | bytes 3703568 | solution.py:44
  383.4 4.1 %conditional.30 = (f32[64,128]{1,0:T(8,128)S(1)}) conditional(s32[]{:T(128)} %convert_element_type.122, () %tuple.156, (bf16[2,64,64,128]{3,2,1,0:T(8,128)(2,1)}, s32[]{:T(128)}, s32[64]{0:T(128)S(1)}, s32[]{:T(128)}, s32[64]{0:T(128)S(1)}, /*index=5*/bf16[2,5,64,4096]{3,2,1,0:T(8,128)(2,1)}) %tuple.157), branch_computations={%region_20.21_spmd, %region_21.22_spmd} | conditional | flops 67633408 | bytes 3703568 | solution.py:44
  387.5 4.1 %conditional.33 = (f32[64,128]{1,0:T(8,128)S(1)}) conditional(s32[]{:T(128)} %convert_element_type.125, () %tuple.162, (bf16[2,64,64,128]{3,2,1,0:T(8,128)(2,1)}, s32[]{:T(128)}, s32[64]{0:T(128)S(1)}, s32[]{:T(128)}, s32[64]{0:T(128)S(1)}, /*index=5*/bf16[2,5,64,4096]{3,2,1,0:T(8,128)(2,1)}) %tuple.163), branch_computations={%region_26.27_spmd, %region_27.28_spmd} | conditional | flops 67633408 | bytes 3703568 | solution.py:44
  391.6 4.7 %conditional.34 = (f32[64,128]{1,0:T(8,128)}) conditional(s32[]{:T(128)} %convert_element_type.126, () %tuple.164, (bf16[2,64,64,128]{3,2,1,0:T(8,128)(2,1)}, s32[]{:T(128)}, s32[64]{0:T(128)S(1)}, s32[]{:T(128)}, s32[64]{0:T(128)S(1)}, /*index=5*/bf16[2,5,64,4096]{3,2,1,0:T(8,128)(2,1)}) %tuple.165), branch_computations={%region_28.29_spmd, %region_29.30_spmd} | conditional | flops 67633408 | bytes 3703568 | solution.py:44
  394.3 2.0 convolution_bitcast_fusion.14
  397.7 2.6 fusion.47
  (202 shorter events, 86.0 us)
Async XLA Ops:
  0.6 91.7 %copy-start = (s32[2,32,5,2]{1,3,2,0:T(2,128)S(1)}, s32[2,32,5,2]{1,3,2,0:T(2,128)}, u32[]{:S(2)}) copy-start(s32[2,32,5,2]{1,3,2,0:T(2,128)} %param.65) | copy-start | bytes 7684
  0.6 29.0 %copy-start.13 = (f32[2,64,16,128]{3,2,1,0:T(8,128)S(1)}, f32[2,64,16,128]{3,2,1,0:T(8,128)}, u32[]{:S(2)}) copy-start(f32[2,64,16,128]{3,2,1,0:T(8,128)} %param.56) | copy-start | bytes 3145732
  2.0 20.5 %collective-permute-start = (bf16[1,16,128]{2,0,1:T(2,128)(2,1)S(1)}, bf16[1,16,128]{2,0,1:T(2,128)(2,1)S(1)}, u32[]{:S(2)}, u32[]{:S(2)}) collective-permute-start(bf16[1,16,128]{2,0,1:T(2,128)(2,1)S(1)} %get-tuple-element.522), channel_id=1, source_target_pairs={{0,8},{8,16},{16,24},{24,32},{32,40},{40,48},{48,56},{56,64},{64,7... | collective-permute-start | bytes 12296 | tf_op jit(solution)/shard_map/ppermute | solution.py:26
  3.9 18.5 %collective-permute-start.1 = (bf16[1,16,128]{2,0,1:T(2,128)(2,1)S(1)}, bf16[1,16,128]{2,0,1:T(2,128)(2,1)S(1)}, u32[]{:S(2)}, u32[]{:S(2)}) collective-permute-start(bf16[1,16,128]{2,0,1:T(2,128)(2,1)S(1)} %get-tuple-element.523), channel_id=1, source_target_pairs={{8,0},{16,8},{24,16},{32,24},{40,32},{48,40},{56,48},{64,56},{72,6... | collective-permute-start | bytes 12296 | tf_op jit(solution)/shard_map/ppermute | solution.py:27
  7.6 235.1 %collective-permute-start.9 = (bf16[2,64,64,128]{3,2,1,0:T(8,128)(2,1)}, bf16[2,64,64,128]{3,2,1,0:T(8,128)(2,1)}, u32[]{:S(2)}, u32[]{:S(2)}) collective-permute-start(bf16[2,64,64,128]{3,2,1,0:T(8,128)(2,1)} %param.63), channel_id=1, source_target_pairs={{8,0},{16,8},{24,16},{32,24},{40,32},{48,40},{56,48},{64,56},{72,6... | collective-permute-start | bytes 6291464 | tf_op jit(solution)/shard_map/ppermute | solution.py:16
  9.5 237.3 %collective-permute-start.10 = (bf16[2,64,64,128]{3,2,1,0:T(8,128)(2,1)}, bf16[2,64,64,128]{3,2,1,0:T(8,128)(2,1)}, u32[]{:S(2)}, u32[]{:S(2)}) collective-permute-start(bf16[2,64,64,128]{3,2,1,0:T(8,128)(2,1)} %param.63), channel_id=1, source_target_pairs={{0,8},{8,16},{16,24},{24,32},{32,40},{40,48},{48,56},{56,64},{64,7... | collective-permute-start | bytes 6291464 | tf_op jit(solution)/shard_map/ppermute | solution.py:16
  14.2 236.7 %collective-permute-start.11 = (bf16[2,64,64,128]{3,2,1,0:T(8,128)(2,1)}, bf16[2,64,64,128]{3,2,1,0:T(8,128)(2,1)}, u32[]{:S(2)}, u32[]{:S(2)}) collective-permute-start(bf16[2,64,64,128]{3,2,1,0:T(8,128)(2,1)} %param.63), channel_id=1, source_target_pairs={{0,16},{8,24},{16,32},{24,40},{32,48},{40,56},{48,64},{56,72},{64,... | collective-permute-start | bytes 6291464 | tf_op jit(solution)/shard_map/ppermute | solution.py:16
  22.7 65.4 %copy-start.14 = (f32[64,16,128]{2,1,0:T(8,128)S(1)}, f32[64,16,128]{2,1,0:T(8,128)}, u32[]{:S(2)}) copy-start(f32[64,16,128]{2,1,0:T(8,128)} %param.58) | copy-start | bytes 1572868
  22.7 58.6 %collective-permute-start.2 = (bf16[66,16,1]{2,0,1:T(8,128)(2,1)S(1)}, bf16[66,16,1]{2,0,1:T(8,128)(2,1)S(1)}, u32[]{:S(2)}, u32[]{:S(2)}) collective-permute-start(bf16[66,16,1]{2,0,1:T(8,128)(2,1)S(1)} %get-tuple-element.516), channel_id=1, source_target_pairs={{0,1},{1,2},{2,3},{3,4},{4,5},{5,6},{6,7},{8,9},{9,10},{10,11},{11... | collective-permute-start | bytes 6344 | tf_op jit(solution)/shard_map/ppermute | solution.py:26
  25.8 61.8 %collective-permute-start.3 = (bf16[66,16,1]{2,0,1:T(8,128)(2,1)S(1)}, bf16[66,16,1]{2,0,1:T(8,128)(2,1)S(1)}, u32[]{:S(2)}, u32[]{:S(2)}) collective-permute-start(bf16[66,16,1]{2,0,1:T(8,128)(2,1)S(1)} %get-tuple-element.517), channel_id=1, source_target_pairs={{1,0},{2,1},{3,2},{4,3},{5,4},{6,5},{7,6},{9,8},{10,9},{11,10},{12... | collective-permute-start | bytes 6344 | tf_op jit(solution)/shard_map/ppermute | solution.py:27
  81.3 173.7 %collective-permute-start.8 = (bf16[2,64,64,128]{3,2,1,0:T(8,128)(2,1)}, bf16[2,64,64,128]{3,2,1,0:T(8,128)(2,1)}, u32[]{:S(2)}, u32[]{:S(2)}) collective-permute-start(bf16[2,64,64,128]{3,2,1,0:T(8,128)(2,1)} %param.63), channel_id=1, source_target_pairs={{16,0},{24,8},{32,16},{40,24},{48,32},{56,40},{64,48},{72,56},{80,... | collective-permute-start | bytes 6291464 | tf_op jit(solution)/shard_map/ppermute | solution.py:16
  89.8 110.8 %copy-start.7 = (f32[64,16,128]{2,0,1:T(8,128)}, f32[64,16,128]{2,0,1:T(8,128)S(1)}, u32[]{:S(2)}) copy-start(f32[64,16,128]{2,0,1:T(8,128)S(1)} %get-tuple-element.490) | copy-start | bytes 1572868
  89.8 110.8 %copy-start.6 = (f32[64,16,128]{2,1,0:T(8,128)S(1)}, f32[64,16,128]{2,1,0:T(8,128)}, u32[]{:S(2)}) copy-start(f32[64,16,128]{2,1,0:T(8,128)} %param.55) | copy-start | bytes 1572868
  90.4 83.4 %collective-permute-start.4 = (f32[2,1,16,128]{3,2,1,0:T(8,128)S(1)}, f32[2,1,16,128]{3,2,1,0:T(8,128)S(1)}, u32[]{:S(2)}, u32[]{:S(2)}) collective-permute-start(f32[2,1,16,128]{3,2,1,0:T(8,128)S(1)} %get-tuple-element.501), channel_id=1, source_target_pairs={{8,0},{16,8},{24,16},{32,24},{40,32},{48,40},{56,48},{64,56},{72,6... | collective-permute-start | bytes 49160 | tf_op jit(solution)/shard_map/ppermute | solution.py:27
  173.8 51.2 %copy-start.24 = (f32[2,1,16,128]{3,2,1,0:T(8,128)}, f32[2,1,16,128]{3,2,1,0:T(8,128)S(1)}, u32[]{:S(2)}) copy-start(f32[2,1,16,128]{3,2,1,0:T(8,128)S(1)} %collective-permute-done.4) | copy-start | bytes 49156
  173.8 51.2 %collective-permute-start.5 = (f32[2,1,16,128]{3,2,1,0:T(8,128)S(1)}, f32[2,1,16,128]{3,2,1,0:T(8,128)S(1)}, u32[]{:S(2)}, u32[]{:S(2)}) collective-permute-start(f32[2,1,16,128]{3,2,1,0:T(8,128)S(1)} %get-tuple-element.500), channel_id=1, source_target_pairs={{0,8},{8,16},{16,24},{24,32},{32,40},{40,48},{48,56},{56,64},{64,7... | collective-permute-start | bytes 49160 | tf_op jit(solution)/shard_map/ppermute | solution.py:26
  225.0 1.8 copy-start.25
  228.5 9.7 %copy-start.15 = (f32[64,128]{1,0:T(8,128)S(1)}, f32[64,128]{1,0:T(8,128)}, u32[]{:S(2)}) copy-start(f32[64,128]{1,0:T(8,128)} %param.62) | copy-start | bytes 98308
  228.5 9.7 %copy-start.16 = (f32[64,128]{1,0:T(8,128)S(1)}, f32[64,128]{1,0:T(8,128)}, u32[]{:S(2)}) copy-start(f32[64,128]{1,0:T(8,128)} %param.61) | copy-start | bytes 98308
  228.5 9.7 %copy-start.28 = (f32[64,128]{1,0:T(8,128)S(1)}, f32[64,128]{1,0:T(8,128)}, u32[]{:S(2)}) copy-start(f32[64,128]{1,0:T(8,128)} %param.60) | copy-start | bytes 98308
  228.5 5.8 %collective-permute-start.6 = (f32[2,66,16,1]{1,2,3,0:T(8,128)S(1)}, f32[2,66,16,1]{1,2,3,0:T(8,128)S(1)}, u32[]{:S(2)}, u32[]{:S(2)}) collective-permute-start(f32[2,66,16,1]{1,2,3,0:T(8,128)S(1)} %copy.115), channel_id=1, source_target_pairs={{1,0},{2,1},{3,2},{4,3},{5,4},{6,5},{7,6},{9,8},{10,9},{11,10},{12... | collective-permute-start | bytes 25352 | tf_op jit(solution)/shard_map/ppermute | solution.py:27
  234.3 6.8 %collective-permute-start.7 = (f32[2,66,16,1]{1,2,3,0:T(8,128)S(1)}, f32[2,66,16,1]{1,2,3,0:T(8,128)S(1)}, u32[]{:S(2)}, u32[]{:S(2)}) collective-permute-start(f32[2,66,16,1]{1,2,3,0:T(8,128)S(1)} %copy.117), channel_id=1, source_target_pairs={{0,1},{1,2},{2,3},{3,4},{4,5},{5,6},{6,7},{8,9},{9,10},{10,11},{11... | collective-permute-start | bytes 25352 | tf_op jit(solution)/shard_map/ppermute | solution.py:26
  267.4 1.5 copy-start.10
  267.4 1.7 copy-start.11
  271.0 17.6 %copy-start.9 = (f32[64,15,128]{2,0,1:T(8,128)S(1)}, f32[64,15,128]{2,0,1:T(8,128)}, u32[]{:S(2)}) copy-start(f32[64,15,128]{2,0,1:T(8,128)} %get-tuple-element.488) | copy-start | bytes 1474564
  272.4 89.0 %collective-permute-start.20 = (bf16[2,64,128]{2,1,0:T(8,128)(2,1)}, bf16[2,64,128]{2,1,0:T(8,128)(2,1)}, u32[]{:S(2)}, u32[]{:S(2)}) collective-permute-start(bf16[2,64,128]{2,1,0:T(8,128)(2,1)} %pad_maximum_fusion.33), channel_id=1, source_target_pairs={{16,0},{24,8},{32,16},{40,24},{48,32},{56,40},{64,48},{72,56},{80,... | collective-permute-start | bytes 98312 | tf_op jit(solution)/shard_map/ppermute | solution.py:16
  274.3 90.3 %collective-permute-start.21 = (bf16[2,64,128]{2,1,0:T(8,128)(2,1)}, bf16[2,64,128]{2,1,0:T(8,128)(2,1)}, u32[]{:S(2)}, u32[]{:S(2)}) collective-permute-start(bf16[2,64,128]{2,1,0:T(8,128)(2,1)} %pad_maximum_fusion.33), channel_id=1, source_target_pairs={{8,0},{16,8},{24,16},{32,24},{40,32},{48,40},{56,48},{64,56},{72,6... | collective-permute-start | bytes 98312 | tf_op jit(solution)/shard_map/ppermute | solution.py:16
  276.2 90.9 %collective-permute-start.22 = (bf16[2,64,128]{2,1,0:T(8,128)(2,1)}, bf16[2,64,128]{2,1,0:T(8,128)(2,1)}, u32[]{:S(2)}, u32[]{:S(2)}) collective-permute-start(bf16[2,64,128]{2,1,0:T(8,128)(2,1)} %pad_maximum_fusion.33), channel_id=1, source_target_pairs={{0,8},{8,16},{16,24},{24,32},{32,40},{40,48},{48,56},{56,64},{64,7... | collective-permute-start | bytes 98312 | tf_op jit(solution)/shard_map/ppermute | solution.py:16
  278.7 10.3 %collective-permute-start.12 = (bf16[1,16,128]{2,1,0:T(8,128)(2,1)S(1)}, bf16[1,16,128]{2,1,0:T(8,128)(2,1)S(1)}, u32[]{:S(2)}, u32[]{:S(2)}) collective-permute-start(bf16[1,16,128]{2,1,0:T(8,128)(2,1)S(1)} %get-tuple-element.520), channel_id=1, source_target_pairs={{0,8},{8,16},{16,24},{24,32},{32,40},{40,48},{48,56},{56,64},{64,7... | collective-permute-start | bytes 12296 | tf_op jit(solution)/shard_map/ppermute | solution.py:26
  286.5 3.2 collective-permute-start.13
  288.6 9.3 %copy-start.2 = (bf16[2,63,64,128]{3,2,1,0:T(8,128)(2,1)S(1)}, bf16[2,63,64,128]{3,2,1,0:T(8,128)(2,1)}, u32[]{:S(2)}) copy-start(bf16[2,63,64,128]{3,2,1,0:T(8,128)(2,1)} %slice.533) | copy-start | bytes 6193156
  289.8 0.6 copy-start.29
  291.2 29.0 %collective-permute-start.14 = (bf16[66,16,1]{2,1,0:T(8,128)(2,1)}, bf16[66,16,1]{2,1,0:T(8,128)(2,1)S(1)}, u32[]{:S(2)}, u32[]{:S(2)}) collective-permute-start(bf16[66,16,1]{2,1,0:T(8,128)(2,1)} %get-tuple-element.518), channel_id=1, source_target_pairs={{0,1},{1,2},{2,3},{3,4},{4,5},{5,6},{6,7},{8,9},{9,10},{10,11},{11... | collective-permute-start | bytes 6344 | tf_op jit(solution)/shard_map/ppermute | solution.py:26
  293.9 26.3 %collective-permute-start.15 = (bf16[66,16,1]{2,1,0:T(8,128)(2,1)S(1)}, bf16[66,16,1]{2,1,0:T(8,128)(2,1)}, u32[]{:S(2)}, u32[]{:S(2)}) collective-permute-start(bf16[66,16,1]{2,1,0:T(8,128)(2,1)S(1)} %get-tuple-element.519), channel_id=1, source_target_pairs={{1,0},{2,1},{3,2},{4,3},{5,4},{6,5},{7,6},{9,8},{10,9},{11,10},{12... | collective-permute-start | bytes 6344 | tf_op jit(solution)/shard_map/ppermute | solution.py:27
  303.8 7.2 %copy-start.18 = (f32[64,128]{1,0:T(8,128)}, f32[64,128]{1,0:T(8,128)S(1)}, u32[]{:S(2)}) copy-start(f32[64,128]{1,0:T(8,128)S(1)} %get-tuple-element.566) | copy-start | bytes 98308
  307.8 6.2 %copy-start.20 = (f32[64,128]{1,0:T(8,128)}, f32[64,128]{1,0:T(8,128)S(1)}, u32[]{:S(2)}) copy-start(f32[64,128]{1,0:T(8,128)S(1)} %get-tuple-element.561) | copy-start | bytes 98308
  317.1 3.2 copy-start.30
  317.1 4.5 %copy-start.8 = (f32[64,16,128]{2,0,1:T(8,128)S(1)}, f32[64,16,128]{2,0,1:T(8,128)}, u32[]{:S(2)}) copy-start(f32[64,16,128]{2,0,1:T(8,128)} %copy-done.7) | copy-start | bytes 1572868
  317.1 4.5 %copy-start.12 = (f32[64,16,128]{2,0,1:T(8,128)S(1)}, f32[64,16,128]{2,0,1:T(8,128)}, u32[]{:S(2)}) copy-start(f32[64,16,128]{2,0,1:T(8,128)} %get-tuple-element.510) | copy-start | bytes 1572868
  321.6 10.9 %copy-start.17 = (f32[64,128]{1,0:T(8,128)S(1)}, f32[64,128]{1,0:T(8,128)}, u32[]{:S(2)}) copy-start(f32[64,128]{1,0:T(8,128)} %get-tuple-element.489) | copy-start | bytes 98308
  321.6 10.9 %copy-start.22 = (f32[64,1,128]{2,1,0:T(1,128)S(1)}, f32[64,1,128]{2,1,0:T(1,128)}, u32[]{:S(2)}) copy-start(f32[64,1,128]{2,1,0:T(1,128)} %get-tuple-element.504) | copy-start | bytes 98308
  321.6 10.9 %copy-start.23 = (f32[64,1,128]{2,1,0:T(1,128)S(1)}, f32[64,1,128]{2,1,0:T(1,128)}, u32[]{:S(2)}) copy-start(f32[64,1,128]{2,1,0:T(1,128)} %get-tuple-element.505) | copy-start | bytes 98308
  322.7 10.5 %collective-permute-start.16 = (f32[2,1,16,128]{3,2,1,0:T(8,128)S(1)}, f32[2,1,16,128]{3,2,1,0:T(8,128)S(1)}, u32[]{:S(2)}, u32[]{:S(2)}) collective-permute-start(f32[2,1,16,128]{3,2,1,0:T(8,128)S(1)} %get-tuple-element.499), channel_id=1, source_target_pairs={{8,0},{16,8},{24,16},{32,24},{40,32},{48,40},{56,48},{64,56},{72,6... | collective-permute-start | bytes 49160 | tf_op jit(solution)/shard_map/ppermute | solution.py:27
  325.8 7.6 %collective-permute-start.17 = (f32[2,1,16,128]{3,2,1,0:T(8,128)S(1)}, f32[2,1,16,128]{3,2,1,0:T(8,128)S(1)}, u32[]{:S(2)}, u32[]{:S(2)}) collective-permute-start(f32[2,1,16,128]{3,2,1,0:T(8,128)S(1)} %get-tuple-element.498), channel_id=1, source_target_pairs={{0,8},{8,16},{16,24},{24,32},{32,40},{40,48},{48,56},{56,64},{64,7... | collective-permute-start | bytes 49160 | tf_op jit(solution)/shard_map/ppermute | solution.py:26
  333.2 1.6 copy-start.26
  333.3 1.4 copy-start.27
  336.4 8.5 %collective-permute-start.18 = (f32[2,66,16,1]{1,2,3,0:T(8,128)S(1)}, f32[2,66,16,1]{1,2,3,0:T(8,128)S(1)}, u32[]{:S(2)}, u32[]{:S(2)}) collective-permute-start(f32[2,66,16,1]{1,2,3,0:T(8,128)S(1)} %copy.134), channel_id=1, source_target_pairs={{1,0},{2,1},{3,2},{4,3},{5,4},{6,5},{7,6},{9,8},{10,9},{11,10},{12... | collective-permute-start | bytes 25352 | tf_op jit(solution)/shard_map/ppermute | solution.py:27
  339.1 20.6 %collective-permute-start.19 = (f32[2,66,16,1]{1,2,3,0:T(8,128)S(1)}, f32[2,66,16,1]{1,2,3,0:T(8,128)S(1)}, u32[]{:S(2)}, u32[]{:S(2)}) collective-permute-start(f32[2,66,16,1]{1,2,3,0:T(8,128)S(1)} %copy.136), channel_id=1, source_target_pairs={{0,1},{1,2},{2,3},{3,4},{4,5},{5,6},{6,7},{8,9},{9,10},{10,11},{11... | collective-permute-start | bytes 25352 | tf_op jit(solution)/shard_map/ppermute | solution.py:26
  344.9 24.6 %collective-permute-start.23 = (bf16[2,64,128]{2,1,0:T(8,128)(2,1)}, bf16[2,64,128]{2,1,0:T(8,128)(2,1)S(1)}, u32[]{:S(2)}, u32[]{:S(2)}) collective-permute-start(bf16[2,64,128]{2,1,0:T(8,128)(2,1)} %pad_maximum_fusion.33), channel_id=1, source_target_pairs={{0,16},{8,24},{16,32},{24,40},{32,48},{40,56},{48,64},{56,72},{64,... | collective-permute-start | bytes 98312 | tf_op jit(solution)/shard_map/ppermute | solution.py:16
  361.4 3.2 copy-start.5
  364.6 2.5 copy-start.4
  367.1 2.5 copy-start.3
  391.6 4.7 %copy-start.19 = (f32[64,128]{1,0:T(8,128)S(1)}, f32[64,128]{1,0:T(8,128)}, u32[]{:S(2)}) copy-start(f32[64,128]{1,0:T(8,128)} %copy-done.18) | copy-start | bytes 98308
  391.6 4.7 %copy-start.21 = (f32[64,128]{1,0:T(8,128)S(1)}, f32[64,128]{1,0:T(8,128)}, u32[]{:S(2)}) copy-start(f32[64,128]{1,0:T(8,128)} %copy-done.20) | copy-start | bytes 98308
  397.7 2.6 copy-start.1
where the time goes:
time: 404 us; the launch traced here: 400 us
  waiting for transfers between devices  138 us (34%)
  starting transfers between devices  115 us (28%)
  other arithmetic  71.9 us (18%)
  local copies, waits for them, and re-layouts  37.2 us (9%)
  matrix products  22.5 us (6%)
  between operations  14.6 us (4%)
    ppermute x8, waiting for transfers between devices, padded_2(): after = lax.ppermute(initial, axis, down)  86.4 us
    ppermute x8, starting transfers between devices, padded_2(): before = lax.ppermute(last, axis, up)  55.1 us
    ppermute x8, waiting for transfers between devices, padded_2(): before = lax.ppermute(last, axis, up)  51.7 us
    ppermute x8, starting transfers between devices, passed_along(): lax.ppermute(value, axis, [(source, source + steps) for source in range(i...  37.3 us
    ppermute x8, starting transfers between devices, padded_2(): after = lax.ppermute(initial, axis, down)  22.8 us
    dot_general x16, matrix products, compute(): jnp.dot(kernel[surface, index], flat, preferred_element_type=jnp.float32)  22.5 us
    mul x16, other arithmetic, compute(): masked = source_history * keep[:, None, None]  21.8 us
    convert_element_type x16, other arithmetic, compute(): keep = ((lag_index >= first) & (lag_index < last)).astype(jnp.bfloat16)  20.9 us
  transfers between devices with their start and end apart: 24, of which 5 were waited for; matrix products, arithmetic and copies ran while one was open for 21% of the time, Pallas kernels for 0%

commit v1 on v0

v1 whole, which is shorter than its diff:
```python
import functools
import jax
import jax.numpy as jnp
from jax import lax
from jax.experimental import pallas as pl
from jax.experimental.pallas import tpu as pltpu
from jax.sharding import PartitionSpec as P

courant = 0.25
bimaterial = 0.5
slip_ref = 0.2
decay_rate = 0.5
impedance = 0.5

GX, GZ = "gx", "gz"
CHUNK = 8
LAG_CHUNK = 16
MIB = 2**20


def swap_pairs(axis, distance, phase):
    size, pairs = lax.axis_size(axis), []
    for i in range(size):
        partner = i + distance if (i - phase) % (2 * distance) < distance else i - distance
        if 0 <= partner < size:
            pairs.append((i, partner))
    return pairs


def parities():
    block = lax.axis_index(GX)
    even = lax.rem(block, 2) == 0
    chip_even = lax.rem(lax.div(block, 2), 2) == 0
    depth_even = lax.rem(lax.axis_index(GZ), 2) == 0
    return even, chip_even, depth_even


def lane_of(shape):
    return lax.broadcasted_iota(jnp.int32, shape, len(shape) - 1)


def turned(value, shift):
    return pltpu.roll(value, shift % value.shape[-1], value.ndim - 1)


def depth_edges(velocity, stress_z, rigidity):
    lane = lane_of(velocity.shape)
    count = velocity.shape[-1]
    after = jnp.where(lane == count - 1, 0.0, turned(velocity, -1))
    before = jnp.where(lane == 0, 0.0, turned(velocity, 1))
    partial = stress_z + courant * 0.5 * rigidity * (after - before)
    packed = jnp.where(
        lane < 2, turned(velocity, 1), jnp.where(lane < 4, turned(rigidity, 3), turned(partial, 5))
    )
    return packed.reshape(-1, count).T[:8]


def first_kernel(
    cone, history, kernel, velocity, stress, rigidity, core, own, later, lead, edges, total, tail
):
    surface, part = pl.program_id(0), pl.program_id(1)
    parts = pl.num_programs(1)
    nodes = own.shape[1] // 3
    offsets = kernel.shape[1] // nodes
    reach = (offsets - 1) // 2
    columns = kernel.shape[2]
    blocks = cone.shape[3]
    block = lax.axis_index(GX)

    lag = lax.div(lane_of((1, columns)), nodes) + part * (columns // nodes)
    masked = []
    for index in range(offsets):
        target = jnp.clip(block + (index - reach), 0, blocks - 1)
        first, last = cone[surface, index, 0, target], cone[surface, index, 1, target]
        keep = jnp.where((lag >= first) & (lag < last), 1.0, 0.0).astype(jnp.bfloat16)
        masked.append(kernel[0, index * nodes : (index + 1) * nodes, :] * keep)
    matrix = jnp.concatenate(masked, axis=0)

    @pl.when(part == 0)
    def _():
        tail[...] = jnp.zeros_like(tail)
        total[...] = jnp.zeros_like(total)
        lead[0] = matrix[:, :nodes]

    now = history[0]
    shifted = jnp.concatenate([tail[...], now[: columns - nodes]], axis=0)
    both = jnp.concatenate([now, shifted], axis=1)
    total[...] += jnp.dot(matrix, both, preferred_element_type=jnp.float32)
    tail[...] = now[columns - nodes :]

    @pl.when(part == parts - 1)
    def _():
        width = now.shape[1]
        for place, index in enumerate((0, 2, 4)):
            own[0, place * nodes : (place + 1) * nodes] = total[
                index * nodes : (index + 1) * nodes, :width
            ]
        base = pl.multiple_of(surface * (2 * nodes), 2 * nodes)
        core[pl.ds(base, nodes), :] = total[nodes : 2 * nodes, :width]
        core[pl.ds(base + nodes, nodes), :] = total[3 * nodes : 4 * nodes, :width]
        later[0] = total[:, width:]

    step = surface * parts + part
    width = velocity.shape[0] * velocity.shape[1]
    edges[:, pl.ds(pl.multiple_of(step * width, width), width)] = depth_edges(
        velocity[...], stress[1], rigidity[...]
    )

    @pl.when(step == 0)
    def _():
        strike_edge(core, 4 * nodes, velocity[0], rigidity[0], stress[0, 0], velocity[1], 1.0)

    @pl.when(step == pl.num_programs(0) * parts - 1)
    def _():
        n = velocity.shape[0]
        strike_edge(
            core,
            4 * nodes + 48,
            velocity[n - 1],
            rigidity[n - 1],
            stress[0, n - 1],
            velocity[n - 2],
            -1.0,
        )


def strike_edge(core, base, velocity, rigidity, stress_x, inner, sign):
    core[base : base + 16] = velocity
    core[base + 16 : base + 32] = rigidity
    core[base + 32 : base + 48] = stress_x + (sign * courant * 0.5) * rigidity * inner


def first_call(cone, history, kernel, velocity, stress, rigidity):
    surfaces, rows, columns = kernel.shape
    nodes = velocity.shape[0]
    width = history.shape[2]
    chunk = LAG_CHUNK * nodes
    parts = columns // chunk
    slab = nodes // (surfaces * parts)
    ny = velocity.shape[1]
    f32 = jnp.float32
    return pl.pallas_call(
        first_kernel,
        grid=(surfaces, parts),
        in_specs=[
            pl.BlockSpec(memory_space=pltpu.SMEM),
            pl.BlockSpec((1, chunk, width), lambda s, k: (s, k, 0)),
            pl.BlockSpec((1, rows, chunk), lambda s, k: (s, 0, k)),
            pl.BlockSpec((slab, ny, width), lambda s, k: (s * parts + k, 0, 0)),
            pl.BlockSpec((2, slab, ny, width), lambda s, k: (0, s * parts + k, 0, 0)),
            pl.BlockSpec((slab, ny, width), lambda s, k: (s * parts + k, 0, 0)),
        ],
        out_specs=[
            pl.BlockSpec((4 * nodes + 96, width), lambda s, k: (0, 0)),
            pl.BlockSpec((1, 3 * nodes, width), lambda s, k: (s, 0, 0)),
            pl.BlockSpec((1, rows, width), lambda s, k: (s, 0, 0)),
            pl.BlockSpec((1, rows, nodes), lambda s, k: (s, 0, 0)),
            pl.BlockSpec((8, nodes * ny), lambda s, k: (0, 0)),
        ],
        out_shape=[
            jax.ShapeDtypeStruct((4 * nodes + 96, width), f32),
            jax.ShapeDtypeStruct((surfaces, 3 * nodes, width), f32),
            jax.ShapeDtypeStruct((surfaces, rows, width), f32),
            jax.ShapeDtypeStruct((surfaces, rows, nodes), jnp.bfloat16),
            jax.ShapeDtypeStruct((8, nodes * ny), f32),
        ],
        scratch_shapes=[
            pltpu.VMEM((rows, 2 * width), f32),
            pltpu.VMEM((nodes, width), jnp.bfloat16),
        ],
        compiler_params=pltpu.CompilerParams(vmem_limit_bytes=16 * MIB),
    )(cone, history, kernel, velocity, stress, rigidity)


def relay_kernel(received, own, near, far):
    even, chip_even, _ = parities()
    nodes = own.shape[1] // 3
    right, left = [], []
    for surface in range(2):
        base = surface * 2 * nodes
        from_left = received[base : base + nodes]
        from_right = received[base + nodes : base + 2 * nodes]
        nothing = jnp.zeros_like(from_left)
        left.append(own[surface, :nodes] + lax.select(even, nothing, from_left))
        right.append(own[surface, 2 * nodes :] + lax.select(even, from_right, nothing))
    left.append(received[4 * nodes : 4 * nodes + 48])
    right.append(received[4 * nodes + 48 :])
    base = 0
    for to_left, to_right in zip(left, right):
        size = to_left.shape[0]
        near[base : base + size] = lax.select(chip_even, to_right, to_left)
        far[base : base + size] = lax.select(chip_even, to_left, to_right)
        base += size


def relay_call(received, own):
    nodes, width = own.shape[1] // 3, own.shape[2]
    shape = jax.ShapeDtypeStruct((2 * nodes + 48, width), jnp.float32)
    return pl.pallas_call(
        relay_kernel,
        out_shape=[shape, shape],
        compiler_params=pltpu.CompilerParams(vmem_limit_bytes=4 * MIB),
    )(received, own)


def step_kernel(last, *refs):
    (velocity, stress, stress_y, rigidity, buoyancy, sigma_star, sigma_zero, friction) = refs[:8]
    (received, near, far, depth_near, depth_far, own) = refs[8:14]
    refs = refs[14:]
    if last:
        velocity_new, stress_new, stress_y_new, state_new, bounds = refs[:5]
        refs = refs[5:]
    else:
        later, lead = refs[:2]
        velocity_new, stress_new, stress_y_new, state_new, core, own_new, edges = refs[2:9]
        refs = refs[9:]
    padded, spread, depth, partial, traction = refs[:5]
    even, chip_even, depth_even = parities()
    nodes, ny, width = velocity.shape
    fault = ny // 2 - 1
    scale = courant * 0.5

    for surface in range(2):
        base = surface * 2 * nodes
        mate = lax.select(
            even, received[base : base + nodes], received[base + nodes : base + 2 * nodes]
        )
        rows = slice(surface * nodes, (surface + 1) * nodes)
        traction[surface] = own[surface, nodes : 2 * nodes] + mate + near[rows] + far[rows]

    near_halo, far_halo = near[2 * nodes :], far[2 * nodes :]
    left = lax.select(
        even, lax.select(chip_even, far_halo, near_halo), received[4 * nodes + 48 :]
    )
    right = lax.select(
        even, received[4 * nodes : 4 * nodes + 48], lax.select(chip_even, near_halo, far_halo)
    )
    padded[0], padded[nodes + 1] = left[:16], right[:16]
    spread[0] = left[32:] + scale * left[16:32] * velocity[0]
    spread[nodes + 1] = right[32:] - scale * right[16:32] * velocity[nodes - 1]

    from_left = lax.select(depth_even, depth_far[...], depth_near[...])
    from_right = lax.select(depth_even, depth_near[...], depth_far[...])
    row = lax.broadcasted_iota(jnp.int32, from_left.shape, 0)
    depth[...] = jnp.where(
        lax.rem(row, 2) == 0, pltpu.roll(from_right, 7, 0), pltpu.roll(from_left, 1, 0)
    )

    def fill(i, carry):
        at = i * CHUNK
        padded[pl.ds(at + 1, CHUNK)] = velocity[pl.ds(at, CHUNK)]
        return carry

    lax.fori_loop(0, nodes // CHUNK, fill, 0)

    shape = (CHUNK, ny, width)
    lane = lane_of(shape)
    level = lax.broadcasted_iota(jnp.int32, shape, 1)

    def stresses(i, carry):
        at = pl.multiple_of(i * CHUNK, CHUNK)
        cells = pl.ds(at, CHUNK)
        here, rigid = velocity[cells], rigidity[cells]
        stress_x = stress[0, cells] + scale * rigid * (
            padded[pl.ds(at + 2, CHUNK)] - padded[cells]
        )
        spread[pl.ds(at + 1, CHUNK)] = stress_x
        stress_new[0, cells] = stress_x

        halo = depth[:, pl.ds(pl.multiple_of(i * CHUNK * ny, CHUNK * ny), CHUNK * ny)]
        halo = jnp.concatenate([halo, jnp.zeros((width - 8, CHUNK * ny), jnp.float32)], axis=0)
        halo = halo.T.reshape(shape)
        sides = turned(halo, -1)
        after = jnp.where(lane == width - 1, sides, turned(here, -1))
        before = jnp.where(lane == 0, sides, turned(here, 1))
        stress_z = stress[1, cells] + scale * rigid * (after - before)
        stress_new[1, cells] = stress_z
        change = scale * turned(halo, -3) * here
        sides = turned(halo, -5) + jnp.where(lane == 0, change, -change)
        after = jnp.where(lane == width - 1, sides, turned(stress_z, -1))
        before = jnp.where(lane == 0, sides, turned(stress_z, 1))
        spreading = 0.5 * (after - before)

        faces = stress_y[cells]
        faces = faces[:, : ny - 1]
        trial = faces + courant * (0.5 * (rigid[:, 1:] + rigid[:, :-1])) * (
            here[:, 1:] - here[:, :-1]
        )
        slip_rate = here[:, fault + 1] - here[:, fault]
        zero = sigma_zero[cells]
        normal = zero + bimaterial * jnp.tanh(stress_x[:, fault + 1] - stress_x[:, fault])
        state = normal + (sigma_star[cells] - normal) * jnp.exp(
            -(jnp.abs(slip_rate) + slip_ref) * decay_rate
        )
        state_new[cells] = state
        strength = friction[cells] * state
        clipped = jnp.clip(trial[:, fault], -strength, strength)
        bottom = traction[0, cells] + impedance * here[:, 0]
        top = traction[1, cells] - impedance * here[:, ny - 1]
        if last:
            bounds[0, cells] = bottom
            bounds[1, cells] = top
        above = jnp.concatenate([trial, top[:, None]], axis=1)
        above = jnp.where(level == fault, clipped[:, None], above)
        stress_y_new[cells] = above[:, : stress_y_new.shape[1]]
        below = jnp.where(level == 0, bottom[:, None], pltpu.roll(above, 1, 1))
        partial[cells] = spreading + above - below
        return carry

    lax.fori_loop(0, nodes // CHUNK, stresses, 0)

    def velocities(i, carry):
        at = pl.multiple_of(i * CHUNK, CHUNK)
        cells = pl.ds(at, CHUNK)
        along = 0.5 * (spread[pl.ds(at + 2, CHUNK)] - spread[cells])
        moved = velocity[cells] + courant * buoyancy[cells] * (along + partial[cells])
        velocity_new[cells] = moved
        if not last:
            newest = refs[5]
            newest[0, cells] = moved[:, 0]
            newest[1, cells] = moved[:, ny - 1]
            edges[:, pl.ds(pl.multiple_of(i * CHUNK * ny, CHUNK * ny), CHUNK * ny)] = depth_edges(
                moved, stress_new[1, cells], rigidity[cells]
            )
        return carry

    lax.fori_loop(0, nodes // CHUNK, velocities, 0)

    if not last:
        newest = refs[5]
        for surface in range(2):
            fresh = newest[surface].astype(jnp.bfloat16)
            total = later[surface] + jnp.dot(
                lead[surface], fresh, preferred_element_type=jnp.float32
            )
            for place, index in enumerate((0, 2, 4)):
                own_new[surface, place * nodes : (place + 1) * nodes] = total[
                    index * nodes : (index + 1) * nodes
                ]
            base = surface * 2 * nodes
            core[base : base + nodes] = total[nodes : 2 * nodes]
            core[base + nodes : base + 2 * nodes] = total[3 * nodes : 4 * nodes]
        strike_edge(
            core, 4 * nodes, velocity_new[0], rigidity[0], stress_new[0, 0], velocity_new[1], 1.0
        )
        strike_edge(
            core,
            4 * nodes + 48,
            velocity_new[nodes - 1],
            rigidity[nodes - 1],
            stress_new[0, nodes - 1],
            velocity_new[nodes - 2],
            -1.0,
        )


def step_call(last, *args):
    nodes, ny, width = args[0].shape
    f32 = jnp.float32

    def shaped(*shape):
        return jax.ShapeDtypeStruct(shape, f32)

    outs = [
        shaped(nodes, ny, width),
        shaped(2, nodes, ny, width),
        shaped(nodes, ny - 1 if last else ny, width),
        shaped(nodes, width),
    ]
    if last:
        outs += [shaped(2, nodes, width)]
    else:
        outs += [
            shaped(4 * nodes + 96, width),
            shaped(2, 3 * nodes, width),
            shaped(8, nodes * ny),
        ]
    scratch = [
        pltpu.VMEM((nodes + 2, ny, width), f32),
        pltpu.VMEM((nodes + 2, ny, width), f32),
        pltpu.VMEM((8, nodes * ny), f32),
        pltpu.VMEM((nodes, ny, width), f32),
        pltpu.VMEM((2, nodes, width), f32),
    ]
    if not last:
        scratch += [pltpu.VMEM((2, nodes, width), f32)]
    return pl.pallas_call(
        functools.partial(step_kernel, last),
        out_shape=outs,
        scratch_shapes=scratch,
        compiler_params=pltpu.CompilerParams(vmem_limit_bytes=24 * MIB),
    )(*args)


def exchange(core, own, edges):
    received = lax.ppermute(core, GX, swap_pairs(GX, 1, 0))
    near, far = relay_call(received, own)
    far = lax.ppermute(far, GX, swap_pairs(GX, 2, 2))
    near = lax.ppermute(near, GX, swap_pairs(GX, 2, 0))
    depth_far = lax.ppermute(edges, GZ, swap_pairs(GZ, 1, 1))
    depth_near = lax.ppermute(edges, GZ, swap_pairs(GZ, 1, 0))
    return received, near, far, depth_near, depth_far


def local(
    velocity,
    stress_xz,
    stress_y,
    rigidity,
    buoyancy,
    sigma_star,
    sigma_zero,
    friction,
    history,
    kernel,
    cone,
):
    surfaces, lags, nodes, width = history.shape
    past = history.reshape(surfaces, lags * nodes, width)
    matrix = kernel.reshape(surfaces, -1, kernel.shape[3])
    turned_cone = jnp.transpose(cone, (0, 2, 3, 1))
    core, own, later, lead, edges = first_call(
        turned_cone, past, matrix, velocity, stress_xz, rigidity
    )
    moved = exchange(core, own, edges)
    velocity, stress_xz, stress_y, state, core, own, edges = step_call(
        False,
        velocity,
        stress_xz,
        stress_y,
        rigidity,
        buoyancy,
        sigma_star,
        sigma_zero,
        friction,
        *moved,
        own,
        later,
        lead,
    )
    moved = exchange(core, own, edges)
    return step_call(
        True,
        velocity,
        stress_xz,
        stress_y,
        rigidity,
        buoyancy,
        state,
        sigma_zero,
        friction,
        *moved,
        own,
    )


def solution(mesh):
    in_specs = (
        P("gx", None, "gz"),
        P(None, "gx", None, "gz"),
        P("gx", None, "gz"),
        P("gx", None, "gz"),
        P("gx", None, "gz"),
        P("gx", "gz"),
        P("gx", "gz"),
        P("gx", "gz"),
        P(None, None, "gx", "gz"),
        P(),
        P(),
    )
    out_specs = (
        P("gx", None, "gz"),
        P(None, "gx", None, "gz"),
        P("gx", None, "gz"),
        P("gx", "gz"),
        P(None, "gx", "gz"),
    )
    return jax.shard_map(
        local, mesh=mesh, in_specs=in_specs, out_specs=tuple(out_specs), check_vma=False
    )
```

time: 404 us -> 54.9 us (0.14)
  the two profiles are of different devices: /device:TPU:86 before, /device:TPU:95 now
where the time goes in v1:
time: 54.9 us; the launch traced here: 54.5 us
  starting transfers between devices  20.7 us (38%)
  Pallas kernels  13.9 us (25%)
  waiting for transfers between devices  9.8 us (18%)
  local copies, waits for them, and re-layouts  9.33 us (17%)
  between operations  0.83 us (2%)
    ppermute x2, starting transfers between devices, exchange(): far = lax.ppermute(far, GX, swap_pairs(GX, 2, 2))  11.6 us
    unnamed x29, local copies, waits for them, and re-layouts  8.4 us
    pallas_call x2, Pallas kernels, step_call(): pl.pallas_call(functools.partial(step_kernel, last), out_shape=outs, scra...  7.46 us
    pallas_call x1, Pallas kernels, first_call(): pl.pallas_call(first_kernel, grid=(surfaces, parts), in_specs=[pl.BlockSp...  6.34 us
    ppermute x2, waiting for transfers between devices, exchange(): depth_far = lax.ppermute(edges, GZ, swap_pairs(GZ, 1, 1))  5.91 us
    ppermute x2, starting transfers between devices, exchange(): depth_far = lax.ppermute(edges, GZ, swap_pairs(GZ, 1, 1))  5.27 us
    ppermute x2, starting transfers between devices, exchange(): received = lax.ppermute(core, GX, swap_pairs(GX, 1, 0))  2.92 us
    ppermute x2, waiting for transfers between devices, exchange(): received = lax.ppermute(core, GX, swap_pairs(GX, 1, 0))  2.1 us
  transfers between devices with their start and end apart: 10, of which 6 were waited for; matrix products, arithmetic and copies ran while one was open for 1% of the time, Pallas kernels for 0%

profile of v1, /device:TPU:95, one launch (start us, length us, event | category | flops | bytes accessed | tf_op | source)
XLA Modules:
  0.0 54.5 jit_solution(7431315464759743845)
XLA Ops:
  0.6 0.0 copy-start
  0.6 2.5 %copy-done = bf16[2,5,64,4096]{3,2,1,0:T(8,128)(2,1)S(1)} copy-done((bf16[2,5,64,4096]{3,2,1,0:T(8,128)(2,1)S(1)}, bf16[2,5,64,4096]{3,2,1,0:T(8,128)(2,1)}, u32[]{:S(2)}) %copy-start) | copy-done | bytes 5242904
  3.1 0.0 copy-start.1
  3.1 1.0 %copy-done.1 = f32[64,16,128]{2,1,0:T(8,128)S(1)} copy-done((f32[64,16,128]{2,1,0:T(8,128)S(1)}, f32[64,16,128]{2,1,0:T(8,128)}, u32[]{:S(2)}) %copy-start.1) | copy-done | bytes 524312
  4.2 0.0 copy-start.3
  4.2 1.2 %copy-done.3 = f32[2,64,16,128]{3,2,1,0:T(8,128)S(1)} copy-done((f32[2,64,16,128]{3,2,1,0:T(8,128)S(1)}, f32[2,64,16,128]{3,2,1,0:T(8,128)}, u32[]{:S(2)}) %copy-start.3) | copy-done | bytes 1048600
  5.4 0.0 copy-start.5
  5.4 1.0 %copy-done.5 = f32[64,16,128]{2,1,0:T(8,128)S(1)} copy-done((f32[64,16,128]{2,1,0:T(8,128)S(1)}, f32[64,16,128]{2,1,0:T(8,128)}, u32[]{:S(2)}) %copy-start.5) | copy-done | bytes 524312
  6.4 0.0 copy-start.7
  6.4 1.6 %copy-done.7 = bf16[2,64,64,128]{3,2,1,0:T(8,128)(2,1)S(1)} copy-done((bf16[2,64,64,128]{3,2,1,0:T(8,128)(2,1)S(1)}, bf16[2,64,64,128]{3,2,1,0:T(8,128)(2,1)}, u32[]{:S(2)}) %copy-start.7) | copy-done | bytes 2097176
  8.0 0.0 copy-start.12
  8.0 0.7 %copy-done.12 = s32[2,32,5,2]{1,3,2,0:T(2,128)S(1)} copy-done((s32[2,32,5,2]{1,3,2,0:T(2,128)S(1)}, s32[2,32,5,2]{1,3,2,0:T(2,128)}, u32[]{:S(2)}) %copy-start.12) | copy-done | bytes 2584
  8.7 0.0 copy-start.13
  8.7 0.0 copy-start.2
  8.7 0.0 copy-start.4
  8.7 0.0 copy-start.6
  8.7 0.0 copy-start.8
  8.7 0.0 copy-start.9
  8.8 0.0 copy-start.10
  8.8 0.0 copy-start.11
  8.8 6.3 %shard_map.146 = (f32[352,128]{1,0:T(8,128)S(1)}, f32[2,192,128]{2,1,0:T(8,128)S(1)}, f32[2,320,128]{2,1,0:T(8,128)S(1)}, bf16[2,320,64]{2,1,0:T(8,128)(2,1)S(1)}, f32[8,1024]{1,0:T(8,128)S(1)}) custom-call(s32[2,5,2,32]{3,2,1,0:T(2,128)S(1)} %bitcast.5, bf16[2,4096,128]{2,1,0:T(8,128)(2,1)S(1)} %bitcast.4, bf16[2,320,4096]{2,1,0:T(8,128)(2,1)S(1)} %bitcast.3, ...), custom_call_target="tpu_custom_call" | custom-call | tf_op jit(solution)/shard_map/pallas_call | solution.py:142
  15.1 0.8 %collective-permute-start = (f32[352,128]{1,0:T(8,128)S(1)}, f32[352,128]{1,0:T(8,128)S(1)}, u32[]{:S(2)}, u32[]{:S(2)}) collective-permute-start(f32[352,128]{1,0:T(8,128)S(1)} %get-tuple-element.21), channel_id=1, source_target_pairs={{0,8},{8,0},{16,24},{24,16},{32,40},{40,32},{48,56},{56,48},{64,72... | collective-permute-start | bytes 540680 | tf_op jit(solution)/shard_map/ppermute | solution.py:396
  15.9 1.0 %collective-permute-done.received.refs_8_ = f32[352,128]{1,0:T(8,128)S(1)} collective-permute-done((f32[352,128]{1,0:T(8,128)S(1)}, f32[352,128]{1,0:T(8,128)S(1)}, u32[]{:S(2)}, u32[]{:S(2)}) %collective-permute-start) | collective-permute-done | bytes 180256 | tf_op jit(solution)/shard_map/ppermute | solution.py:396
  17.0 0.6 %collective-permute-start.1 = (f32[176,128]{1,0:T(8,128)S(1)}, f32[176,128]{1,0:T(8,128)S(1)}, u32[]{:S(2)}, u32[]{:S(2)}) collective-permute-start(f32[176,128]{1,0:T(8,128)S(1)} %get-tuple-element.23), channel_id=1, source_target_pairs={{0,16},{8,24},{16,0},{24,8},{32,48},{40,56},{48,32},{56,40},{64,80... | collective-permute-start | bytes 270344 | tf_op jit(solution)/shard_map/ppermute | solution.py:399
  17.6 6.7 %collective-permute-start.2 = (f32[176,128]{1,0:T(8,128)S(1)}, f32[176,128]{1,0:T(8,128)S(1)}, u32[]{:S(2)}, u32[]{:S(2)}) collective-permute-start(f32[176,128]{1,0:T(8,128)S(1)} %get-tuple-element.24), channel_id=1, source_target_pairs={{16,32},{24,40},{32,16},{40,24},{48,64},{56,72},{64,48},{72,56},{8... | collective-permute-start | bytes 270344 | tf_op jit(solution)/shard_map/ppermute | solution.py:398
  24.3 2.8 %collective-permute-start.4 = (f32[8,1024]{1,0:T(8,128)S(1)}, f32[8,1024]{1,0:T(8,128)S(1)}, u32[]{:S(2)}, u32[]{:S(2)}) collective-permute-start(f32[8,1024]{1,0:T(8,128)S(1)} %get-tuple-element.25), channel_id=1, source_target_pairs={{1,2},{2,1},{3,4},{4,3},{5,6},{6,5},{9,10},{10,9},{11,12},{12,11},... | collective-permute-start | bytes 98312 | tf_op jit(solution)/shard_map/ppermute | solution.py:400
  27.1 0.1 collective-permute-start.3
  27.2 0.0 copy-done.13
  27.2 0.3 copy.16.refs_2_
  27.5 2.6 %collective-permute-done.4.refs_12_ = f32[8,1024]{1,0:T(8,128)S(1)} collective-permute-done((f32[8,1024]{1,0:T(8,128)S(1)}, f32[8,1024]{1,0:T(8,128)S(1)}, u32[]{:S(2)}, u32[]{:S(2)}) %collective-permute-start.4) | collective-permute-done | bytes 32800 | tf_op jit(solution)/shard_map/ppermute | solution.py:400
  30.1 0.1 collective-permute-done.3.refs_11_
  30.3 0.0 collective-permute-done.1.refs_9_
  30.3 0.0 collective-permute-done.2.refs_10_
  30.3 0.0 copy-done.2
  30.3 0.0 copy-done.4
  30.3 0.0 copy-done.6
  30.3 0.0 copy-done.8
  30.3 0.0 copy-done.9
  30.3 0.0 copy-done.10
  30.3 0.0 copy-done.11
  30.3 4.0 %shard_map.148 = (f32[64,16,128]{2,1,0:T(8,128)S(1)}, f32[2,64,16,128]{3,2,1,0:T(8,128)S(1)}, f32[64,16,128]{2,1,0:T(8,128)S(1)}, f32[64,128]{1,0:T(8,128)S(1)},...) custom-call(f32[64,16,128]{2,1,0:T(8,128)S(1)} %copy-done.6, ...), custom_call_target="tpu_custom_call" | custom-call | tf_op jit(solution)/shard_map/pallas_call | solution.py:387
  34.4 2.1 %collective-permute-start.5 = (f32[352,128]{1,0:T(8,128)S(1)}, f32[352,128]{1,0:T(8,128)S(1)}, u32[]{:S(2)}, u32[]{:S(2)}) collective-permute-start(f32[352,128]{1,0:T(8,128)S(1)} %get-tuple-element.32), channel_id=1, source_target_pairs={{0,8},{8,0},{16,24},{24,16},{32,40},{40,32},{48,56},{56,48},{64,72... | collective-permute-start | bytes 540680 | tf_op jit(solution)/shard_map/ppermute | solution.py:396
  36.5 1.0 %collective-permute-done.5.received.refs_8_ = f32[352,128]{1,0:T(8,128)S(1)} collective-permute-done((f32[352,128]{1,0:T(8,128)S(1)}, f32[352,128]{1,0:T(8,128)S(1)}, u32[]{:S(2)}, u32[]{:S(2)}) %collective-permute-start.5) | collective-permute-done | bytes 180256 | tf_op jit(solution)/shard_map/ppermute | solution.py:396
  37.6 0.1 collective-permute-start.6
  37.7 4.9 %collective-permute-start.7 = (f32[176,128]{1,0:T(8,128)S(1)}, f32[176,128]{1,0:T(8,128)S(1)}, u32[]{:S(2)}, u32[]{:S(2)}) collective-permute-start(f32[176,128]{1,0:T(8,128)S(1)} %get-tuple-element.35), channel_id=1, source_target_pairs={{16,32},{24,40},{32,16},{40,24},{48,64},{56,72},{64,48},{72,56},{8... | collective-permute-start | bytes 270344 | tf_op jit(solution)/shard_map/ppermute | solution.py:398
  42.6 2.5 %collective-permute-start.9 = (f32[8,1024]{1,0:T(8,128)S(1)}, f32[8,1024]{1,0:T(8,128)S(1)}, u32[]{:S(2)}, u32[]{:S(2)}) collective-permute-start(f32[8,1024]{1,0:T(8,128)S(1)} %get-tuple-element.36), channel_id=1, source_target_pairs={{1,2},{2,1},{3,4},{4,3},{5,6},{6,5},{9,10},{10,9},{11,12},{12,11},... | collective-permute-start | bytes 98312 | tf_op jit(solution)/shard_map/ppermute | solution.py:400
  45.1 0.1 collective-permute-start.8
  45.2 3.3 %collective-permute-done.9.refs_12_ = f32[8,1024]{1,0:T(8,128)S(1)} collective-permute-done((f32[8,1024]{1,0:T(8,128)S(1)}, f32[8,1024]{1,0:T(8,128)S(1)}, u32[]{:S(2)}, u32[]{:S(2)}) %collective-permute-start.9) | collective-permute-done | bytes 32800 | tf_op jit(solution)/shard_map/ppermute | solution.py:400
  48.5 0.0 collective-permute-done.8.refs_11_
  48.5 0.0 collective-permute-done.6.refs_9_
  48.5 1.7 %collective-permute-done.7.refs_10_ = f32[176,128]{1,0:T(8,128)S(1)} collective-permute-done((f32[176,128]{1,0:T(8,128)S(1)}, f32[176,128]{1,0:T(8,128)S(1)}, u32[]{:S(2)}, u32[]{:S(2)}) %collective-permute-start.7) | collective-permute-done | bytes 90144 | tf_op jit(solution)/shard_map/ppermute | solution.py:398
  50.1 3.4 %shard_map.150 = (f32[64,16,128]{2,1,0:T(8,128)}, f32[2,64,16,128]{3,2,1,0:T(8,128)}, f32[64,15,128]{2,1,0:T(8,128)S(1)}, f32[64,128]{1,0:T(8,128)}, f32[2,64,128]{2,1,0:T(8,128)}) custom-call(f32[64,16,128]{2,1,0:T(8,128)S(1)} %get-tuple-element.28.refs_0_, f32[2,64,16,128]{3,2,1,0:T(8,128)S(1)} %get-tuple-element.29.refs_1_, ...), custom_call_target="tpu_custom_call" | custom-call | tf_op jit(solution)/shard_map/pallas_call | solution.py:387
  53.6 0.9 %copy.17 = f32[64,15,128]{2,0,1:T(8,128)} copy(f32[64,15,128]{2,1,0:T(8,128)S(1)} %get-tuple-element.39) | data formatting | bytes 983040 | tf_op jit(solution)/shard_map/pallas_call | solution.py:387
  (2 shorter events, 0.1 us)
Async XLA Ops:
  0.6 2.5 %copy-start = (bf16[2,5,64,4096]{3,2,1,0:T(8,128)(2,1)S(1)}, bf16[2,5,64,4096]{3,2,1,0:T(8,128)(2,1)}, u32[]{:S(2)}) copy-start(bf16[2,5,64,4096]{3,2,1,0:T(8,128)(2,1)} %param.20) | copy-start | bytes 15728644
  3.1 1.0 %copy-start.1 = (f32[64,16,128]{2,1,0:T(8,128)S(1)}, f32[64,16,128]{2,1,0:T(8,128)}, u32[]{:S(2)}) copy-start(f32[64,16,128]{2,1,0:T(8,128)} %refs_3_.3) | copy-start | bytes 1572868
  4.2 1.2 %copy-start.3 = (f32[2,64,16,128]{3,2,1,0:T(8,128)S(1)}, f32[2,64,16,128]{3,2,1,0:T(8,128)}, u32[]{:S(2)}) copy-start(f32[2,64,16,128]{3,2,1,0:T(8,128)} %refs_1_.1) | copy-start | bytes 3145732
  5.4 1.0 %copy-start.5 = (f32[64,16,128]{2,1,0:T(8,128)S(1)}, f32[64,16,128]{2,1,0:T(8,128)}, u32[]{:S(2)}) copy-start(f32[64,16,128]{2,1,0:T(8,128)} %refs_0_.1) | copy-start | bytes 1572868
  6.4 1.6 %copy-start.7 = (bf16[2,64,64,128]{3,2,1,0:T(8,128)(2,1)S(1)}, bf16[2,64,64,128]{3,2,1,0:T(8,128)(2,1)}, u32[]{:S(2)}) copy-start(bf16[2,64,64,128]{3,2,1,0:T(8,128)(2,1)} %param.19) | copy-start | bytes 6291460
  8.0 0.7 %copy-start.12 = (s32[2,32,5,2]{1,3,2,0:T(2,128)S(1)}, s32[2,32,5,2]{1,3,2,0:T(2,128)}, u32[]{:S(2)}) copy-start(s32[2,32,5,2]{1,3,2,0:T(2,128)} %param.21) | copy-start | bytes 7684
  8.7 18.5 %copy-start.13 = (f32[64,15,128]{2,0,1:T(8,128)S(1)}, f32[64,15,128]{2,0,1:T(8,128)}, u32[]{:S(2)}) copy-start(f32[64,15,128]{2,0,1:T(8,128)} %param.13) | copy-start | bytes 1474564
  8.7 21.6 %copy-start.2 = (f32[64,16,128]{2,1,0:T(8,128)S(1)}, f32[64,16,128]{2,1,0:T(8,128)}, u32[]{:S(2)}) copy-start(f32[64,16,128]{2,1,0:T(8,128)} %refs_3_.3) | copy-start | bytes 1572868
  8.7 21.6 %copy-start.4 = (f32[2,64,16,128]{3,2,1,0:T(8,128)S(1)}, f32[2,64,16,128]{3,2,1,0:T(8,128)}, u32[]{:S(2)}) copy-start(f32[2,64,16,128]{3,2,1,0:T(8,128)} %refs_1_.1) | copy-start | bytes 3145732
  8.7 21.6 %copy-start.6 = (f32[64,16,128]{2,1,0:T(8,128)S(1)}, f32[64,16,128]{2,1,0:T(8,128)}, u32[]{:S(2)}) copy-start(f32[64,16,128]{2,1,0:T(8,128)} %refs_0_.1) | copy-start | bytes 1572868
  8.7 21.6 %copy-start.8 = (f32[64,16,128]{2,1,0:T(8,128)S(1)}, f32[64,16,128]{2,1,0:T(8,128)}, u32[]{:S(2)}) copy-start(f32[64,16,128]{2,1,0:T(8,128)} %refs_4_.3) | copy-start | bytes 1572868
  8.7 21.6 %copy-start.9 = (f32[64,128]{1,0:T(8,128)S(1)}, f32[64,128]{1,0:T(8,128)}, u32[]{:S(2)}) copy-start(f32[64,128]{1,0:T(8,128)} %refs_6_.3) | copy-start | bytes 98308
  8.8 21.6 %copy-start.10 = (f32[64,128]{1,0:T(8,128)S(1)}, f32[64,128]{1,0:T(8,128)}, u32[]{:S(2)}) copy-start(f32[64,128]{1,0:T(8,128)} %refs_7_.3) | copy-start | bytes 98308
  8.8 21.6 %copy-start.11 = (f32[64,128]{1,0:T(8,128)S(1)}, f32[64,128]{1,0:T(8,128)}, u32[]{:S(2)}) copy-start(f32[64,128]{1,0:T(8,128)} %refs_5_.1) | copy-start | bytes 98308
  15.1 1.8 %collective-permute-start = (f32[352,128]{1,0:T(8,128)S(1)}, f32[352,128]{1,0:T(8,128)S(1)}, u32[]{:S(2)}, u32[]{:S(2)}) collective-permute-start(f32[352,128]{1,0:T(8,128)S(1)} %get-tuple-element.21), channel_id=1, source_target_pairs={{0,8},{8,0},{16,24},{24,16},{32,40},{40,32},{48,56},{56,48},{64,72... | collective-permute-start | bytes 540680 | tf_op jit(solution)/shard_map/ppermute | solution.py:396
  17.0 13.3 %collective-permute-start.1 = (f32[176,128]{1,0:T(8,128)S(1)}, f32[176,128]{1,0:T(8,128)S(1)}, u32[]{:S(2)}, u32[]{:S(2)}) collective-permute-start(f32[176,128]{1,0:T(8,128)S(1)} %get-tuple-element.23), channel_id=1, source_target_pairs={{0,16},{8,24},{16,0},{24,8},{32,48},{40,56},{48,32},{56,40},{64,80... | collective-permute-start | bytes 270344 | tf_op jit(solution)/shard_map/ppermute | solution.py:399
  17.6 12.7 %collective-permute-start.2 = (f32[176,128]{1,0:T(8,128)S(1)}, f32[176,128]{1,0:T(8,128)S(1)}, u32[]{:S(2)}, u32[]{:S(2)}) collective-permute-start(f32[176,128]{1,0:T(8,128)S(1)} %get-tuple-element.24), channel_id=1, source_target_pairs={{16,32},{24,40},{32,16},{40,24},{48,64},{56,72},{64,48},{72,56},{8... | collective-permute-start | bytes 270344 | tf_op jit(solution)/shard_map/ppermute | solution.py:398
  24.3 5.9 %collective-permute-start.4 = (f32[8,1024]{1,0:T(8,128)S(1)}, f32[8,1024]{1,0:T(8,128)S(1)}, u32[]{:S(2)}, u32[]{:S(2)}) collective-permute-start(f32[8,1024]{1,0:T(8,128)S(1)} %get-tuple-element.25), channel_id=1, source_target_pairs={{1,2},{2,1},{3,4},{4,3},{5,6},{6,5},{9,10},{10,9},{11,12},{12,11},... | collective-permute-start | bytes 98312 | tf_op jit(solution)/shard_map/ppermute | solution.py:400
  27.1 3.1 %collective-permute-start.3 = (f32[8,1024]{1,0:T(8,128)S(1)}, f32[8,1024]{1,0:T(8,128)S(1)}, u32[]{:S(2)}, u32[]{:S(2)}) collective-permute-start(f32[8,1024]{1,0:T(8,128)S(1)} %get-tuple-element.25), channel_id=1, source_target_pairs={{0,1},{1,0},{2,3},{3,2},{4,5},{5,4},{6,7},{7,6},{8,9},{9,8},{10,11... | collective-permute-start | bytes 98312 | tf_op jit(solution)/shard_map/ppermute | solution.py:401
  34.4 3.2 %collective-permute-start.5 = (f32[352,128]{1,0:T(8,128)S(1)}, f32[352,128]{1,0:T(8,128)S(1)}, u32[]{:S(2)}, u32[]{:S(2)}) collective-permute-start(f32[352,128]{1,0:T(8,128)S(1)} %get-tuple-element.32), channel_id=1, source_target_pairs={{0,8},{8,0},{16,24},{24,16},{32,40},{40,32},{48,56},{56,48},{64,72... | collective-permute-start | bytes 540680 | tf_op jit(solution)/shard_map/ppermute | solution.py:396
  37.6 10.9 %collective-permute-start.6 = (f32[176,128]{1,0:T(8,128)S(1)}, f32[176,128]{1,0:T(8,128)S(1)}, u32[]{:S(2)}, u32[]{:S(2)}) collective-permute-start(f32[176,128]{1,0:T(8,128)S(1)} %get-tuple-element.34), channel_id=1, source_target_pairs={{0,16},{8,24},{16,0},{24,8},{32,48},{40,56},{48,32},{56,40},{64,80... | collective-permute-start | bytes 270344 | tf_op jit(solution)/shard_map/ppermute | solution.py:399
  37.7 12.4 %collective-permute-start.7 = (f32[176,128]{1,0:T(8,128)S(1)}, f32[176,128]{1,0:T(8,128)S(1)}, u32[]{:S(2)}, u32[]{:S(2)}) collective-permute-start(f32[176,128]{1,0:T(8,128)S(1)} %get-tuple-element.35), channel_id=1, source_target_pairs={{16,32},{24,40},{32,16},{40,24},{48,64},{56,72},{64,48},{72,56},{8... | collective-permute-start | bytes 270344 | tf_op jit(solution)/shard_map/ppermute | solution.py:398
  42.6 5.9 %collective-permute-start.9 = (f32[8,1024]{1,0:T(8,128)S(1)}, f32[8,1024]{1,0:T(8,128)S(1)}, u32[]{:S(2)}, u32[]{:S(2)}) collective-permute-start(f32[8,1024]{1,0:T(8,128)S(1)} %get-tuple-element.36), channel_id=1, source_target_pairs={{1,2},{2,1},{3,4},{4,3},{5,6},{6,5},{9,10},{10,9},{11,12},{12,11},... | collective-permute-start | bytes 98312 | tf_op jit(solution)/shard_map/ppermute | solution.py:400
  45.1 3.4 %collective-permute-start.8 = (f32[8,1024]{1,0:T(8,128)S(1)}, f32[8,1024]{1,0:T(8,128)S(1)}, u32[]{:S(2)}, u32[]{:S(2)}) collective-permute-start(f32[8,1024]{1,0:T(8,128)S(1)} %get-tuple-element.36), channel_id=1, source_target_pairs={{0,1},{1,0},{2,3},{3,2},{4,5},{5,4},{6,7},{7,6},{8,9},{9,8},{10,11... | collective-permute-start | bytes 98312 | tf_op jit(solution)/shard_map/ppermute | solution.py:401

commit v2 on v1

v2 whole, which is shorter than its diff:
```python
import functools

import jax
import jax.numpy as jnp
from jax import lax
from jax.experimental import pallas as pl
from jax.experimental.pallas import tpu as pltpu
from jax.sharding import PartitionSpec as P

courant = 0.25
bimaterial = 0.5
slip_ref = 0.2
decay_rate = 0.5
impedance = 0.5

GX, GZ = "gx", "gz"
CHUNK = 8
CHUNK_COLUMNS = 1024
SPARE = 8
MIB = 2**20
FIRST_LIMIT = 12 * MIB


def swap_pairs(axis, distance, phase):
    size, pairs = lax.axis_size(axis), []
    for i in range(size):
        partner = i + distance if (i - phase) % (2 * distance) < distance else i - distance
        if 0 <= partner < size:
            pairs.append((i, partner))
    return pairs


def parities():
    block = lax.axis_index(GX)
    even = lax.rem(block, 2) == 0
    chip_even = lax.rem(lax.div(block, 2), 2) == 0
    depth_even = lax.rem(lax.axis_index(GZ), 2) == 0
    return even, chip_even, depth_even


def lane_of(shape):
    return lax.broadcasted_iota(jnp.int32, shape, len(shape) - 1)


def turned(value, shift):
    return pltpu.roll(value, shift % value.shape[-1], value.ndim - 1)


def depth_edges(edges, cells):
    packed, group = None, 8
    for place, (velocity, stress_z, rigidity) in enumerate(cells):
        base = place * group
        lane = lane_of(velocity.shape)
        if packed is None:
            packed = jnp.zeros(velocity.shape, velocity.dtype)
        packed = jnp.where(
            lane < base,
            packed,
            jnp.where(
                lane < base + 4,
                turned(velocity, base + 2),
                jnp.where(lane < base + 6, turned(stress_z, base + 5), turned(rigidity, base + 7)),
            ),
        )
    size = packed.shape[0] * packed.shape[1]
    rows = packed.reshape(size, -1).T
    for place in range(len(cells)):
        edges[:, place * size : (place + 1) * size] = rows[place * group : (place + 1) * group]


def depth_sides(own, near, far, chunks):
    _, _, depth_even = parities()
    left = lax.select(depth_even, far, near)
    right = lax.select(depth_even, near, far)
    scale = courant * 0.5
    stress_left = left[4:5] + scale * left[6:7] * (own[2:3] - left[0:1])
    stress_right = right[5:6] + scale * right[7:8] * (right[3:4] - own[1:2])
    rows = jnp.concatenate(
        [right[2:3], left[1:2], stress_right, stress_left, jnp.zeros_like(left[:4])], axis=0
    )
    size = rows.shape[1] // chunks
    pieces = [rows[:, place * size : (place + 1) * size] for place in range(chunks)]
    pieces.append(jnp.zeros((size - 8 * chunks, size), rows.dtype))
    return jnp.concatenate(pieces, axis=0).T


def strike_edge(target, base, velocity, rigidity, stress_x, inner, sign):
    target[base : base + 16] = velocity
    target[base + 16 : base + 32] = rigidity
    target[base + 32 : base + 48] = stress_x + (sign * courant * 0.5) * rigidity * inner


def deal(total, core, own, surface):
    nodes = total.shape[0] // 5
    for place, index in enumerate((0, 2, 4)):
        own[surface, place * nodes : (place + 1) * nodes] = total[
            index * nodes : (index + 1) * nodes
        ]
    base = surface * 2 * nodes
    core[base : base + nodes] = total[nodes : 2 * nodes]
    core[base + nodes : base + 2 * nodes] = total[3 * nodes : 4 * nodes]


def first_kernel(*refs):
    (velocity, stress, rigidity, cone, history, kernel), rest = refs[:6], refs[6:11]
    core, own, later, lead, edges, speed, tension, rigid = refs[11:19]
    rest_held = refs[19:24]
    limits, past, matrix, slab_sems, part_sems, rest_sems = refs[24:]
    surfaces, rows, columns = kernel.shape
    nodes, ny, width = velocity.shape
    offsets = rows // nodes
    reach = (offsets - 1) // 2
    parts = columns // CHUNK_COLUMNS

    slab = [
        pltpu.make_async_copy(source, target, slab_sems.at[place])
        for place, (source, target) in enumerate(
            ((cone, limits), (velocity, speed), (rigidity, rigid), (stress, tension))
        )
    ]
    fetches = [
        (
            pltpu.make_async_copy(history.at[s], past.at[s], part_sems.at[0, s]),
            pltpu.make_async_copy(kernel.at[s], matrix.at[s], part_sems.at[1, s]),
        )
        for s in range(surfaces)
    ]
    others = [
        pltpu.make_async_copy(source, target, rest_sems.at[place])
        for place, (source, target) in enumerate(zip(rest, rest_held))
    ]
    for copy in (*slab, *fetches[0], *fetches[1], *others):
        copy.start()
    for copy in slab:
        copy.wait()

    cells = [slice(at, at + CHUNK) for at in range(0, nodes, CHUNK)]
    depth_edges(edges, [(speed[c], tension[1, c], rigid[c]) for c in cells])
    base = 4 * nodes
    strike_edge(core, base, speed[0], rigid[0], tension[0, 0], speed[1], 1.0)
    strike_edge(
        core,
        base + 48,
        speed[nodes - 1],
        rigid[nodes - 1],
        tension[0, nodes - 1],
        speed[nodes - 2],
        -1.0,
    )

    block = lax.axis_index(GX)
    blocks = cone.shape[3]
    lag = lax.div(lane_of((1, CHUNK_COLUMNS)), nodes)
    for surface in range(surfaces):
        for copy in fetches[surface]:
            copy.wait()
        total = None
        for part in range(parts):
            at = part * CHUNK_COLUMNS
            masked = []
            for index in range(offsets):
                target = jnp.clip(block + (index - reach), 0, blocks - 1)
                first = limits[surface, index, 0, target]
                last = limits[surface, index, 1, target]
                now = lag + at // nodes
                keep = jnp.where((now >= first) & (now < last), 1.0, 0.0).astype(jnp.bfloat16)
                masked.append(
                    matrix[surface, index * nodes : (index + 1) * nodes, at : at + CHUNK_COLUMNS]
                    * keep
                )
            kept = jnp.concatenate(masked, axis=0)
            now = past[surface, at : at + CHUNK_COLUMNS]
            if part:
                before = past[surface, at - nodes : at + CHUNK_COLUMNS - nodes]
            else:
                before = jnp.concatenate(
                    [jnp.zeros((nodes, width), now.dtype), now[: CHUNK_COLUMNS - nodes]], axis=0
                )
                lead[surface] = kept[:, :nodes]
            both = jnp.concatenate([now, before], axis=1)
            product = jnp.dot(kept, both, preferred_element_type=jnp.float32)
            total = total + product if part else product
        later[surface] = total[:, width:]
        deal(total[:, :width], core, own, surface)
    for copy in others:
        copy.wait()


def pinned(x):
    return pltpu.with_memory_space_constraint(x, pltpu.HBM)


def first_call(velocity, stress, rigidity, cone, history, kernel, *rest):
    surfaces, rows, columns = kernel.shape
    nodes, ny, width = velocity.shape
    f32 = jnp.float32
    return pl.pallas_call(
        first_kernel,
        in_specs=[pl.BlockSpec(memory_space=pltpu.HBM)] * (6 + len(rest)),
        out_specs=[pl.BlockSpec(memory_space=pltpu.VMEM)] * (8 + len(rest)),
        out_shape=[
            jax.ShapeDtypeStruct((4 * nodes + 96, width), f32),
            jax.ShapeDtypeStruct((surfaces, 3 * nodes, width), f32),
            jax.ShapeDtypeStruct((surfaces, rows, width), f32),
            jax.ShapeDtypeStruct((surfaces, rows, nodes), jnp.bfloat16),
            jax.ShapeDtypeStruct((8, nodes * ny), f32),
        ]
        + [jax.ShapeDtypeStruct(x.shape, x.dtype) for x in (velocity, stress, rigidity, *rest)],
        scratch_shapes=[
            pltpu.SMEM(cone.shape, jnp.int32),
            pltpu.VMEM(history.shape, history.dtype),
            pltpu.VMEM(kernel.shape, kernel.dtype),
            pltpu.SemaphoreType.DMA((4,)),
            pltpu.SemaphoreType.DMA((2, surfaces)),
            pltpu.SemaphoreType.DMA((len(rest),)),
        ],
        compiler_params=pltpu.CompilerParams(vmem_limit_bytes=FIRST_LIMIT),
    )(*(pinned(x) for x in (velocity, stress, rigidity, cone, history, kernel, *rest)))


def relay_kernel(received, own, far, near):
    even, chip_even, _ = parities()
    nodes = own.shape[1] // 3
    right, left = [], []
    for surface in range(2):
        base = surface * 2 * nodes
        from_left = received[base : base + nodes]
        from_right = received[base + nodes : base + 2 * nodes]
        nothing = jnp.zeros_like(from_left)
        left.append(own[surface, :nodes] + lax.select(even, nothing, from_left))
        right.append(own[surface, 2 * nodes :] + lax.select(even, from_right, nothing))
    left.append(received[4 * nodes : 4 * nodes + 48])
    right.append(received[4 * nodes + 48 :])
    base = 0
    for to_left, to_right in zip(left, right):
        size = to_left.shape[0]
        near[base : base + size] = lax.select(chip_even, to_right, to_left)
        far[base : base + size] = lax.select(chip_even, to_left, to_right)
        base += size
    far[base:] = jnp.zeros_like(far[base:])


def relay_call(received, own):
    nodes, width = own.shape[1] // 3, own.shape[2]
    rows = 2 * nodes + 48
    return pl.pallas_call(
        relay_kernel,
        out_shape=[
            jax.ShapeDtypeStruct((rows + SPARE, width), jnp.float32),
            jax.ShapeDtypeStruct((rows, width), jnp.float32),
        ],
        compiler_params=pltpu.CompilerParams(vmem_limit_bytes=4 * MIB),
    )(received, own)


def step_kernel(last, *refs):
    (velocity, stress, stress_y, rigidity, buoyancy, sigma_star, sigma_zero, friction) = refs[:8]
    (received, near, far, depth_own, depth_near, depth_far, own) = refs[8:15]
    refs = refs[15:]
    if last:
        results, held, sems = refs[:5], refs[5:10], refs[10]
        velocity_new, stress_new, stress_y_new, state_new, bounds = held
        traction = refs[11]
        copies = []

        def send(sources, targets):
            for source, target in zip(sources, targets):
                copies.append(pltpu.make_async_copy(source, target, sems.at[len(copies)]))
                copies[-1].start()

    else:
        later, lead = refs[:2]
        velocity_new, stress_new, stress_y_new, state_new, core, own_new, edges = refs[2:9]
        traction, newest = refs[9:]
    even, chip_even, _ = parities()
    nodes, ny, width = velocity.shape
    chunks = nodes // CHUNK
    fault = ny // 2 - 1
    scale = courant * 0.5

    for surface in range(2):
        base = surface * 2 * nodes
        mate = lax.select(
            even, received[base : base + nodes], received[base + nodes : base + 2 * nodes]
        )
        rows = slice(surface * nodes, (surface + 1) * nodes)
        traction[surface] = own[surface, nodes : 2 * nodes] + mate + near[rows] + far[rows]

    near_halo, far_halo = (x[2 * nodes : 2 * nodes + 48] for x in (near, far))
    left = lax.select(
        even, lax.select(chip_even, far_halo, near_halo), received[4 * nodes + 48 :]
    )
    right = lax.select(
        even, received[4 * nodes : 4 * nodes + 48], lax.select(chip_even, near_halo, far_halo)
    )
    stress_left = left[32:] + scale * left[16:32] * velocity[0]
    stress_right = right[32:] - scale * right[16:32] * velocity[nodes - 1]
    sides = depth_sides(depth_own[...], depth_near[...], depth_far[...], chunks)

    shape = (CHUNK, ny, width)
    sides = sides.reshape(shape)
    lane = lane_of(shape)
    level = lax.broadcasted_iota(jnp.int32, shape, 1)

    def beside(ref, at, before, after):
        up = ref[at + 1 : min(at + CHUNK + 1, nodes)]
        down = ref[max(at - 1, 0) : at + CHUNK - 1]
        if at + CHUNK == nodes:
            up = jnp.concatenate([up, after[None]], axis=0)
        if at == 0:
            down = jnp.concatenate([before[None], down], axis=0)
        return up, down

    def stresses(at):
        cells = slice(at, at + CHUNK)
        here, rigid = velocity[cells], rigidity[cells]
        up, down = beside(velocity, at, left[:16], right[:16])
        stress_x = stress[0, cells] + scale * rigid * (up - down)
        stress_new[0, cells] = stress_x

        place = 8 * (at // CHUNK)
        side = turned(sides, -(place + 1))
        after = jnp.where(lane == width - 1, side, turned(here, -1))
        before = jnp.where(lane == 0, side, turned(here, 1))
        stress_z = stress[1, cells] + scale * rigid * (after - before)
        stress_new[1, cells] = stress_z
        side = turned(sides, -(place + 3))
        after = jnp.where(lane == width - 1, side, turned(stress_z, -1))
        before = jnp.where(lane == 0, side, turned(stress_z, 1))
        spreading = 0.5 * (after - before)

        if last:
            faces = stress_y[cells][:, : ny - 1]
        else:
            faces = jnp.stack(
                [stress_y[pl.ds(at + r, ny - 1, stride=nodes), :] for r in range(CHUNK)]
            )
        trial = faces + courant * (0.5 * (rigid[:, 1:] + rigid[:, :-1])) * (
            here[:, 1:] - here[:, :-1]
        )
        slip_rate = here[:, fault + 1] - here[:, fault]
        zero = sigma_zero[cells]
        normal = zero + bimaterial * jnp.tanh(stress_x[:, fault + 1] - stress_x[:, fault])
        state = normal + (sigma_star[cells] - normal) * jnp.exp(
            -(jnp.abs(slip_rate) + slip_ref) * decay_rate
        )
        state_new[cells] = state
        strength = friction[cells] * state
        clipped = jnp.clip(trial[:, fault], -strength, strength)
        bottom = traction[0, cells] + impedance * here[:, 0]
        top = traction[1, cells] - impedance * here[:, ny - 1]
        above = jnp.concatenate([trial, top[:, None]], axis=1)
        above = jnp.where(level == fault, clipped[:, None], above)
        if last:
            bounds[0, cells] = bottom
            bounds[1, cells] = top
            for r in range(CHUNK):
                stress_y_new[pl.ds(at + r, ny - 1, stride=nodes), :] = above[r, : ny - 1]
        else:
            stress_y_new[cells] = above
        below = jnp.where(level == 0, bottom[:, None], pltpu.roll(above, 1, 1))
        return spreading + above - below

    def velocities(at, partial):
        cells = slice(at, at + CHUNK)
        up, down = beside(stress_new.at[0], at, stress_left, stress_right)
        moved = velocity[cells] + courant * buoyancy[cells] * (0.5 * (up - down) + partial)
        velocity_new[cells] = moved
        if not last:
            newest[0, cells] = moved[:, 0]
            newest[1, cells] = moved[:, ny - 1]

    partial = stresses(0)
    for at in range(CHUNK, nodes, CHUNK):
        following = stresses(at)
        velocities(at - CHUNK, partial)
        partial = following
        if last and at == nodes // 2:
            half = pl.ds(0, at)
            send(
                [stress_new.at[:, half], velocity_new.at[pl.ds(0, at - CHUNK)]],
                [results[1].at[:, half], results[0].at[pl.ds(0, at - CHUNK)]],
            )
    if last:
        half = pl.ds(nodes // 2, nodes // 2)
        send(
            [stress_new.at[:, half], stress_y_new, state_new, bounds],
            [results[1].at[:, half], results[2], results[3], results[4]],
        )
    velocities(nodes - CHUNK, partial)
    if last:
        half = pl.ds(nodes // 2 - CHUNK, nodes // 2 + CHUNK)
        send([velocity_new.at[half]], [results[0].at[half]])
        for copy in copies:
            copy.wait()
        return

    for surface in range(2):
        fresh = newest[surface].astype(jnp.bfloat16)
        total = later[surface] + jnp.dot(
            lead[surface], fresh, preferred_element_type=jnp.float32
        )
        deal(total, core, own_new, surface)
    strike_edge(
        core, 4 * nodes, velocity_new[0], rigidity[0], stress_new[0, 0], velocity_new[1], 1.0
    )
    strike_edge(
        core,
        4 * nodes + 48,
        velocity_new[nodes - 1],
        rigidity[nodes - 1],
        stress_new[0, nodes - 1],
        velocity_new[nodes - 2],
        -1.0,
    )
    cells = [slice(at, at + CHUNK) for at in range(0, nodes, CHUNK)]
    depth_edges(edges, [(velocity_new[c], stress_new[1, c], rigidity[c]) for c in cells])


def step_call(last, *args):
    nodes, ny, width = args[0].shape
    f32 = jnp.float32
    shapes = [(nodes, ny, width), (2, nodes, ny, width)]
    if last:
        shapes += [(nodes * (ny - 1), width), (nodes, width), (2, nodes, width)]
        scratch = [pltpu.VMEM(shape, f32) for shape in shapes]
        scratch += [pltpu.SemaphoreType.DMA((7,)), pltpu.VMEM((2, nodes, width), f32)]
        out_specs = [pl.BlockSpec(memory_space=pltpu.HBM)] * len(shapes)
    else:
        shapes += [
            (nodes, ny, width),
            (nodes, width),
            (4 * nodes + 96, width),
            (2, 3 * nodes, width),
            (8, nodes * ny),
        ]
        scratch = [pltpu.VMEM((2, nodes, width), f32)] * 2
        out_specs = [pl.BlockSpec(memory_space=pltpu.VMEM)] * len(shapes)
    return pl.pallas_call(
        functools.partial(step_kernel, last),
        out_shape=[jax.ShapeDtypeStruct(shape, f32) for shape in shapes],
        out_specs=out_specs,
        scratch_shapes=scratch,
        compiler_params=pltpu.CompilerParams(vmem_limit_bytes=16 * MIB),
    )(*args)


def depth_exchange(edges):
    far = lax.ppermute(edges, GZ, swap_pairs(GZ, 1, 1))
    near = lax.ppermute(edges, GZ, swap_pairs(GZ, 1, 0))
    return near, far


def strike_exchange(core, own):
    received = lax.ppermute(core, GX, swap_pairs(GX, 1, 0))
    far, near = relay_call(received, own)
    far = lax.ppermute(far, GX, swap_pairs(GX, 2, 2))
    near = lax.ppermute(near, GX, swap_pairs(GX, 2, 0))
    return received, near, far


def local(
    velocity,
    stress_xz,
    stress_y,
    rigidity,
    buoyancy,
    sigma_star,
    sigma_zero,
    friction,
    history,
    kernel,
    cone,
):
    surfaces, lags, nodes, width = history.shape
    faces = stress_y.shape[1]
    past = history.reshape(surfaces, lags * nodes, width)
    matrix = kernel.reshape(surfaces, -1, kernel.shape[3])
    turned_cone = jnp.transpose(cone, (0, 2, 3, 1))
    face_rows = jnp.transpose(stress_y, (1, 0, 2)).reshape(faces * nodes, width)
    core, own, later, lead, edges, velocity, stress_xz, rigidity, *rest = first_call(
        velocity,
        stress_xz,
        rigidity,
        turned_cone,
        past,
        matrix,
        face_rows,
        buoyancy,
        sigma_star,
        sigma_zero,
        friction,
    )
    face_rows, buoyancy, sigma_star, sigma_zero, friction = rest
    moved = (*strike_exchange(core, own), edges, *depth_exchange(edges))
    velocity, stress_xz, stress_y, state, core, own, edges = step_call(
        False,
        velocity,
        stress_xz,
        face_rows,
        rigidity,
        buoyancy,
        sigma_star,
        sigma_zero,
        friction,
        *moved,
        own,
        later,
        lead,
    )
    moved = (*strike_exchange(core, own), edges, *depth_exchange(edges))
    velocity, stress_xz, face_rows, state, bounds = step_call(
        True,
        velocity,
        stress_xz,
        stress_y,
        rigidity,
        buoyancy,
        state,
        sigma_zero,
        friction,
        *moved,
        own,
    )
    stress_y = jnp.transpose(face_rows.reshape(faces, nodes, width), (1, 0, 2))
    return velocity, stress_xz, stress_y, state, bounds


def solution(mesh):
    in_specs = (
        P("gx", None, "gz"),
        P(None, "gx", None, "gz"),
        P("gx", None, "gz"),
        P("gx", None, "gz"),
        P("gx", None, "gz"),
        P("gx", "gz"),
        P("gx", "gz"),
        P("gx", "gz"),
        P(None, None, "gx", "gz"),
        P(),
        P(),
    )
    out_specs = (
        P("gx", None, "gz"),
        P(None, "gx", None, "gz"),
        P("gx", None, "gz"),
        P("gx", "gz"),
        P(None, "gx", "gz"),
    )
    return jax.shard_map(
        local, mesh=mesh, in_specs=in_specs, out_specs=tuple(out_specs), check_vma=False
    )
```

time: 54.9 us -> 43.8 us (0.80)
  the two profiles are of different devices: /device:TPU:95 before, /device:TPU:76 now
where the time goes in v2:
time: 43.8 us; the launch traced here: 43.5 us
  starting transfers between devices  23.5 us (54%)
  Pallas kernels  12.2 us (28%)
  waiting for transfers between devices  7.08 us (16%)
  between operations  0.7 us (2%)
    ppermute x2, starting transfers between devices, strike_exchange(): near = lax.ppermute(near, GX, swap_pairs(GX, 2, 0))  8.99 us
    pallas_call x1, Pallas kernels, first_call(): pl.pallas_call(first_kernel, in_specs=[pl.BlockSpec(memory_space=pltpu.HB...  7.69 us
    ppermute x2, starting transfers between devices, depth_exchange(): far = lax.ppermute(edges, GZ, swap_pairs(GZ, 1, 1))  5.59 us
    pallas_call x2, Pallas kernels, step_call(): pl.pallas_call(functools.partial(step_kernel, last), out_shape=[jax.Shape...  4.48 us
    ppermute x2, starting transfers between devices, depth_exchange(): near = lax.ppermute(edges, GZ, swap_pairs(GZ, 1, 0))  4.38 us
    ppermute x2, starting transfers between devices, strike_exchange(): far = lax.ppermute(far, GX, swap_pairs(GX, 2, 2))  4.36 us
    ppermute x2, waiting for transfers between devices, depth_exchange(): far = lax.ppermute(edges, GZ, swap_pairs(GZ, 1, 1))  3.41 us
    ppermute x2, waiting for transfers between devices, strike_exchange(): received = lax.ppermute(core, GX, swap_pairs(GX, 1, 0))  2.81 us
  transfers between devices with their start and end apart: 10, of which 6 were waited for; matrix products, arithmetic and copies ran while one was open for 0% of the time, Pallas kernels for 0%

profile of v2, /device:TPU:76, one launch (start us, length us, event | category | flops | bytes accessed | tf_op | source)
XLA Modules:
  0.0 43.5 jit_solution(17315482575375755701)
XLA Ops:
  0.6 7.7 %shard_map.146 = (f32[352,128]{1,0:T(8,128)S(1)}, f32[2,192,128]{2,1,0:T(8,128)S(1)}, f32[2,320,128]{2,1,0:T(8,128)S(1)}, bf16[2,320,64]{2,1,0:T(8,128)(2,1)S(1)...) custom-call(f32[64,16,128]{2,1,0:T(8,128)} %refs_0_.1, ...), custom_call_target="tpu_custom_call" | custom-call | tf_op jit(solution)/shard_map/pallas_call | solution.py:197
  8.3 0.1 collective-permute-start
  8.4 1.4 %collective-permute-done.received.refs_8_ = f32[352,128]{1,0:T(8,128)S(1)} collective-permute-done((f32[352,128]{1,0:T(8,128)S(1)}, f32[352,128]{1,0:T(8,128)S(1)}, u32[]{:S(2)}, u32[]{:S(2)}) %collective-permute-start) | collective-permute-done | bytes 180256 | tf_op jit(solution)/shard_map/ppermute | solution.py:455
  9.9 2.4 %collective-permute-start.2 = (f32[184,128]{1,0:T(8,128)S(1)}, f32[184,128]{1,0:T(8,128)S(1)}, u32[]{:S(2)}, u32[]{:S(2)}) collective-permute-start(f32[184,128]{1,0:T(8,128)S(1)} %get-tuple-element.45), channel_id=1, source_target_pairs={{16,32},{24,40},{32,16},{40,24},{48,64},{56,72},{64,48},{72,56},{8... | collective-permute-start | bytes 282632 | tf_op jit(solution)/shard_map/ppermute | solution.py:457
  12.3 5.1 %collective-permute-start.1 = (f32[176,128]{1,0:T(8,128)S(1)}, f32[176,128]{1,0:T(8,128)S(1)}, u32[]{:S(2)}, u32[]{:S(2)}) collective-permute-start(f32[176,128]{1,0:T(8,128)S(1)} %get-tuple-element.44), channel_id=1, source_target_pairs={{0,16},{8,24},{16,0},{24,8},{32,48},{40,56},{48,32},{56,40},{64,80... | collective-permute-start | bytes 270344 | tf_op jit(solution)/shard_map/ppermute | solution.py:458
  17.5 2.8 %collective-permute-start.4 = (f32[8,1024]{1,0:T(8,128)S(1)}, f32[8,1024]{1,0:T(8,128)S(1)}, u32[]{:S(2)}, u32[]{:S(2)}) collective-permute-start(f32[8,1024]{1,0:T(8,128)S(1)} %get-tuple-element.46.refs_11_), channel_id=1, source_target_pairs={{1,2},{2,1},{3,4},{4,3},{5,6},{6,5},{9,10},{10,9},{11,12},{12,11},... | collective-permute-start | bytes 98312 | tf_op jit(solution)/shard_map/ppermute | solution.py:449
  20.3 2.2 %collective-permute-start.3 = (f32[8,1024]{1,0:T(8,128)S(1)}, f32[8,1024]{1,0:T(8,128)S(1)}, u32[]{:S(2)}, u32[]{:S(2)}) collective-permute-start(f32[8,1024]{1,0:T(8,128)S(1)} %get-tuple-element.46.refs_11_), channel_id=1, source_target_pairs={{0,1},{1,0},{2,3},{3,2},{4,5},{5,4},{6,7},{7,6},{8,9},{9,8},{10,11... | collective-permute-start | bytes 98312 | tf_op jit(solution)/shard_map/ppermute | solution.py:450
  22.5 1.7 %collective-permute-done.4.refs_13_ = f32[8,1024]{1,0:T(8,128)S(1)} collective-permute-done((f32[8,1024]{1,0:T(8,128)S(1)}, f32[8,1024]{1,0:T(8,128)S(1)}, u32[]{:S(2)}, u32[]{:S(2)}) %collective-permute-start.4) | collective-permute-done | bytes 32800 | tf_op jit(solution)/shard_map/ppermute | solution.py:449
  24.2 0.5 %collective-permute-done.3.refs_12_ = f32[8,1024]{1,0:T(8,128)S(1)} collective-permute-done((f32[8,1024]{1,0:T(8,128)S(1)}, f32[8,1024]{1,0:T(8,128)S(1)}, u32[]{:S(2)}, u32[]{:S(2)}) %collective-permute-start.3) | collective-permute-done | bytes 32800 | tf_op jit(solution)/shard_map/ppermute | solution.py:450
  24.6 0.0 collective-permute-done.1.refs_9_
  24.6 0.0 collective-permute-done.2.refs_10_
  24.6 1.9 %shard_map.148 = (f32[64,16,128]{2,1,0:T(8,128)S(1)}, f32[2,64,16,128]{3,2,1,0:T(8,128)S(1)}, f32[64,16,128]{2,1,0:T(8,128)S(1)}, f32[64,128]{1,0:T(8,128)S(1)},...) custom-call(f32[64,16,128]{2,1,0:T(8,128)S(1)} %get-tuple-element.34.refs_0_, ...), custom_call_target="tpu_custom_call" | custom-call | tf_op jit(solution)/shard_map/pallas_call | solution.py:439
  26.5 0.1 collective-permute-start.5
  26.6 1.4 %collective-permute-done.5.received.refs_8_ = f32[352,128]{1,0:T(8,128)S(1)} collective-permute-done((f32[352,128]{1,0:T(8,128)S(1)}, f32[352,128]{1,0:T(8,128)S(1)}, u32[]{:S(2)}, u32[]{:S(2)}) %collective-permute-start.5) | collective-permute-done | bytes 180256 | tf_op jit(solution)/shard_map/ppermute | solution.py:455
  28.0 1.9 %collective-permute-start.7 = (f32[184,128]{1,0:T(8,128)S(1)}, f32[184,128]{1,0:T(8,128)S(1)}, u32[]{:S(2)}, u32[]{:S(2)}) collective-permute-start(f32[184,128]{1,0:T(8,128)S(1)} %get-tuple-element.56), channel_id=1, source_target_pairs={{16,32},{24,40},{32,16},{40,24},{48,64},{56,72},{64,48},{72,56},{8... | collective-permute-start | bytes 282632 | tf_op jit(solution)/shard_map/ppermute | solution.py:457
  30.0 3.8 %collective-permute-start.6 = (f32[176,128]{1,0:T(8,128)S(1)}, f32[176,128]{1,0:T(8,128)S(1)}, u32[]{:S(2)}, u32[]{:S(2)}) collective-permute-start(f32[176,128]{1,0:T(8,128)S(1)} %get-tuple-element.55), channel_id=1, source_target_pairs={{0,16},{8,24},{16,0},{24,8},{32,48},{40,56},{48,32},{56,40},{64,80... | collective-permute-start | bytes 270344 | tf_op jit(solution)/shard_map/ppermute | solution.py:458
  33.8 2.8 %collective-permute-start.9 = (f32[8,1024]{1,0:T(8,128)S(1)}, f32[8,1024]{1,0:T(8,128)S(1)}, u32[]{:S(2)}, u32[]{:S(2)}) collective-permute-start(f32[8,1024]{1,0:T(8,128)S(1)} %get-tuple-element.57.refs_11_), channel_id=1, source_target_pairs={{1,2},{2,1},{3,4},{4,3},{5,6},{6,5},{9,10},{10,9},{11,12},{12,11},... | collective-permute-start | bytes 98312 | tf_op jit(solution)/shard_map/ppermute | solution.py:449
  36.6 2.2 %collective-permute-start.8 = (f32[8,1024]{1,0:T(8,128)S(1)}, f32[8,1024]{1,0:T(8,128)S(1)}, u32[]{:S(2)}, u32[]{:S(2)}) collective-permute-start(f32[8,1024]{1,0:T(8,128)S(1)} %get-tuple-element.57.refs_11_), channel_id=1, source_target_pairs={{0,1},{1,0},{2,3},{3,2},{4,5},{5,4},{6,7},{7,6},{8,9},{9,8},{10,11... | collective-permute-start | bytes 98312 | tf_op jit(solution)/shard_map/ppermute | solution.py:450
  38.8 1.7 %collective-permute-done.9.refs_13_ = f32[8,1024]{1,0:T(8,128)S(1)} collective-permute-done((f32[8,1024]{1,0:T(8,128)S(1)}, f32[8,1024]{1,0:T(8,128)S(1)}, u32[]{:S(2)}, u32[]{:S(2)}) %collective-permute-start.9) | collective-permute-done | bytes 32800 | tf_op jit(solution)/shard_map/ppermute | solution.py:449
  40.5 0.4 collective-permute-done.8.refs_12_
  40.9 0.0 collective-permute-done.6.refs_9_
  40.9 0.0 collective-permute-done.7.refs_10_
  40.9 2.6 %shard_map.150 = (f32[64,16,128]{2,1,0:T(8,128)}, f32[2,64,16,128]{3,2,1,0:T(8,128)}, f32[960,128]{1,0:T(8,128)}, f32[64,128]{1,0:T(8,128)}, f32[2,64,128]{2,1,0:T(8,128)}) custom-call(f32[64,16,128]{2,1,0:T(8,128)S(1)} %get-tuple-element.49.refs_0_, f32[2,64,16,128]{3,2,1,0:T(8,128)S(1)} %get-tuple-element.50.refs_1_, ...), custom_call_target="tpu_custom_call" | custom-call | tf_op jit(solution)/shard_map/pallas_call | solution.py:439
  (2 shorter events, 0.1 us)
Async XLA Ops:
  8.3 1.5 %collective-permute-start = (f32[352,128]{1,0:T(8,128)S(1)}, f32[352,128]{1,0:T(8,128)S(1)}, u32[]{:S(2)}, u32[]{:S(2)}) collective-permute-start(f32[352,128]{1,0:T(8,128)S(1)} %get-tuple-element.42), channel_id=1, source_target_pairs={{0,8},{8,0},{16,24},{24,16},{32,40},{40,32},{48,56},{56,48},{64,72... | collective-permute-start | bytes 540680 | tf_op jit(solution)/shard_map/ppermute | solution.py:455
  9.9 14.8 %collective-permute-start.2 = (f32[184,128]{1,0:T(8,128)S(1)}, f32[184,128]{1,0:T(8,128)S(1)}, u32[]{:S(2)}, u32[]{:S(2)}) collective-permute-start(f32[184,128]{1,0:T(8,128)S(1)} %get-tuple-element.45), channel_id=1, source_target_pairs={{16,32},{24,40},{32,16},{40,24},{48,64},{56,72},{64,48},{72,56},{8... | collective-permute-start | bytes 282632 | tf_op jit(solution)/shard_map/ppermute | solution.py:457
  12.3 12.3 %collective-permute-start.1 = (f32[176,128]{1,0:T(8,128)S(1)}, f32[176,128]{1,0:T(8,128)S(1)}, u32[]{:S(2)}, u32[]{:S(2)}) collective-permute-start(f32[176,128]{1,0:T(8,128)S(1)} %get-tuple-element.44), channel_id=1, source_target_pairs={{0,16},{8,24},{16,0},{24,8},{32,48},{40,56},{48,32},{56,40},{64,80... | collective-permute-start | bytes 270344 | tf_op jit(solution)/shard_map/ppermute | solution.py:458
  17.5 6.7 %collective-permute-start.4 = (f32[8,1024]{1,0:T(8,128)S(1)}, f32[8,1024]{1,0:T(8,128)S(1)}, u32[]{:S(2)}, u32[]{:S(2)}) collective-permute-start(f32[8,1024]{1,0:T(8,128)S(1)} %get-tuple-element.46.refs_11_), channel_id=1, source_target_pairs={{1,2},{2,1},{3,4},{4,3},{5,6},{6,5},{9,10},{10,9},{11,12},{12,11},... | collective-permute-start | bytes 98312 | tf_op jit(solution)/shard_map/ppermute | solution.py:449
  20.3 4.4 %collective-permute-start.3 = (f32[8,1024]{1,0:T(8,128)S(1)}, f32[8,1024]{1,0:T(8,128)S(1)}, u32[]{:S(2)}, u32[]{:S(2)}) collective-permute-start(f32[8,1024]{1,0:T(8,128)S(1)} %get-tuple-element.46.refs_11_), channel_id=1, source_target_pairs={{0,1},{1,0},{2,3},{3,2},{4,5},{5,4},{6,7},{7,6},{8,9},{9,8},{10,11... | collective-permute-start | bytes 98312 | tf_op jit(solution)/shard_map/ppermute | solution.py:450
  26.5 1.5 %collective-permute-start.5 = (f32[352,128]{1,0:T(8,128)S(1)}, f32[352,128]{1,0:T(8,128)S(1)}, u32[]{:S(2)}, u32[]{:S(2)}) collective-permute-start(f32[352,128]{1,0:T(8,128)S(1)} %get-tuple-element.53), channel_id=1, source_target_pairs={{0,8},{8,0},{16,24},{24,16},{32,40},{40,32},{48,56},{56,48},{64,72... | collective-permute-start | bytes 540680 | tf_op jit(solution)/shard_map/ppermute | solution.py:455
  28.0 12.9 %collective-permute-start.7 = (f32[184,128]{1,0:T(8,128)S(1)}, f32[184,128]{1,0:T(8,128)S(1)}, u32[]{:S(2)}, u32[]{:S(2)}) collective-permute-start(f32[184,128]{1,0:T(8,128)S(1)} %get-tuple-element.56), channel_id=1, source_target_pairs={{16,32},{24,40},{32,16},{40,24},{48,64},{56,72},{64,48},{72,56},{8... | collective-permute-start | bytes 282632 | tf_op jit(solution)/shard_map/ppermute | solution.py:457
  30.0 10.9 %collective-permute-start.6 = (f32[176,128]{1,0:T(8,128)S(1)}, f32[176,128]{1,0:T(8,128)S(1)}, u32[]{:S(2)}, u32[]{:S(2)}) collective-permute-start(f32[176,128]{1,0:T(8,128)S(1)} %get-tuple-element.55), channel_id=1, source_target_pairs={{0,16},{8,24},{16,0},{24,8},{32,48},{40,56},{48,32},{56,40},{64,80... | collective-permute-start | bytes 270344 | tf_op jit(solution)/shard_map/ppermute | solution.py:458
  33.8 6.7 %collective-permute-start.9 = (f32[8,1024]{1,0:T(8,128)S(1)}, f32[8,1024]{1,0:T(8,128)S(1)}, u32[]{:S(2)}, u32[]{:S(2)}) collective-permute-start(f32[8,1024]{1,0:T(8,128)S(1)} %get-tuple-element.57.refs_11_), channel_id=1, source_target_pairs={{1,2},{2,1},{3,4},{4,3},{5,6},{6,5},{9,10},{10,9},{11,12},{12,11},... | collective-permute-start | bytes 98312 | tf_op jit(solution)/shard_map/ppermute | solution.py:449
  36.6 4.3 %collective-permute-start.8 = (f32[8,1024]{1,0:T(8,128)S(1)}, f32[8,1024]{1,0:T(8,128)S(1)}, u32[]{:S(2)}, u32[]{:S(2)}) collective-permute-start(f32[8,1024]{1,0:T(8,128)S(1)} %get-tuple-element.57.refs_11_), channel_id=1, source_target_pairs={{0,1},{1,0},{2,3},{3,2},{4,5},{5,4},{6,7},{7,6},{8,9},{9,8},{10,11... | collective-permute-start | bytes 98312 | tf_op jit(solution)/shard_map/ppermute | solution.py:450

commit v3 on v2

--- a/solution.py
+++ b/solution.py
@@ -16,7 +16,7 @@
 GX, GZ = "gx", "gz"
 CHUNK = 8
 CHUNK_COLUMNS = 1024
-SPARE = 8
+SPARE = 32
 MIB = 2**20
 FIRST_LIMIT = 12 * MIB
 
@@ -30,6 +30,15 @@
     return pairs
 
 
+def onward_pairs(axis):
+    size, pairs = lax.axis_size(axis), []
+    for i in range(size):
+        partner = i + 2 if i % 2 == 0 else i - 2
+        if 0 <= partner < size:
+            pairs.append((i, partner))
+    return pairs
+
+
 def parities():
     block = lax.axis_index(GX)
     even = lax.rem(block, 2) == 0
@@ -46,7 +55,7 @@
     return pltpu.roll(value, shift % value.shape[-1], value.ndim - 1)
 
 
-def depth_edges(edges, cells):
+def depth_edges(edges, edges_sent, cells):
     packed, group = None, 8
     for place, (velocity, stress_z, rigidity) in enumerate(cells):
         base = place * group
@@ -66,10 +75,15 @@
     rows = packed.reshape(size, -1).T
     for place in range(len(cells)):
         edges[:, place * size : (place + 1) * size] = rows[place * group : (place + 1) * group]
+    edges_sent[...] = rows[: edges_sent.shape[0]].astype(edges_sent.dtype)
 
 
 def depth_sides(own, near, far, chunks):
     _, _, depth_even = parities()
+    near, far = (
+        jnp.concatenate([x[at : at + 8] for at in range(0, x.shape[0], 8)], axis=1)
+        for x in (near.astype(jnp.float32), far.astype(jnp.float32))
+    )
     left = lax.select(depth_even, far, near)
     right = lax.select(depth_even, near, far)
     scale = courant * 0.5
@@ -103,9 +117,9 @@
 
 def first_kernel(*refs):
     (velocity, stress, rigidity, cone, history, kernel), rest = refs[:6], refs[6:11]
-    core, own, later, lead, edges, speed, tension, rigid = refs[11:19]
-    rest_held = refs[19:24]
-    limits, past, matrix, slab_sems, part_sems, rest_sems = refs[24:]
+    core, own, later, lead, edges, edges_sent, speed, tension, rigid = refs[11:20]
+    rest_held = refs[20:25]
+    limits, past, matrix, slab_sems, part_sems, rest_sems = refs[25:]
     surfaces, rows, columns = kernel.shape
     nodes, ny, width = velocity.shape
     offsets = rows // nodes
@@ -129,24 +143,11 @@
         pltpu.make_async_copy(source, target, rest_sems.at[place])
         for place, (source, target) in enumerate(zip(rest, rest_held))
     ]
-    for copy in (*slab, *fetches[0], *fetches[1], *others):
+    for copy in (slab[0], *fetches[0]):
         copy.start()
-    for copy in slab:
-        copy.wait()
-
-    cells = [slice(at, at + CHUNK) for at in range(0, nodes, CHUNK)]
-    depth_edges(edges, [(speed[c], tension[1, c], rigid[c]) for c in cells])
-    base = 4 * nodes
-    strike_edge(core, base, speed[0], rigid[0], tension[0, 0], speed[1], 1.0)
-    strike_edge(
-        core,
-        base + 48,
-        speed[nodes - 1],
-        rigid[nodes - 1],
-        tension[0, nodes - 1],
-        speed[nodes - 2],
-        -1.0,
-    )
+    slab[0].wait()
+    for copy in (*fetches[1], *slab[1:]):
+        copy.start()
 
     block = lax.axis_index(GX)
     blocks = cone.shape[3]
@@ -154,6 +155,9 @@
     for surface in range(surfaces):
         for copy in fetches[surface]:
             copy.wait()
+        if surface == 0:
+            for copy in others:
+                copy.start()
         total = None
         for part in range(parts):
             at = part * CHUNK_COLUMNS
@@ -182,6 +186,22 @@
             total = total + product if part else product
         later[surface] = total[:, width:]
         deal(total[:, :width], core, own, surface)
+        if surface == 0:
+            for copy in slab[1:]:
+                copy.wait()
+            cells = [slice(at, at + CHUNK) for at in range(0, nodes, CHUNK)]
+            depth_edges(edges, edges_sent, [(speed[c], tension[1, c], rigid[c]) for c in cells])
+            base = 4 * nodes
+            strike_edge(core, base, speed[0], rigid[0], tension[0, 0], speed[1], 1.0)
+            strike_edge(
+                core,
+                base + 48,
+                speed[nodes - 1],
+                rigid[nodes - 1],
+                tension[0, nodes - 1],
+                speed[nodes - 2],
+                -1.0,
+            )
     for copy in others:
         copy.wait()
 
@@ -197,13 +217,14 @@
     return pl.pallas_call(
         first_kernel,
         in_specs=[pl.BlockSpec(memory_space=pltpu.HBM)] * (6 + len(rest)),
-        out_specs=[pl.BlockSpec(memory_space=pltpu.VMEM)] * (8 + len(rest)),
+        out_specs=[pl.BlockSpec(memory_space=pltpu.VMEM)] * (9 + len(rest)),
         out_shape=[
             jax.ShapeDtypeStruct((4 * nodes + 96, width), f32),
             jax.ShapeDtypeStruct((surfaces, 3 * nodes, width), f32),
             jax.ShapeDtypeStruct((surfaces, rows, width), f32),
             jax.ShapeDtypeStruct((surfaces, rows, nodes), jnp.bfloat16),
             jax.ShapeDtypeStruct((8, nodes * ny), f32),
+            jax.ShapeDtypeStruct((nodes, width), jnp.bfloat16),
         ]
         + [jax.ShapeDtypeStruct(x.shape, x.dtype) for x in (velocity, stress, rigidity, *rest)],
         scratch_shapes=[
@@ -218,39 +239,60 @@
     )(*(pinned(x) for x in (velocity, stress, rigidity, cone, history, kernel, *rest)))
 
 
-def relay_kernel(received, own, far, near):
+def packed_into(target, parts):
+    base, powers = 0, []
+    for part in parts:
+        size = part.shape[0]
+        most = jnp.max(jnp.abs(part), axis=0, keepdims=True)
+        power = jnp.ceil(jnp.log2(jnp.maximum(most, 2.0**-100)))
+        powers.append(power)
+        target[base : base + size] = jnp.round(part * jnp.exp2(14.0 - power)).astype(jnp.int16)
+        base += size
+    powers.append(jnp.zeros((16 - len(powers), powers[0].shape[1]), jnp.float32))
+    target[base : base + 16] = jnp.concatenate(powers, axis=0).astype(jnp.int16)
+    if target.shape[0] > base + 16:
+        target[base + 16 :] = jnp.zeros_like(target[base + 16 :])
+
+
+def unpacked(source, nodes):
+    sizes = (nodes, nodes, 16, 16, 16)
+    base, parts = 0, []
+    last = sum(sizes)
+    scales = jnp.exp2(source[last : last + 16].astype(jnp.float32) - 14.0)
+    for place, size in enumerate(sizes):
+        part = source[base : base + size].astype(jnp.float32)
+        parts.append(part * scales[place : place + 1])
+        base += size
+    return parts
+
+
+def relay_kernel(near, received, own, *refs):
+    target = refs[-1]
     even, chip_even, _ = parities()
+    to_right = chip_even if near else jnp.logical_not(chip_even)
     nodes = own.shape[1] // 3
-    right, left = [], []
+    parts = []
     for surface in range(2):
         base = surface * 2 * nodes
         from_left = received[base : base + nodes]
         from_right = received[base + nodes : base + 2 * nodes]
         nothing = jnp.zeros_like(from_left)
-        left.append(own[surface, :nodes] + lax.select(even, nothing, from_left))
-        right.append(own[surface, 2 * nodes :] + lax.select(even, from_right, nothing))
-    left.append(received[4 * nodes : 4 * nodes + 48])
-    right.append(received[4 * nodes + 48 :])
-    base = 0
-    for to_left, to_right in zip(left, right):
-        size = to_left.shape[0]
-        near[base : base + size] = lax.select(chip_even, to_right, to_left)
-        far[base : base + size] = lax.select(chip_even, to_left, to_right)
-        base += size
-    far[base:] = jnp.zeros_like(far[base:])
-
-
-def relay_call(received, own):
+        left = own[surface, :nodes] + lax.select(even, nothing, from_left)
+        right = own[surface, 2 * nodes :] + lax.select(even, from_right, nothing)
+        parts.append(lax.select(to_right, right, left))
+    base = 4 * nodes
+    halo = lax.select(to_right, received[base + 48 :], received[base : base + 48])
+    packed_into(target, parts + [halo[at : at + 16] for at in (0, 16, 32)])
+
+
+def relay_call(near, received, own, *after):
     nodes, width = own.shape[1] // 3, own.shape[2]
-    rows = 2 * nodes + 48
+    rows = 2 * nodes + 64 + (0 if near else SPARE)
     return pl.pallas_call(
-        relay_kernel,
-        out_shape=[
-            jax.ShapeDtypeStruct((rows + SPARE, width), jnp.float32),
-            jax.ShapeDtypeStruct((rows, width), jnp.float32),
-        ],
+        functools.partial(relay_kernel, near),
+        out_shape=jax.ShapeDtypeStruct((rows, width), jnp.int16),
         compiler_params=pltpu.CompilerParams(vmem_limit_bytes=4 * MIB),
-    )(received, own)
+    )(received, own, *after)
 
 
 def step_kernel(last, *refs):
@@ -271,22 +313,25 @@
     else:
         later, lead = refs[:2]
         velocity_new, stress_new, stress_y_new, state_new, core, own_new, edges = refs[2:9]
-        traction, newest = refs[9:]
+        edges_sent, traction, newest = refs[9:]
     even, chip_even, _ = parities()
     nodes, ny, width = velocity.shape
     chunks = nodes // CHUNK
     fault = ny // 2 - 1
     scale = courant * 0.5
 
+    near_parts, far_parts = unpacked(near, nodes), unpacked(far, nodes)
     for surface in range(2):
         base = surface * 2 * nodes
         mate = lax.select(
             even, received[base : base + nodes], received[base + nodes : base + 2 * nodes]
         )
         rows = slice(surface * nodes, (surface + 1) * nodes)
-        traction[surface] = own[surface, nodes : 2 * nodes] + mate + near[rows] + far[rows]
-
-    near_halo, far_halo = (x[2 * nodes : 2 * nodes + 48] for x in (near, far))
+        traction[surface] = (
+            own[surface, nodes : 2 * nodes] + mate + (near_parts[surface] + far_parts[surface])
+        )
+
+    near_halo, far_halo = (jnp.concatenate(x[2:], axis=0) for x in (near_parts, far_parts))
     left = lax.select(
         even, lax.select(chip_even, far_halo, near_halo), received[4 * nodes + 48 :]
     )
@@ -414,7 +459,7 @@
         -1.0,
     )
     cells = [slice(at, at + CHUNK) for at in range(0, nodes, CHUNK)]
-    depth_edges(edges, [(velocity_new[c], stress_new[1, c], rigidity[c]) for c in cells])
+    depth_edges(edges, edges_sent, [(velocity_new[c], stress_new[1, c], rigidity[c]) for c in cells])
 
 
 def step_call(last, *args):
@@ -435,28 +480,27 @@
             (8, nodes * ny),
         ]
         scratch = [pltpu.VMEM((2, nodes, width), f32)] * 2
-        out_specs = [pl.BlockSpec(memory_space=pltpu.VMEM)] * len(shapes)
+        out_specs = [pl.BlockSpec(memory_space=pltpu.VMEM)] * (len(shapes) + 1)
+    out_shape = [jax.ShapeDtypeStruct(shape, f32) for shape in shapes]
+    if not last:
+        out_shape.append(jax.ShapeDtypeStruct((nodes, width), jnp.bfloat16))
     return pl.pallas_call(
         functools.partial(step_kernel, last),
-        out_shape=[jax.ShapeDtypeStruct(shape, f32) for shape in shapes],
+        out_shape=out_shape,
         out_specs=out_specs,
         scratch_shapes=scratch,
         compiler_params=pltpu.CompilerParams(vmem_limit_bytes=16 * MIB),
     )(*args)
 
 
-def depth_exchange(edges):
-    far = lax.ppermute(edges, GZ, swap_pairs(GZ, 1, 1))
-    near = lax.ppermute(edges, GZ, swap_pairs(GZ, 1, 0))
-    return near, far
-
-
-def strike_exchange(core, own):
+def exchange(core, own, edges, edges_sent):
     received = lax.ppermute(core, GX, swap_pairs(GX, 1, 0))
-    far, near = relay_call(received, own)
-    far = lax.ppermute(far, GX, swap_pairs(GX, 2, 2))
+    depth_near = lax.ppermute(edges_sent, GZ, swap_pairs(GZ, 1, 0))
+    far = lax.ppermute(relay_call(False, received, own), GX, swap_pairs(GX, 2, 2))
+    near = relay_call(True, received, own, depth_near)
     near = lax.ppermute(near, GX, swap_pairs(GX, 2, 0))
-    return received, near, far
+    depth_far = lax.ppermute(depth_near, GZ, onward_pairs(GZ))
+    return received, near, far, edges, depth_near, depth_far
 
 
 def local(
@@ -478,7 +522,7 @@
     matrix = kernel.reshape(surfaces, -1, kernel.shape[3])
     turned_cone = jnp.transpose(cone, (0, 2, 3, 1))
     face_rows = jnp.transpose(stress_y, (1, 0, 2)).reshape(faces * nodes, width)
-    core, own, later, lead, edges, velocity, stress_xz, rigidity, *rest = first_call(
+    core, own, later, lead, edges, sent, velocity, stress_xz, rigidity, *rest = first_call(
         velocity,
         stress_xz,
         rigidity,
@@ -492,8 +536,8 @@
         friction,
     )
     face_rows, buoyancy, sigma_star, sigma_zero, friction = rest
-    moved = (*strike_exchange(core, own), edges, *depth_exchange(edges))
-    velocity, stress_xz, stress_y, state, core, own, edges = step_call(
+    moved = exchange(core, own, edges, sent)
+    velocity, stress_xz, stress_y, state, core, own, edges, sent = step_call(
         False,
         velocity,
         stress_xz,
@@ -508,7 +552,7 @@
         later,
         lead,
     )
-    moved = (*strike_exchange(core, own), edges, *depth_exchange(edges))
+    moved = exchange(core, own, edges, sent)
     velocity, stress_xz, face_rows, state, bounds = step_call(
         True,
         velocity,

time: 43.8 us -> 39.1 us (0.89)
  waiting for transfers between devices: 7.08 us -> 5.02 us
  Pallas kernels: 12.2 us -> 10.8 us
  starting transfers between devices: 23.5 us -> 22.3 us
    ppermute x10, waiting for transfers between devices: 7.08 us -> 5.02 us  [the longest x2 4.28 us: exchange(): depth_far = lax.ppermute(depth_near, GZ, onward_pairs(GZ))]
    pallas_call x1, Pallas kernels: 7.69 us -> 6.07 us  [first_call(): pl.pallas_call(first_kernel, in_specs=[pl.BlockSpec(memory_space=pltpu.HB...]
    ppermute x10, starting transfers between devices: 23.5 us -> 22.3 us  [the longest x2 7.69 us: exchange(): near = lax.ppermute(near, GX, swap_pairs(GX, 2, 0))]
    pallas_call x4 -> x6, Pallas kernels: 4.53 us -> 4.73 us  [the longest x2 4.49 us: step_call(): pl.pallas_call(functools.partial(step_kernel, last), out_shape=out_shape,...]
  transfers between devices with their start and end apart: 10 -> 10, of which waited for: 6 -> 4; matrix products, arithmetic and copies ran while one was open for 0% -> 0% of each run, Pallas kernels for 0% -> 1%
where the time goes in v3:
time: 39.1 us; the launch traced here: 38.9 us
  starting transfers between devices  22.3 us (57%)
  Pallas kernels  10.8 us (28%)
  waiting for transfers between devices  5.02 us (13%)
  between operations  0.74 us (2%)
    ppermute x2, starting transfers between devices, exchange(): near = lax.ppermute(near, GX, swap_pairs(GX, 2, 0))  7.69 us
    ppermute x2, starting transfers between devices, exchange(): depth_far = lax.ppermute(depth_near, GZ, onward_pairs(GZ))  6.95 us
    pallas_call x1, Pallas kernels, first_call(): pl.pallas_call(first_kernel, in_specs=[pl.BlockSpec(memory_space=pltpu.HB...  6.07 us
    pallas_call x2, Pallas kernels, step_call(): pl.pallas_call(functools.partial(step_kernel, last), out_shape=out_shape,...  4.49 us
    ppermute x2, starting transfers between devices, exchange(): lax.ppermute(relay_call(False, received, own), GX, swap_pairs(GX, 2, 2))  4.36 us
    ppermute x2, waiting for transfers between devices, exchange(): depth_far = lax.ppermute(depth_near, GZ, onward_pairs(GZ))  4.28 us
    ppermute x2, starting transfers between devices, exchange(): depth_near = lax.ppermute(edges_sent, GZ, swap_pairs(GZ, 1, 0))  3.11 us
  transfers between devices with their start and end apart: 10, of which 4 were waited for; matrix products, arithmetic and copies ran while one was open for 0% of the time, Pallas kernels for 1%

profile of v3, /device:TPU:76, one launch (start us, length us, event | category | flops | bytes accessed | tf_op | source)
XLA Modules:
  0.0 38.9 jit_solution(398128306044103177)
XLA Ops:
  0.6 6.1 %shard_map.146 = (f32[352,128]{1,0:T(8,128)S(1)}, f32[2,192,128]{2,1,0:T(8,128)S(1)}, f32[2,320,128]{2,1,0:T(8,128)S(1)}, bf16[2,320,64]{2,1,0:T(8,128)(2,1)S(1)...) custom-call(f32[64,16,128]{2,1,0:T(8,128)} %refs_0_.1, ...), custom_call_target="tpu_custom_call" | custom-call | tf_op jit(solution)/shard_map/pallas_call | solution.py:217
  6.7 0.1 collective-permute-start
  6.8 2.0 %collective-permute-start.1 = (bf16[64,128]{1,0:T(8,128)(2,1)S(1)}, bf16[64,128]{1,0:T(8,128)(2,1)S(1)}, u32[]{:S(2)}, u32[]{:S(2)}) collective-permute-start(bf16[64,128]{1,0:T(8,128)(2,1)S(1)} %get-tuple-element.42), channel_id=1, source_target_pairs={{0,1},{1,0},{2,3},{3,2},{4,5},{5,4},{6,7},{7,6},{8,9},{9,8},{10,11... | collective-permute-start | bytes 49160 | tf_op jit(solution)/shard_map/ppermute | solution.py:498
  8.8 0.0 collective-permute-done.received.refs_8_
  8.8 0.1 shard_map.148
  8.9 2.4 %collective-permute-start.3 = (s16[224,128]{1,0:T(8,128)(2,1)S(1)}, s16[224,128]{1,0:T(8,128)(2,1)S(1)}, u32[]{:S(2)}, u32[]{:S(2)}) collective-permute-start(s16[224,128]{1,0:T(8,128)(2,1)S(1)} %shard_map.148), channel_id=1, source_target_pairs={{16,32},{24,40},{32,16},{40,24},{48,64},{56,72},{64,48},{72,56},{8... | collective-permute-start | bytes 172040 | tf_op jit(solution)/shard_map/ppermute | solution.py:499
  11.3 0.0 collective-permute-done.1.refs_0_.refs_12_
  11.4 0.1 shard_map.147
  11.4 4.5 %collective-permute-start.2 = (s16[192,128]{1,0:T(8,128)(2,1)S(1)}, s16[192,128]{1,0:T(8,128)(2,1)S(1)}, u32[]{:S(2)}, u32[]{:S(2)}) collective-permute-start(s16[192,128]{1,0:T(8,128)(2,1)S(1)} %shard_map.147), channel_id=1, source_target_pairs={{0,16},{8,24},{16,0},{24,8},{32,48},{40,56},{48,32},{56,40},{64,80... | collective-permute-start | bytes 147464 | tf_op jit(solution)/shard_map/ppermute | solution.py:501
  16.0 3.5 %collective-permute-start.4 = (bf16[64,128]{1,0:T(8,128)(2,1)S(1)}, bf16[64,128]{1,0:T(8,128)(2,1)S(1)}, u32[]{:S(2)}, u32[]{:S(2)}) collective-permute-start(bf16[64,128]{1,0:T(8,128)(2,1)S(1)} %collective-permute-done.1.refs_0_.refs_12_), channel_id=1, source_target_pairs={{0,2},{2,4},{3,1},{4,6},{5,3},{7,5},{8,10},{10,12},{11,9},{12,14},... | collective-permute-start | bytes 49160 | tf_op jit(solution)/shard_map/ppermute | solution.py:502
  19.5 2.1 %collective-permute-done.4.refs_13_ = bf16[64,128]{1,0:T(8,128)(2,1)S(1)} collective-permute-done((bf16[64,128]{1,0:T(8,128)(2,1)S(1)}, bf16[64,128]{1,0:T(8,128)(2,1)S(1)}, u32[]{:S(2)}, u32[]{:S(2)}) %collective-permute-start.4) | collective-permute-done | bytes 16416 | tf_op jit(solution)/shard_map/ppermute | solution.py:502
  21.6 0.0 collective-permute-done.2.refs_9_
  21.6 0.0 collective-permute-done.3.refs_10_
  21.6 1.9 %shard_map.149 = (f32[64,16,128]{2,1,0:T(8,128)S(1)}, f32[2,64,16,128]{3,2,1,0:T(8,128)S(1)}, f32[64,16,128]{2,1,0:T(8,128)S(1)}, f32[64,128]{1,0:T(8,128)S(1)},...) custom-call(f32[64,16,128]{2,1,0:T(8,128)S(1)} %get-tuple-element.32., ...), custom_call_target="tpu_custom_call" | custom-call | tf_op jit(solution)/shard_map/pallas_call | solution.py:487
  23.5 0.1 collective-permute-start.5
  23.6 1.1 %collective-permute-start.6 = (bf16[64,128]{1,0:T(8,128)(2,1)S(1)}, bf16[64,128]{1,0:T(8,128)(2,1)S(1)}, u32[]{:S(2)}, u32[]{:S(2)}) collective-permute-start(bf16[64,128]{1,0:T(8,128)(2,1)S(1)} %get-tuple-element.52), channel_id=1, source_target_pairs={{0,1},{1,0},{2,3},{3,2},{4,5},{5,4},{6,7},{7,6},{8,9},{9,8},{10,11... | collective-permute-start | bytes 49160 | tf_op jit(solution)/shard_map/ppermute | solution.py:498
  24.7 0.3 collective-permute-done.5.received.refs_8_
  25.0 0.1 shard_map.151
  25.1 1.9 %collective-permute-start.8 = (s16[224,128]{1,0:T(8,128)(2,1)S(1)}, s16[224,128]{1,0:T(8,128)(2,1)S(1)}, u32[]{:S(2)}, u32[]{:S(2)}) collective-permute-start(s16[224,128]{1,0:T(8,128)(2,1)S(1)} %shard_map.151), channel_id=1, source_target_pairs={{16,32},{24,40},{32,16},{40,24},{48,64},{56,72},{64,48},{72,56},{8... | collective-permute-start | bytes 172040 | tf_op jit(solution)/shard_map/ppermute | solution.py:499
  27.0 0.4 %collective-permute-done.6.refs_0_.refs_12_ = bf16[64,128]{1,0:T(8,128)(2,1)S(1)} collective-permute-done((bf16[64,128]{1,0:T(8,128)(2,1)S(1)}, bf16[64,128]{1,0:T(8,128)(2,1)S(1)}, u32[]{:S(2)}, u32[]{:S(2)}) %collective-permute-start.6) | collective-permute-done | bytes 16416 | tf_op jit(solution)/shard_map/ppermute | solution.py:498
  27.5 0.1 shard_map.150
  27.5 3.1 %collective-permute-start.7 = (s16[192,128]{1,0:T(8,128)(2,1)S(1)}, s16[192,128]{1,0:T(8,128)(2,1)S(1)}, u32[]{:S(2)}, u32[]{:S(2)}) collective-permute-start(s16[192,128]{1,0:T(8,128)(2,1)S(1)} %shard_map.150), channel_id=1, source_target_pairs={{0,16},{8,24},{16,0},{24,8},{32,48},{40,56},{48,32},{56,40},{64,80... | collective-permute-start | bytes 147464 | tf_op jit(solution)/shard_map/ppermute | solution.py:501
  30.7 3.5 %collective-permute-start.9 = (bf16[64,128]{1,0:T(8,128)(2,1)S(1)}, bf16[64,128]{1,0:T(8,128)(2,1)S(1)}, u32[]{:S(2)}, u32[]{:S(2)}) collective-permute-start(bf16[64,128]{1,0:T(8,128)(2,1)S(1)} %collective-permute-done.6.refs_0_.refs_12_), channel_id=1, source_target_pairs={{0,2},{2,4},{3,1},{4,6},{5,3},{7,5},{8,10},{10,12},{11,9},{12,14},... | collective-permute-start | bytes 49160 | tf_op jit(solution)/shard_map/ppermute | solution.py:502
  34.1 2.1 %collective-permute-done.9.refs_13_ = bf16[64,128]{1,0:T(8,128)(2,1)S(1)} collective-permute-done((bf16[64,128]{1,0:T(8,128)(2,1)S(1)}, bf16[64,128]{1,0:T(8,128)(2,1)S(1)}, u32[]{:S(2)}, u32[]{:S(2)}) %collective-permute-start.9) | collective-permute-done | bytes 16416 | tf_op jit(solution)/shard_map/ppermute | solution.py:502
  36.3 0.0 collective-permute-done.7.refs_9_
  36.3 0.0 collective-permute-done.8.refs_10_
  36.3 2.6 %shard_map.152 = (f32[64,16,128]{2,1,0:T(8,128)}, f32[2,64,16,128]{3,2,1,0:T(8,128)}, f32[960,128]{1,0:T(8,128)}, f32[64,128]{1,0:T(8,128)}, f32[2,64,128]{2,1,0:T(8,128)}) custom-call(f32[64,16,128]{2,1,0:T(8,128)S(1)} %get-tuple-element.46.refs_0_, f32[2,64,16,128]{3,2,1,0:T(8,128)S(1)} %get-tuple-element.47.refs_1_, ...), custom_call_target="tpu_custom_call" | custom-call | tf_op jit(solution)/shard_map/pallas_call | solution.py:487
Async XLA Ops:
  6.7 2.1 %collective-permute-start = (f32[352,128]{1,0:T(8,128)S(1)}, f32[352,128]{1,0:T(8,128)S(1)}, u32[]{:S(2)}, u32[]{:S(2)}) collective-permute-start(f32[352,128]{1,0:T(8,128)S(1)} %get-tuple-element.40), channel_id=1, source_target_pairs={{0,8},{8,0},{16,24},{24,16},{32,40},{40,32},{48,56},{56,48},{64,72... | collective-permute-start | bytes 540680 | tf_op jit(solution)/shard_map/ppermute | solution.py:497
  6.8 4.5 %collective-permute-start.1 = (bf16[64,128]{1,0:T(8,128)(2,1)S(1)}, bf16[64,128]{1,0:T(8,128)(2,1)S(1)}, u32[]{:S(2)}, u32[]{:S(2)}) collective-permute-start(bf16[64,128]{1,0:T(8,128)(2,1)S(1)} %get-tuple-element.42), channel_id=1, source_target_pairs={{0,1},{1,0},{2,3},{3,2},{4,5},{5,4},{6,7},{7,6},{8,9},{9,8},{10,11... | collective-permute-start | bytes 49160 | tf_op jit(solution)/shard_map/ppermute | solution.py:498
  8.9 12.7 %collective-permute-start.3 = (s16[224,128]{1,0:T(8,128)(2,1)S(1)}, s16[224,128]{1,0:T(8,128)(2,1)S(1)}, u32[]{:S(2)}, u32[]{:S(2)}) collective-permute-start(s16[224,128]{1,0:T(8,128)(2,1)S(1)} %shard_map.148), channel_id=1, source_target_pairs={{16,32},{24,40},{32,16},{40,24},{48,64},{56,72},{64,48},{72,56},{8... | collective-permute-start | bytes 172040 | tf_op jit(solution)/shard_map/ppermute | solution.py:499
  11.4 10.2 %collective-permute-start.2 = (s16[192,128]{1,0:T(8,128)(2,1)S(1)}, s16[192,128]{1,0:T(8,128)(2,1)S(1)}, u32[]{:S(2)}, u32[]{:S(2)}) collective-permute-start(s16[192,128]{1,0:T(8,128)(2,1)S(1)} %shard_map.147), channel_id=1, source_target_pairs={{0,16},{8,24},{16,0},{24,8},{32,48},{40,56},{48,32},{56,40},{64,80... | collective-permute-start | bytes 147464 | tf_op jit(solution)/shard_map/ppermute | solution.py:501
  16.0 5.6 %collective-permute-start.4 = (bf16[64,128]{1,0:T(8,128)(2,1)S(1)}, bf16[64,128]{1,0:T(8,128)(2,1)S(1)}, u32[]{:S(2)}, u32[]{:S(2)}) collective-permute-start(bf16[64,128]{1,0:T(8,128)(2,1)S(1)} %collective-permute-done.1.refs_0_.refs_12_), channel_id=1, source_target_pairs={{0,2},{2,4},{3,1},{4,6},{5,3},{7,5},{8,10},{10,12},{11,9},{12,14},... | collective-permute-start | bytes 49160 | tf_op jit(solution)/shard_map/ppermute | solution.py:502
  23.5 1.5 %collective-permute-start.5 = (f32[352,128]{1,0:T(8,128)S(1)}, f32[352,128]{1,0:T(8,128)S(1)}, u32[]{:S(2)}, u32[]{:S(2)}) collective-permute-start(f32[352,128]{1,0:T(8,128)S(1)} %get-tuple-element.50), channel_id=1, source_target_pairs={{0,8},{8,0},{16,24},{24,16},{32,40},{40,32},{48,56},{56,48},{64,72... | collective-permute-start | bytes 540680 | tf_op jit(solution)/shard_map/ppermute | solution.py:497
  23.6 3.8 %collective-permute-start.6 = (bf16[64,128]{1,0:T(8,128)(2,1)S(1)}, bf16[64,128]{1,0:T(8,128)(2,1)S(1)}, u32[]{:S(2)}, u32[]{:S(2)}) collective-permute-start(bf16[64,128]{1,0:T(8,128)(2,1)S(1)} %get-tuple-element.52), channel_id=1, source_target_pairs={{0,1},{1,0},{2,3},{3,2},{4,5},{5,4},{6,7},{7,6},{8,9},{9,8},{10,11... | collective-permute-start | bytes 49160 | tf_op jit(solution)/shard_map/ppermute | solution.py:498
  25.1 11.2 %collective-permute-start.8 = (s16[224,128]{1,0:T(8,128)(2,1)S(1)}, s16[224,128]{1,0:T(8,128)(2,1)S(1)}, u32[]{:S(2)}, u32[]{:S(2)}) collective-permute-start(s16[224,128]{1,0:T(8,128)(2,1)S(1)} %shard_map.151), channel_id=1, source_target_pairs={{16,32},{24,40},{32,16},{40,24},{48,64},{56,72},{64,48},{72,56},{8... | collective-permute-start | bytes 172040 | tf_op jit(solution)/shard_map/ppermute | solution.py:499
  27.5 8.8 %collective-permute-start.7 = (s16[192,128]{1,0:T(8,128)(2,1)S(1)}, s16[192,128]{1,0:T(8,128)(2,1)S(1)}, u32[]{:S(2)}, u32[]{:S(2)}) collective-permute-start(s16[192,128]{1,0:T(8,128)(2,1)S(1)} %shard_map.150), channel_id=1, source_target_pairs={{0,16},{8,24},{16,0},{24,8},{32,48},{40,56},{48,32},{56,40},{64,80... | collective-permute-start | bytes 147464 | tf_op jit(solution)/shard_map/ppermute | solution.py:501
  30.7 5.6 %collective-permute-start.9 = (bf16[64,128]{1,0:T(8,128)(2,1)S(1)}, bf16[64,128]{1,0:T(8,128)(2,1)S(1)}, u32[]{:S(2)}, u32[]{:S(2)}) collective-permute-start(bf16[64,128]{1,0:T(8,128)(2,1)S(1)} %collective-permute-done.6.refs_0_.refs_12_), channel_id=1, source_target_pairs={{0,2},{2,4},{3,1},{4,6},{5,3},{7,5},{8,10},{10,12},{11,9},{12,14},... | collective-permute-start | bytes 49160 | tf_op jit(solution)/shard_map/ppermute | solution.py:502

commit v4 on v3

--- a/solution.py
+++ b/solution.py
@@ -89,9 +89,11 @@
     scale = courant * 0.5
     stress_left = left[4:5] + scale * left[6:7] * (own[2:3] - left[0:1])
     stress_right = right[5:6] + scale * right[7:8] * (right[3:4] - own[1:2])
-    rows = jnp.concatenate(
-        [right[2:3], left[1:2], stress_right, stress_left, jnp.zeros_like(left[:4])], axis=0
-    )
+    first = -scale * own[7:8] * left[1:2]
+    last = scale * own[6:7] * right[2:3]
+    nothing = jnp.zeros_like(first)
+    rows = [0.5 * last, 0.5 * stress_right, -0.5 * stress_left, -0.5 * first]
+    rows = jnp.concatenate([*rows, last, first, nothing, nothing], axis=0)
     size = rows.shape[1] // chunks
     pieces = [rows[:, place * size : (place + 1) * size] for place in range(chunks)]
     pieces.append(jnp.zeros((size - 8 * chunks, size), rows.dtype))
@@ -140,7 +142,7 @@
         for s in range(surfaces)
     ]
     others = [
-        pltpu.make_async_copy(source, target, rest_sems.at[place])
+        pltpu.make_async_copy(source, target.at[pl.ds(0, source.shape[0])], rest_sems.at[place])
         for place, (source, target) in enumerate(zip(rest, rest_held))
     ]
     for copy in (slab[0], *fetches[0]):
@@ -158,6 +160,22 @@
         if surface == 0:
             for copy in others:
                 copy.start()
+        else:
+            for copy in slab[1:]:
+                copy.wait()
+            cells = [slice(at, at + CHUNK) for at in range(0, nodes, CHUNK)]
+            depth_edges(edges, edges_sent, [(speed[c], tension[1, c], rigid[c]) for c in cells])
+            base = 4 * nodes
+            strike_edge(core, base, speed[0], rigid[0], tension[0, 0], speed[1], 1.0)
+            strike_edge(
+                core,
+                base + 48,
+                speed[nodes - 1],
+                rigid[nodes - 1],
+                tension[0, nodes - 1],
+                speed[nodes - 2],
+                -1.0,
+            )
         total = None
         for part in range(parts):
             at = part * CHUNK_COLUMNS
@@ -186,22 +204,6 @@
             total = total + product if part else product
         later[surface] = total[:, width:]
         deal(total[:, :width], core, own, surface)
-        if surface == 0:
-            for copy in slab[1:]:
-                copy.wait()
-            cells = [slice(at, at + CHUNK) for at in range(0, nodes, CHUNK)]
-            depth_edges(edges, edges_sent, [(speed[c], tension[1, c], rigid[c]) for c in cells])
-            base = 4 * nodes
-            strike_edge(core, base, speed[0], rigid[0], tension[0, 0], speed[1], 1.0)
-            strike_edge(
-                core,
-                base + 48,
-                speed[nodes - 1],
-                rigid[nodes - 1],
-                tension[0, nodes - 1],
-                speed[nodes - 2],
-                -1.0,
-            )
     for copy in others:
         copy.wait()
 
@@ -226,7 +228,11 @@
             jax.ShapeDtypeStruct((8, nodes * ny), f32),
             jax.ShapeDtypeStruct((nodes, width), jnp.bfloat16),
         ]
-        + [jax.ShapeDtypeStruct(x.shape, x.dtype) for x in (velocity, stress, rigidity, *rest)],
+        + [
+            jax.ShapeDtypeStruct(shape, f32)
+            for shape in (velocity.shape, stress.shape, rigidity.shape, (nodes * ny, width))
+        ]
+        + [jax.ShapeDtypeStruct(x.shape, f32) for x in rest[1:]],
         scratch_shapes=[
             pltpu.SMEM(cone.shape, jnp.int32),
             pltpu.VMEM(history.shape, history.dtype),
@@ -295,39 +301,129 @@
     )(received, own, *after)
 
 
+def beside(ref, at):
+    nodes = ref.shape[0]
+    up = ref[at + 1 : min(at + CHUNK + 1, nodes)]
+    down = ref[max(at - 1, 0) : at + CHUNK - 1]
+    nothing = jnp.zeros((1, *ref.shape[1:]), jnp.float32)
+    if at + CHUNK == nodes:
+        up = jnp.concatenate([up, nothing], axis=0)
+    if at == 0:
+        down = jnp.concatenate([nothing, down], axis=0)
+    return up, down
+
+
+def inner_kernel(last, *refs):
+    velocity, stress, stress_y, rigidity, buoyancy = refs[:5]
+    if last:
+        stiffness, moved, stress_new, faces_new = refs[5:]
+    else:
+        moved, stress_new, faces_new, stiffness = refs[5:]
+    nodes, ny, width = velocity.shape
+    scale = courant * 0.5
+    shape = (CHUNK, ny, width)
+    lane = lane_of(shape)
+    level = lax.broadcasted_iota(jnp.int32, shape, 1)
+
+    def across(value):
+        after = jnp.where(lane == width - 1, 0.0, turned(value, -1))
+        before = jnp.where(lane == 0, 0.0, turned(value, 1))
+        return after - before
+
+    def stresses(at):
+        cells = slice(at, at + CHUNK)
+        here, rigid = velocity[cells], rigidity[cells]
+        up, down = beside(velocity, at)
+        stress_new[0, cells] = stress[0, cells] + scale * rigid * (up - down)
+        stress_z = stress[1, cells] + scale * rigid * across(here)
+        stress_new[1, cells] = stress_z
+        if last:
+            faces, stiff = stress_y[cells], stiffness[cells]
+        else:
+            faces = jnp.stack(
+                [stress_y[pl.ds(at + r, ny, stride=nodes), :] for r in range(CHUNK)]
+            )
+            stiff = courant * (0.5 * (pltpu.roll(rigid, ny - 1, 1) + rigid))
+            stiffness[cells] = stiff
+        trial = faces + stiff * (pltpu.roll(here, ny - 1, 1) - here)
+        trial = jnp.where(level == ny - 1, 0.0, trial)
+        if last:
+            for r in range(CHUNK):
+                faces_new[pl.ds(at + r, ny, stride=nodes), :] = trial[r]
+        else:
+            faces_new[cells] = trial
+        return 0.5 * across(stress_z) + trial - pltpu.roll(trial, 1, 1)
+
+    def velocities(at, partial):
+        cells = slice(at, at + CHUNK)
+        up, down = beside(stress_new.at[0], at)
+        moved[cells] = velocity[cells] + courant * buoyancy[cells] * (0.5 * (up - down) + partial)
+
+    partial = stresses(0)
+    for at in range(CHUNK, nodes, CHUNK):
+        following = stresses(at)
+        velocities(at - CHUNK, partial)
+        partial = following
+    velocities(nodes - CHUNK, partial)
+
+
+def inner_call(last, *args):
+    nodes, ny, width = args[0].shape
+    shapes = [(nodes, ny, width), (2, nodes, ny, width)]
+    shapes += [(nodes * ny, width)] if last else [(nodes, ny, width)] * 2
+    return pl.pallas_call(
+        functools.partial(inner_kernel, last),
+        out_shape=[jax.ShapeDtypeStruct(shape, jnp.float32) for shape in shapes],
+        out_specs=[pl.BlockSpec(memory_space=pltpu.VMEM)] * len(shapes),
+        compiler_params=pltpu.CompilerParams(vmem_limit_bytes=8 * MIB),
+    )(*args)
+
+
 def step_kernel(last, *refs):
-    (velocity, stress, stress_y, rigidity, buoyancy, sigma_star, sigma_zero, friction) = refs[:8]
-    (received, near, far, depth_own, depth_near, depth_far, own) = refs[8:15]
-    refs = refs[15:]
-    if last:
-        results, held, sems = refs[:5], refs[5:10], refs[10]
-        velocity_new, stress_new, stress_y_new, state_new, bounds = held
-        traction = refs[11]
-        copies = []
-
-        def send(sources, targets):
-            for source, target in zip(sources, targets):
-                copies.append(pltpu.make_async_copy(source, target, sems.at[len(copies)]))
-                copies[-1].start()
-
-    else:
-        later, lead = refs[:2]
-        velocity_new, stress_new, stress_y_new, state_new, core, own_new, edges = refs[2:9]
-        edges_sent, traction, newest = refs[9:]
-    even, chip_even, _ = parities()
+    (moved, stress, faces, velocity, rigidity, buoyancy) = refs[:6]
+    (sigma_star, sigma_zero, friction) = refs[6:9]
+    (received, near, far, depth_own, depth_near, depth_far, own) = refs[9:16]
+    refs = refs[16:]
     nodes, ny, width = velocity.shape
     chunks = nodes // CHUNK
     fault = ny // 2 - 1
     scale = courant * 0.5
+    copies = []
+    if last:
+        results, (velocity_new, shear, tips, broken, state_new, bounds), sems = (
+            refs[:5],
+            refs[5:11],
+            refs[11],
+        )
+
+        def send(source, target):
+            copies.append(pltpu.make_async_copy(source, target, sems.at[len(copies)]))
+            copies[-1].start()
+
+        inner = pl.ds(1, nodes - 2)
+        send(stress.at[0, inner], results[1].at[0, inner])
+        base = fault * nodes
+        send(faces.at[pl.ds(0, base)], results[2].at[pl.ds(0, base)])
+        above = pl.ds(base + nodes, (ny - 2 - fault) * nodes)
+        send(faces.at[above], results[2].at[above])
+    else:
+        later, lead = refs[:2]
+        velocity_new, stress_new, faces_new, state_new, core, own_new, edges = refs[2:9]
+        edges_sent = refs[9]
+        shear = stress_new.at[1]
+    even, chip_even, _ = parities()
+
+    def level_of(ref, y):
+        return ref.reshape(nodes * ny, width)[pl.ds(y, nodes, stride=ny), :]
 
     near_parts, far_parts = unpacked(near, nodes), unpacked(far, nodes)
+    traction = []
     for surface in range(2):
         base = surface * 2 * nodes
         mate = lax.select(
             even, received[base : base + nodes], received[base + nodes : base + 2 * nodes]
         )
-        rows = slice(surface * nodes, (surface + 1) * nodes)
-        traction[surface] = (
+        traction.append(
             own[surface, nodes : 2 * nodes] + mate + (near_parts[surface] + far_parts[surface])
         )
 
@@ -340,108 +436,87 @@
     )
     stress_left = left[32:] + scale * left[16:32] * velocity[0]
     stress_right = right[32:] - scale * right[16:32] * velocity[nodes - 1]
-    sides = depth_sides(depth_own[...], depth_near[...], depth_far[...], chunks)
+    added_left = -scale * rigidity[0] * left[:16]
+    added_right = scale * rigidity[nodes - 1] * right[:16]
 
     shape = (CHUNK, ny, width)
-    sides = sides.reshape(shape)
+    sides = depth_sides(depth_own[...], depth_near[...], depth_far[...], chunks).reshape(shape)
     lane = lane_of(shape)
-    level = lax.broadcasted_iota(jnp.int32, shape, 1)
-
-    def beside(ref, at, before, after):
-        up = ref[at + 1 : min(at + CHUNK + 1, nodes)]
-        down = ref[max(at - 1, 0) : at + CHUNK - 1]
-        if at + CHUNK == nodes:
-            up = jnp.concatenate([up, after[None]], axis=0)
-        if at == 0:
-            down = jnp.concatenate([before[None], down], axis=0)
-        return up, down
-
-    def stresses(at):
+    edge = (lane == 0) | (lane == width - 1)
+    margin = (lane < 2) | (lane >= width - 2)
+
+    for at in range(0, nodes, CHUNK):
         cells = slice(at, at + CHUNK)
-        here, rigid = velocity[cells], rigidity[cells]
-        up, down = beside(velocity, at, left[:16], right[:16])
-        stress_x = stress[0, cells] + scale * rigid * (up - down)
-        stress_new[0, cells] = stress_x
-
         place = 8 * (at // CHUNK)
-        side = turned(sides, -(place + 1))
-        after = jnp.where(lane == width - 1, side, turned(here, -1))
-        before = jnp.where(lane == 0, side, turned(here, 1))
-        stress_z = stress[1, cells] + scale * rigid * (after - before)
-        stress_new[1, cells] = stress_z
-        side = turned(sides, -(place + 3))
-        after = jnp.where(lane == width - 1, side, turned(stress_z, -1))
-        before = jnp.where(lane == 0, side, turned(stress_z, 1))
-        spreading = 0.5 * (after - before)
-
-        if last:
-            faces = stress_y[cells][:, : ny - 1]
-        else:
-            faces = jnp.stack(
-                [stress_y[pl.ds(at + r, ny - 1, stride=nodes), :] for r in range(CHUNK)]
-            )
-        trial = faces + courant * (0.5 * (rigid[:, 1:] + rigid[:, :-1])) * (
-            here[:, 1:] - here[:, :-1]
-        )
-        slip_rate = here[:, fault + 1] - here[:, fault]
-        zero = sigma_zero[cells]
-        normal = zero + bimaterial * jnp.tanh(stress_x[:, fault + 1] - stress_x[:, fault])
-        state = normal + (sigma_star[cells] - normal) * jnp.exp(
-            -(jnp.abs(slip_rate) + slip_ref) * decay_rate
-        )
-        state_new[cells] = state
-        strength = friction[cells] * state
-        clipped = jnp.clip(trial[:, fault], -strength, strength)
-        bottom = traction[0, cells] + impedance * here[:, 0]
-        top = traction[1, cells] - impedance * here[:, ny - 1]
-        above = jnp.concatenate([trial, top[:, None]], axis=1)
-        above = jnp.where(level == fault, clipped[:, None], above)
-        if last:
-            bounds[0, cells] = bottom
-            bounds[1, cells] = top
-            for r in range(CHUNK):
-                stress_y_new[pl.ds(at + r, ny - 1, stride=nodes), :] = above[r, : ny - 1]
-        else:
-            stress_y_new[cells] = above
-        below = jnp.where(level == 0, bottom[:, None], pltpu.roll(above, 1, 1))
-        return spreading + above - below
-
-    def velocities(at, partial):
-        cells = slice(at, at + CHUNK)
-        up, down = beside(stress_new.at[0], at, stress_left, stress_right)
-        moved = velocity[cells] + courant * buoyancy[cells] * (0.5 * (up - down) + partial)
-        velocity_new[cells] = moved
+        extra = jnp.where(margin, turned(sides, -(place + 2)), 0.0)
+        velocity_new[cells] = moved[cells] + courant * buoyancy[cells] * extra
+        extra = jnp.where(edge, turned(sides, -(place + 5)), 0.0)
+        shear[cells] = stress[1, cells] + extra
+        if last and (at + CHUNK) % (nodes // 2) == 0:
+            half = pl.ds(at + CHUNK - nodes // 2, nodes // 2)
+            send(shear.at[half], results[1].at[1, half])
         if not last:
-            newest[0, cells] = moved[:, 0]
-            newest[1, cells] = moved[:, ny - 1]
-
-    partial = stresses(0)
-    for at in range(CHUNK, nodes, CHUNK):
-        following = stresses(at)
-        velocities(at - CHUNK, partial)
-        partial = following
-        if last and at == nodes // 2:
-            half = pl.ds(0, at)
-            send(
-                [stress_new.at[:, half], velocity_new.at[pl.ds(0, at - CHUNK)]],
-                [results[1].at[:, half], results[0].at[pl.ds(0, at - CHUNK)]],
-            )
+            stress_new[0, cells] = stress[0, cells]
+            faces_new[cells] = faces[cells]
+
+    first_row, last_row = stress[0, 0] + added_left, stress[0, nodes - 1] + added_right
     if last:
-        half = pl.ds(nodes // 2, nodes // 2)
-        send(
-            [stress_new.at[:, half], stress_y_new, state_new, bounds],
-            [results[1].at[:, half], results[2], results[3], results[4]],
-        )
-    velocities(nodes - CHUNK, partial)
+        tips[0], tips[1] = first_row, last_row
+        send(tips.at[0], results[1].at[0, 0])
+        send(tips.at[1], results[1].at[0, nodes - 1])
+    else:
+        stress_new[0, 0], stress_new[0, nodes - 1] = first_row, last_row
+
+    row = lax.broadcasted_iota(jnp.int32, (nodes, width), 0)
+    lower, upper = slice(fault, fault + 1), slice(fault + 1, fault + 2)
+    across = level_of(stress.at[0], fault + 1) - level_of(stress.at[0], fault)
+    across = across + jnp.where(row == 0, added_left[upper] - added_left[lower], 0.0)
+    across = across + jnp.where(row == nodes - 1, added_right[upper] - added_right[lower], 0.0)
+    slip_rate = level_of(velocity, fault + 1) - level_of(velocity, fault)
+    normal = sigma_zero[...] + bimaterial * jnp.tanh(across)
+    state = normal + (sigma_star[...] - normal) * jnp.exp(
+        -(jnp.abs(slip_rate) + slip_ref) * decay_rate
+    )
+    state_new[...] = state
+    strength = friction[...] * state
+    trial = faces[fault * nodes : (fault + 1) * nodes] if last else level_of(faces, fault)
+    clipped = jnp.clip(trial, -strength, strength)
+    bottom = traction[0] + impedance * level_of(velocity, 0)
+    top = traction[1] - impedance * level_of(velocity, ny - 1)
     if last:
-        half = pl.ds(nodes // 2 - CHUNK, nodes // 2 + CHUNK)
-        send([velocity_new.at[half]], [results[0].at[half]])
+        broken[...] = clipped
+        bounds[0], bounds[1] = bottom, top
+        send(broken, results[2].at[pl.ds(fault * nodes, nodes)])
+        send(state_new, results[3])
+        send(bounds, results[4])
+    else:
+        faces_new.reshape(nodes * ny, width)[pl.ds(fault, nodes, stride=ny), :] = clipped
+
+    flat = velocity_new.reshape(nodes * ny, width)
+    for y, change in (
+        (fault, clipped - trial),
+        (fault + 1, trial - clipped),
+        (0, -bottom),
+        (ny - 1, top),
+    ):
+        at = pl.ds(y, nodes, stride=ny)
+        flat[at, :] = flat[at, :] + courant * level_of(buoyancy, y) * change
+    for x, change in (
+        (0, -stress_left),
+        (1, -added_left),
+        (nodes - 2, added_right),
+        (nodes - 1, stress_right),
+    ):
+        velocity_new[x] = velocity_new[x] + (0.5 * courant) * buoyancy[x] * change
+
+    if last:
+        send(velocity_new, results[0])
         for copy in copies:
             copy.wait()
         return
 
     for surface in range(2):
-        fresh = newest[surface].astype(jnp.bfloat16)
+        fresh = level_of(velocity_new, surface * (ny - 1)).astype(jnp.bfloat16)
         total = later[surface] + jnp.dot(
             lead[surface], fresh, preferred_element_type=jnp.float32
         )
@@ -468,9 +543,10 @@
     shapes = [(nodes, ny, width), (2, nodes, ny, width)]
     if last:
         shapes += [(nodes * (ny - 1), width), (nodes, width), (2, nodes, width)]
-        scratch = [pltpu.VMEM(shape, f32) for shape in shapes]
-        scratch += [pltpu.SemaphoreType.DMA((7,)), pltpu.VMEM((2, nodes, width), f32)]
-        out_specs = [pl.BlockSpec(memory_space=pltpu.HBM)] * len(shapes)
+        held = [(nodes, ny, width)] * 2 + [(2, ny, width), (nodes, width), *shapes[3:]]
+        scratch = [pltpu.VMEM(shape, f32) for shape in held]
+        scratch += [pltpu.SemaphoreType.DMA((11,))]
+        space = pltpu.HBM
     else:
         shapes += [
             (nodes, ny, width),
@@ -479,15 +555,14 @@
             (2, 3 * nodes, width),
             (8, nodes * ny),
         ]
-        scratch = [pltpu.VMEM((2, nodes, width), f32)] * 2
-        out_specs = [pl.BlockSpec(memory_space=pltpu.VMEM)] * (len(shapes) + 1)
+        scratch, space = [], pltpu.VMEM
     out_shape = [jax.ShapeDtypeStruct(shape, f32) for shape in shapes]
     if not last:
         out_shape.append(jax.ShapeDtypeStruct((nodes, width), jnp.bfloat16))
     return pl.pallas_call(
         functools.partial(step_kernel, last),
         out_shape=out_shape,
-        out_specs=out_specs,
+        out_specs=[pl.BlockSpec(memory_space=space)] * len(out_shape),
         scratch_shapes=scratch,
         compiler_params=pltpu.CompilerParams(vmem_limit_bytes=16 * MIB),
     )(*args)
@@ -536,34 +611,32 @@
         friction,
     )
     face_rows, buoyancy, sigma_star, sigma_zero, friction = rest
-    moved = exchange(core, own, edges, sent)
+    *inner, stiffness = inner_call(False, velocity, stress_xz, face_rows, rigidity, buoyancy)
     velocity, stress_xz, stress_y, state, core, own, edges, sent = step_call(
         False,
+        *inner,
         velocity,
-        stress_xz,
-        face_rows,
         rigidity,
         buoyancy,
         sigma_star,
         sigma_zero,
         friction,
-        *moved,
+        *exchange(core, own, edges, sent),
         own,
         later,
         lead,
     )
-    moved = exchange(core, own, edges, sent)
+    inner = inner_call(True, velocity, stress_xz, stress_y, rigidity, buoyancy, stiffness)
     velocity, stress_xz, face_rows, state, bounds = step_call(
         True,
+        *inner,
         velocity,
-        stress_xz,
-        stress_y,
         rigidity,
         buoyancy,
         state,
         sigma_zero,
         friction,
-        *moved,
+        *exchange(core, own, edges, sent),
         own,
     )
     stress_y = jnp.transpose(face_rows.reshape(faces, nodes, width), (1, 0, 2))

time: 39.1 us -> 36.8 us (0.941)
  waiting for transfers between devices: 5.02 us -> 2.43 us
    ppermute x2, waiting for transfers between devices: 4.28 us -> 1.69 us  [exchange(): depth_far = lax.ppermute(depth_near, GZ, onward_pairs(GZ))]
    pallas_call x0 -> x2, Pallas kernels: none -> 2.58 us  [inner_call(): pl.pallas_call(functools.partial(inner_kernel, last), out_shape=[jax.Shap...]
    pallas_call x2, Pallas kernels: 4.49 us -> 2.73 us  [step_call(): pl.pallas_call(functools.partial(step_kernel, last), out_shape=out_shape,...]
    pallas_call x1, Pallas kernels: 6.07 us -> 5.55 us  [first_call(): pl.pallas_call(first_kernel, in_specs=[pl.BlockSpec(memory_space=pltpu.HB...]
  transfers between devices with their start and end apart: 10 -> 10, of which waited for: 4 -> 4; matrix products, arithmetic and copies ran while one was open for 0% -> 0% of each run, Pallas kernels for 1% -> 8%
where the time goes in v4:
time: 36.8 us; the launch traced here: 36.6 us
  starting transfers between devices  22.3 us (61%)
  Pallas kernels  11.1 us (30%)
  waiting for transfers between devices  2.43 us (7%)
  between operations  0.75 us (2%)
    ppermute x2, starting transfers between devices, exchange(): near = lax.ppermute(near, GX, swap_pairs(GX, 2, 0))  7.68 us
    ppermute x2, starting transfers between devices, exchange(): depth_far = lax.ppermute(depth_near, GZ, onward_pairs(GZ))  6.95 us
    pallas_call x1, Pallas kernels, first_call(): pl.pallas_call(first_kernel, in_specs=[pl.BlockSpec(memory_space=pltpu.HB...  5.55 us
    ppermute x2, starting transfers between devices, exchange(): lax.ppermute(relay_call(False, received, own), GX, swap_pairs(GX, 2, 2))  4.36 us
    ppermute x2, starting transfers between devices, exchange(): depth_near = lax.ppermute(edges_sent, GZ, swap_pairs(GZ, 1, 0))  3.11 us
    pallas_call x2, Pallas kernels, step_call(): pl.pallas_call(functools.partial(step_kernel, last), out_shape=out_shape,...  2.73 us
    pallas_call x2, Pallas kernels, inner_call(): pl.pallas_call(functools.partial(inner_kernel, last), out_shape=[jax.Shap...  2.58 us
    ppermute x2, waiting for transfers between devices, exchange(): depth_far = lax.ppermute(depth_near, GZ, onward_pairs(GZ))  1.69 us
  transfers between devices with their start and end apart: 10, of which 4 were waited for; matrix products, arithmetic and copies ran while one was open for 0% of the time, Pallas kernels for 8%

profile of v4, /device:TPU:76, one launch (start us, length us, event | category | flops | bytes accessed | tf_op | source)
XLA Modules:
  0.0 36.6 jit_solution(14650857531975124593)
XLA Ops:
  0.6 5.5 %shard_map.146 = (f32[352,128]{1,0:T(8,128)S(1)}, f32[2,192,128]{2,1,0:T(8,128)S(1)}, f32[2,320,128]{2,1,0:T(8,128)S(1)}, bf16[2,320,64]{2,1,0:T(8,128)(2,1)S(1)...) custom-call(f32[64,16,128]{2,1,0:T(8,128)} %refs_0_.1, ...), custom_call_target="tpu_custom_call" | custom-call | tf_op jit(solution)/shard_map/pallas_call | solution.py:219
  6.2 0.1 collective-permute-start
  6.3 2.0 %collective-permute-start.1 = (bf16[64,128]{1,0:T(8,128)(2,1)S(1)}, bf16[64,128]{1,0:T(8,128)(2,1)S(1)}, u32[]{:S(2)}, u32[]{:S(2)}) collective-permute-start(bf16[64,128]{1,0:T(8,128)(2,1)S(1)} %get-tuple-element.52), channel_id=1, source_target_pairs={{0,1},{1,0},{2,3},{3,2},{4,5},{5,4},{6,7},{7,6},{8,9},{9,8},{10,11... | collective-permute-start | bytes 49160 | tf_op jit(solution)/shard_map/ppermute | solution.py:573
  8.3 0.0 collective-permute-done.received.refs_9_
  8.3 0.1 shard_map.149
  8.4 2.4 %collective-permute-start.3 = (s16[224,128]{1,0:T(8,128)(2,1)S(1)}, s16[224,128]{1,0:T(8,128)(2,1)S(1)}, u32[]{:S(2)}, u32[]{:S(2)}) collective-permute-start(s16[224,128]{1,0:T(8,128)(2,1)S(1)} %shard_map.149), channel_id=1, source_target_pairs={{16,32},{24,40},{32,16},{40,24},{48,64},{56,72},{64,48},{72,56},{8... | collective-permute-start | bytes 172040 | tf_op jit(solution)/shard_map/ppermute | solution.py:574
  10.8 0.0 collective-permute-done.1.refs_0_.refs_13_
  10.8 0.1 shard_map.148
  10.9 4.5 %collective-permute-start.2 = (s16[192,128]{1,0:T(8,128)(2,1)S(1)}, s16[192,128]{1,0:T(8,128)(2,1)S(1)}, u32[]{:S(2)}, u32[]{:S(2)}) collective-permute-start(s16[192,128]{1,0:T(8,128)(2,1)S(1)} %shard_map.148), channel_id=1, source_target_pairs={{0,16},{8,24},{16,0},{24,8},{32,48},{40,56},{48,32},{56,40},{64,80... | collective-permute-start | bytes 147464 | tf_op jit(solution)/shard_map/ppermute | solution.py:576
  15.4 3.5 %collective-permute-start.4 = (bf16[64,128]{1,0:T(8,128)(2,1)S(1)}, bf16[64,128]{1,0:T(8,128)(2,1)S(1)}, u32[]{:S(2)}, u32[]{:S(2)}) collective-permute-start(bf16[64,128]{1,0:T(8,128)(2,1)S(1)} %collective-permute-done.1.refs_0_.refs_13_), channel_id=1, source_target_pairs={{0,2},{2,4},{3,1},{4,6},{5,3},{7,5},{8,10},{10,12},{11,9},{12,14},... | collective-permute-start | bytes 49160 | tf_op jit(solution)/shard_map/ppermute | solution.py:577
  18.9 1.2 %shard_map.147 = (f32[64,16,128]{2,1,0:T(8,128)S(1)}, f32[2,64,16,128]{3,2,1,0:T(8,128)S(1)}, f32[64,16,128]{2,1,0:T(8,128)S(1)}, f32[64,16,128]{2,1,0:T(8,128)S(1)}) custom-call(f32[64,16,128]{2,1,0:T(8,128)S(1)} %get-tuple-element.39.refs_0_.refs_3_, f32[2,64,16,128]{3,2,1,0:T(8,128)S(1)} %get-tuple-element.40.refs_1_, ...), custom_call_target="tpu_custom_call" | custom-call | tf_op jit(solution)/shard_map/pallas_call | solution.py:374
  20.1 1.0 %collective-permute-done.4.refs_14_ = bf16[64,128]{1,0:T(8,128)(2,1)S(1)} collective-permute-done((bf16[64,128]{1,0:T(8,128)(2,1)S(1)}, bf16[64,128]{1,0:T(8,128)(2,1)S(1)}, u32[]{:S(2)}, u32[]{:S(2)}) %collective-permute-start.4) | collective-permute-done | bytes 16416 | tf_op jit(solution)/shard_map/ppermute | solution.py:577
  21.1 0.0 collective-permute-done.2.refs_10_
  21.1 0.0 collective-permute-done.3.refs_11_
  21.1 1.1 %shard_map.150 = (f32[64,16,128]{2,1,0:T(8,128)S(1)}, f32[2,64,16,128]{3,2,1,0:T(8,128)S(1)}, f32[64,16,128]{2,1,0:T(8,128)S(1)}, f32[64,128]{1,0:T(8,128)S(1)},...) custom-call(f32[64,16,128]{2,1,0:T(8,128)S(1)} %get-tuple-element.44., ...), custom_call_target="tpu_custom_call" | custom-call | tf_op jit(solution)/shard_map/pallas_call | solution.py:562
  22.2 0.1 collective-permute-start.5
  22.3 1.1 %collective-permute-start.6 = (bf16[64,128]{1,0:T(8,128)(2,1)S(1)}, bf16[64,128]{1,0:T(8,128)(2,1)S(1)}, u32[]{:S(2)}, u32[]{:S(2)}) collective-permute-start(bf16[64,128]{1,0:T(8,128)(2,1)S(1)} %get-tuple-element.66), channel_id=1, source_target_pairs={{0,1},{1,0},{2,3},{3,2},{4,5},{5,4},{6,7},{7,6},{8,9},{9,8},{10,11... | collective-permute-start | bytes 49160 | tf_op jit(solution)/shard_map/ppermute | solution.py:573
  23.4 0.3 collective-permute-done.5.received.refs_9_
  23.7 0.1 shard_map.153
  23.8 1.9 %collective-permute-start.8 = (s16[224,128]{1,0:T(8,128)(2,1)S(1)}, s16[224,128]{1,0:T(8,128)(2,1)S(1)}, u32[]{:S(2)}, u32[]{:S(2)}) collective-permute-start(s16[224,128]{1,0:T(8,128)(2,1)S(1)} %shard_map.153), channel_id=1, source_target_pairs={{16,32},{24,40},{32,16},{40,24},{48,64},{56,72},{64,48},{72,56},{8... | collective-permute-start | bytes 172040 | tf_op jit(solution)/shard_map/ppermute | solution.py:574
  25.7 0.4 %collective-permute-done.6.refs_0_.refs_13_ = bf16[64,128]{1,0:T(8,128)(2,1)S(1)} collective-permute-done((bf16[64,128]{1,0:T(8,128)(2,1)S(1)}, bf16[64,128]{1,0:T(8,128)(2,1)S(1)}, u32[]{:S(2)}, u32[]{:S(2)}) %collective-permute-start.6) | collective-permute-done | bytes 16416 | tf_op jit(solution)/shard_map/ppermute | solution.py:573
  26.1 0.1 shard_map.152
  26.2 3.1 %collective-permute-start.7 = (s16[192,128]{1,0:T(8,128)(2,1)S(1)}, s16[192,128]{1,0:T(8,128)(2,1)S(1)}, u32[]{:S(2)}, u32[]{:S(2)}) collective-permute-start(s16[192,128]{1,0:T(8,128)(2,1)S(1)} %shard_map.152), channel_id=1, source_target_pairs={{0,16},{8,24},{16,0},{24,8},{32,48},{40,56},{48,32},{56,40},{64,80... | collective-permute-start | bytes 147464 | tf_op jit(solution)/shard_map/ppermute | solution.py:576
  29.3 3.5 %collective-permute-start.9 = (bf16[64,128]{1,0:T(8,128)(2,1)S(1)}, bf16[64,128]{1,0:T(8,128)(2,1)S(1)}, u32[]{:S(2)}, u32[]{:S(2)}) collective-permute-start(bf16[64,128]{1,0:T(8,128)(2,1)S(1)} %collective-permute-done.6.refs_0_.refs_13_), channel_id=1, source_target_pairs={{0,2},{2,4},{3,1},{4,6},{5,3},{7,5},{8,10},{10,12},{11,9},{12,14},... | collective-permute-start | bytes 49160 | tf_op jit(solution)/shard_map/ppermute | solution.py:577
  32.8 1.4 %shard_map.151 = (f32[64,16,128]{2,1,0:T(8,128)S(1)}, f32[2,64,16,128]{3,2,1,0:T(8,128)S(1)}, f32[1024,128]{1,0:T(8,128)S(1)}) custom-call(f32[64,16,128]{2,1,0:T(8,128)S(1)} %get-tuple-element.56.refs_0_.refs_3_, f32[2,64,16,128]{3,2,1,0:T(8,128)S(1)} %get-tuple-element.57.refs_1_, f32[64,16,128]{2,1,0:T(8,128)S(1)} %get-tuple-element.58.refs_2_, ...), custom_call_target="tpu_custom_call" | custom-call | tf_op jit(solution)/shard_map/pallas_call | solution.py:374
  34.2 0.7 %collective-permute-done.9.refs_14_ = bf16[64,128]{1,0:T(8,128)(2,1)S(1)} collective-permute-done((bf16[64,128]{1,0:T(8,128)(2,1)S(1)}, bf16[64,128]{1,0:T(8,128)(2,1)S(1)}, u32[]{:S(2)}, u32[]{:S(2)}) %collective-permute-start.9) | collective-permute-done | bytes 16416 | tf_op jit(solution)/shard_map/ppermute | solution.py:577
  34.9 0.0 collective-permute-done.7.refs_10_
  35.0 0.0 collective-permute-done.8.refs_11_
  35.0 1.6 %shard_map.154 = (f32[64,16,128]{2,1,0:T(8,128)}, f32[2,64,16,128]{3,2,1,0:T(8,128)}, f32[960,128]{1,0:T(8,128)}, f32[64,128]{1,0:T(8,128)}, f32[2,64,128]{2,1,0:T(8,128)}) custom-call(f32[64,16,128]{2,1,0:T(8,128)S(1)} %get-tuple-element.60.refs_0_, f32[2,64,16,128]{3,2,1,0:T(8,128)S(1)} %get-tuple-element.61.refs_1_, ...), custom_call_target="tpu_custom_call" | custom-call | tf_op jit(solution)/shard_map/pallas_call | solution.py:562
Async XLA Ops:
  6.2 2.1 %collective-permute-start = (f32[352,128]{1,0:T(8,128)S(1)}, f32[352,128]{1,0:T(8,128)S(1)}, u32[]{:S(2)}, u32[]{:S(2)}) collective-permute-start(f32[352,128]{1,0:T(8,128)S(1)} %get-tuple-element.50), channel_id=1, source_target_pairs={{0,8},{8,0},{16,24},{24,16},{32,40},{40,32},{48,56},{56,48},{64,72... | collective-permute-start | bytes 540680 | tf_op jit(solution)/shard_map/ppermute | solution.py:572
  6.3 4.5 %collective-permute-start.1 = (bf16[64,128]{1,0:T(8,128)(2,1)S(1)}, bf16[64,128]{1,0:T(8,128)(2,1)S(1)}, u32[]{:S(2)}, u32[]{:S(2)}) collective-permute-start(bf16[64,128]{1,0:T(8,128)(2,1)S(1)} %get-tuple-element.52), channel_id=1, source_target_pairs={{0,1},{1,0},{2,3},{3,2},{4,5},{5,4},{6,7},{7,6},{8,9},{9,8},{10,11... | collective-permute-start | bytes 49160 | tf_op jit(solution)/shard_map/ppermute | solution.py:573
  8.4 12.7 %collective-permute-start.3 = (s16[224,128]{1,0:T(8,128)(2,1)S(1)}, s16[224,128]{1,0:T(8,128)(2,1)S(1)}, u32[]{:S(2)}, u32[]{:S(2)}) collective-permute-start(s16[224,128]{1,0:T(8,128)(2,1)S(1)} %shard_map.149), channel_id=1, source_target_pairs={{16,32},{24,40},{32,16},{40,24},{48,64},{56,72},{64,48},{72,56},{8... | collective-permute-start | bytes 172040 | tf_op jit(solution)/shard_map/ppermute | solution.py:574
  10.9 10.2 %collective-permute-start.2 = (s16[192,128]{1,0:T(8,128)(2,1)S(1)}, s16[192,128]{1,0:T(8,128)(2,1)S(1)}, u32[]{:S(2)}, u32[]{:S(2)}) collective-permute-start(s16[192,128]{1,0:T(8,128)(2,1)S(1)} %shard_map.148), channel_id=1, source_target_pairs={{0,16},{8,24},{16,0},{24,8},{32,48},{40,56},{48,32},{56,40},{64,80... | collective-permute-start | bytes 147464 | tf_op jit(solution)/shard_map/ppermute | solution.py:576
  15.4 5.6 %collective-permute-start.4 = (bf16[64,128]{1,0:T(8,128)(2,1)S(1)}, bf16[64,128]{1,0:T(8,128)(2,1)S(1)}, u32[]{:S(2)}, u32[]{:S(2)}) collective-permute-start(bf16[64,128]{1,0:T(8,128)(2,1)S(1)} %collective-permute-done.1.refs_0_.refs_13_), channel_id=1, source_target_pairs={{0,2},{2,4},{3,1},{4,6},{5,3},{7,5},{8,10},{10,12},{11,9},{12,14},... | collective-permute-start | bytes 49160 | tf_op jit(solution)/shard_map/ppermute | solution.py:577
  22.2 1.5 %collective-permute-start.5 = (f32[352,128]{1,0:T(8,128)S(1)}, f32[352,128]{1,0:T(8,128)S(1)}, u32[]{:S(2)}, u32[]{:S(2)}) collective-permute-start(f32[352,128]{1,0:T(8,128)S(1)} %get-tuple-element.64), channel_id=1, source_target_pairs={{0,8},{8,0},{16,24},{24,16},{32,40},{40,32},{48,56},{56,48},{64,72... | collective-permute-start | bytes 540680 | tf_op jit(solution)/shard_map/ppermute | solution.py:572
  22.3 3.8 %collective-permute-start.6 = (bf16[64,128]{1,0:T(8,128)(2,1)S(1)}, bf16[64,128]{1,0:T(8,128)(2,1)S(1)}, u32[]{:S(2)}, u32[]{:S(2)}) collective-permute-start(bf16[64,128]{1,0:T(8,128)(2,1)S(1)} %get-tuple-element.66), channel_id=1, source_target_pairs={{0,1},{1,0},{2,3},{3,2},{4,5},{5,4},{6,7},{7,6},{8,9},{9,8},{10,11... | collective-permute-start | bytes 49160 | tf_op jit(solution)/shard_map/ppermute | solution.py:573
  23.8 11.2 %collective-permute-start.8 = (s16[224,128]{1,0:T(8,128)(2,1)S(1)}, s16[224,128]{1,0:T(8,128)(2,1)S(1)}, u32[]{:S(2)}, u32[]{:S(2)}) collective-permute-start(s16[224,128]{1,0:T(8,128)(2,1)S(1)} %shard_map.153), channel_id=1, source_target_pairs={{16,32},{24,40},{32,16},{40,24},{48,64},{56,72},{64,48},{72,56},{8... | collective-permute-start | bytes 172040 | tf_op jit(solution)/shard_map/ppermute | solution.py:574
  26.2 8.8 %collective-permute-start.7 = (s16[192,128]{1,0:T(8,128)(2,1)S(1)}, s16[192,128]{1,0:T(8,128)(2,1)S(1)}, u32[]{:S(2)}, u32[]{:S(2)}) collective-permute-start(s16[192,128]{1,0:T(8,128)(2,1)S(1)} %shard_map.152), channel_id=1, source_target_pairs={{0,16},{8,24},{16,0},{24,8},{32,48},{40,56},{48,32},{56,40},{64,80... | collective-permute-start | bytes 147464 | tf_op jit(solution)/shard_map/ppermute | solution.py:576
  29.3 5.6 %collective-permute-start.9 = (bf16[64,128]{1,0:T(8,128)(2,1)S(1)}, bf16[64,128]{1,0:T(8,128)(2,1)S(1)}, u32[]{:S(2)}, u32[]{:S(2)}) collective-permute-start(bf16[64,128]{1,0:T(8,128)(2,1)S(1)} %collective-permute-done.6.refs_0_.refs_13_), channel_id=1, source_target_pairs={{0,2},{2,4},{3,1},{4,6},{5,3},{7,5},{8,10},{10,12},{11,9},{12,14},... | collective-permute-start | bytes 49160 | tf_op jit(solution)/shard_map/ppermute | solution.py:577

commit v5 on v4

--- a/solution.py
+++ b/solution.py
@@ -16,6 +16,7 @@
 GX, GZ = "gx", "gz"
 CHUNK = 8
 CHUNK_COLUMNS = 1024
+SPLIT = 2
 SPARE = 32
 MIB = 2**20
 FIRST_LIMIT = 12 * MIB
@@ -134,33 +135,47 @@
             ((cone, limits), (velocity, speed), (rigidity, rigid), (stress, tension))
         )
     ]
-    fetches = [
-        (
-            pltpu.make_async_copy(history.at[s], past.at[s], part_sems.at[0, s]),
-            pltpu.make_async_copy(kernel.at[s], matrix.at[s], part_sems.at[1, s]),
-        )
-        for s in range(surfaces)
-    ]
+    piece = columns // SPLIT
+    fetches = []
+    for surface in range(surfaces):
+        for half in range(SPLIT):
+            place, span = len(fetches), pl.ds(half * piece, piece)
+            fetches.append(
+                (
+                    pltpu.make_async_copy(
+                        history.at[surface, span], past.at[surface, span], part_sems.at[0, place]
+                    ),
+                    pltpu.make_async_copy(
+                        kernel.at[surface, :, span],
+                        matrix.at[surface, :, span],
+                        part_sems.at[1, place],
+                    ),
+                )
+            )
     others = [
         pltpu.make_async_copy(source, target.at[pl.ds(0, source.shape[0])], rest_sems.at[place])
         for place, (source, target) in enumerate(zip(rest, rest_held))
     ]
-    for copy in (slab[0], *fetches[0]):
+    following = {0: (*fetches[3], *slab[1:]), 1: others}
+    for copy in (slab[0], *fetches[0], *fetches[1]):
         copy.start()
     slab[0].wait()
-    for copy in (*fetches[1], *slab[1:]):
+    for copy in fetches[2]:
         copy.start()
 
     block = lax.axis_index(GX)
     blocks = cone.shape[3]
     lag = lax.div(lane_of((1, CHUNK_COLUMNS)), nodes)
-    for surface in range(surfaces):
-        for copy in fetches[surface]:
-            copy.wait()
-        if surface == 0:
-            for copy in others:
+    order = [(surface, part) for surface in range(surfaces) for part in range(parts)]
+    for surface, part in order:
+        at = part * CHUNK_COLUMNS
+        if at % piece == 0:
+            place = surface * SPLIT + at // piece
+            for copy in fetches[place]:
+                copy.wait()
+            for copy in following.get(place, ()):
                 copy.start()
-        else:
+        if (surface, part) == order[-1]:
             for copy in slab[1:]:
                 copy.wait()
             cells = [slice(at, at + CHUNK) for at in range(0, nodes, CHUNK)]
@@ -176,34 +191,32 @@
                 speed[nodes - 2],
                 -1.0,
             )
-        total = None
-        for part in range(parts):
-            at = part * CHUNK_COLUMNS
-            masked = []
-            for index in range(offsets):
-                target = jnp.clip(block + (index - reach), 0, blocks - 1)
-                first = limits[surface, index, 0, target]
-                last = limits[surface, index, 1, target]
-                now = lag + at // nodes
-                keep = jnp.where((now >= first) & (now < last), 1.0, 0.0).astype(jnp.bfloat16)
-                masked.append(
-                    matrix[surface, index * nodes : (index + 1) * nodes, at : at + CHUNK_COLUMNS]
-                    * keep
-                )
-            kept = jnp.concatenate(masked, axis=0)
-            now = past[surface, at : at + CHUNK_COLUMNS]
-            if part:
-                before = past[surface, at - nodes : at + CHUNK_COLUMNS - nodes]
-            else:
-                before = jnp.concatenate(
-                    [jnp.zeros((nodes, width), now.dtype), now[: CHUNK_COLUMNS - nodes]], axis=0
-                )
-                lead[surface] = kept[:, :nodes]
-            both = jnp.concatenate([now, before], axis=1)
-            product = jnp.dot(kept, both, preferred_element_type=jnp.float32)
-            total = total + product if part else product
-        later[surface] = total[:, width:]
-        deal(total[:, :width], core, own, surface)
+        masked = []
+        for index in range(offsets):
+            target = jnp.clip(block + (index - reach), 0, blocks - 1)
+            first = limits[surface, index, 0, target]
+            last = limits[surface, index, 1, target]
+            now = lag + at // nodes
+            keep = jnp.where((now >= first) & (now < last), 1.0, 0.0).astype(jnp.bfloat16)
+            masked.append(
+                matrix[surface, index * nodes : (index + 1) * nodes, at : at + CHUNK_COLUMNS]
+                * keep
+            )
+        kept = jnp.concatenate(masked, axis=0)
+        now = past[surface, at : at + CHUNK_COLUMNS]
+        if part:
+            before = past[surface, at - nodes : at + CHUNK_COLUMNS - nodes]
+        else:
+            before = jnp.concatenate(
+                [jnp.zeros((nodes, width), now.dtype), now[: CHUNK_COLUMNS - nodes]], axis=0
+            )
+            lead[surface] = kept[:, :nodes]
+        both = jnp.concatenate([now, before], axis=1)
+        product = jnp.dot(kept, both, preferred_element_type=jnp.float32)
+        total = total + product if part else product
+        if part == parts - 1:
+            later[surface] = total[:, width:]
+            deal(total[:, :width], core, own, surface)
     for copy in others:
         copy.wait()
 
@@ -238,7 +251,7 @@
             pltpu.VMEM(history.shape, history.dtype),
             pltpu.VMEM(kernel.shape, kernel.dtype),
             pltpu.SemaphoreType.DMA((4,)),
-            pltpu.SemaphoreType.DMA((2, surfaces)),
+            pltpu.SemaphoreType.DMA((2, surfaces * SPLIT)),
             pltpu.SemaphoreType.DMA((len(rest),)),
         ],
         compiler_params=pltpu.CompilerParams(vmem_limit_bytes=FIRST_LIMIT),

time: 36.8 us -> 36.1 us (0.981)
  Pallas kernels: 11.1 us -> 10.4 us
    pallas_call x1, Pallas kernels: 5.55 us -> 4.82 us  [first_call(): pl.pallas_call(first_kernel, in_specs=[pl.BlockSpec(memory_space=pltpu.HB...]
where the time goes in v5:
time: 36.1 us; the launch traced here: 35.8 us
  starting transfers between devices  22.3 us (62%)
  Pallas kernels  10.4 us (29%)
  waiting for transfers between devices  2.43 us (7%)
  between operations  0.75 us (2%)
    ppermute x2, starting transfers between devices, exchange(): near = lax.ppermute(near, GX, swap_pairs(GX, 2, 0))  7.68 us
    ppermute x2, starting transfers between devices, exchange(): depth_far = lax.ppermute(depth_near, GZ, onward_pairs(GZ))  6.94 us
    pallas_call x1, Pallas kernels, first_call(): pl.pallas_call(first_kernel, in_specs=[pl.BlockSpec(memory_space=pltpu.HB...  4.82 us
    ppermute x2, starting transfers between devices, exchange(): lax.ppermute(relay_call(False, received, own), GX, swap_pairs(GX, 2, 2))  4.36 us
    ppermute x2, starting transfers between devices, exchange(): depth_near = lax.ppermute(edges_sent, GZ, swap_pairs(GZ, 1, 0))  3.11 us
    pallas_call x2, Pallas kernels, step_call(): pl.pallas_call(functools.partial(step_kernel, last), out_shape=out_shape,...  2.73 us
    pallas_call x2, Pallas kernels, inner_call(): pl.pallas_call(functools.partial(inner_kernel, last), out_shape=[jax.Shap...  2.58 us
    ppermute x2, waiting for transfers between devices, exchange(): depth_far = lax.ppermute(depth_near, GZ, onward_pairs(GZ))  1.69 us
  transfers between devices with their start and end apart: 10, of which 4 were waited for; matrix products, arithmetic and copies ran while one was open for 0% of the time, Pallas kernels for 8%

profile of v5, /device:TPU:76, one launch (start us, length us, event | category | flops | bytes accessed | tf_op | source)
XLA Modules:
  0.0 35.8 jit_solution(14207392332489117465)
XLA Ops:
  0.6 4.8 %shard_map.146 = (f32[352,128]{1,0:T(8,128)S(1)}, f32[2,192,128]{2,1,0:T(8,128)S(1)}, f32[2,320,128]{2,1,0:T(8,128)S(1)}, bf16[2,320,64]{2,1,0:T(8,128)(2,1)S(1)...) custom-call(f32[64,16,128]{2,1,0:T(8,128)} %refs_0_.1, ...), custom_call_target="tpu_custom_call" | custom-call | tf_op jit(solution)/shard_map/pallas_call | solution.py:232
  5.5 0.1 collective-permute-start
  5.6 2.0 %collective-permute-start.1 = (bf16[64,128]{1,0:T(8,128)(2,1)S(1)}, bf16[64,128]{1,0:T(8,128)(2,1)S(1)}, u32[]{:S(2)}, u32[]{:S(2)}) collective-permute-start(bf16[64,128]{1,0:T(8,128)(2,1)S(1)} %get-tuple-element.52), channel_id=1, source_target_pairs={{0,1},{1,0},{2,3},{3,2},{4,5},{5,4},{6,7},{7,6},{8,9},{9,8},{10,11... | collective-permute-start | bytes 49160 | tf_op jit(solution)/shard_map/ppermute | solution.py:586
  7.6 0.0 collective-permute-done.received.refs_9_
  7.6 0.1 shard_map.149
  7.6 2.4 %collective-permute-start.3 = (s16[224,128]{1,0:T(8,128)(2,1)S(1)}, s16[224,128]{1,0:T(8,128)(2,1)S(1)}, u32[]{:S(2)}, u32[]{:S(2)}) collective-permute-start(s16[224,128]{1,0:T(8,128)(2,1)S(1)} %shard_map.149), channel_id=1, source_target_pairs={{16,32},{24,40},{32,16},{40,24},{48,64},{56,72},{64,48},{72,56},{8... | collective-permute-start | bytes 172040 | tf_op jit(solution)/shard_map/ppermute | solution.py:587
  10.1 0.0 collective-permute-done.1.refs_0_.refs_13_
  10.1 0.1 shard_map.148
  10.2 4.5 %collective-permute-start.2 = (s16[192,128]{1,0:T(8,128)(2,1)S(1)}, s16[192,128]{1,0:T(8,128)(2,1)S(1)}, u32[]{:S(2)}, u32[]{:S(2)}) collective-permute-start(s16[192,128]{1,0:T(8,128)(2,1)S(1)} %shard_map.148), channel_id=1, source_target_pairs={{0,16},{8,24},{16,0},{24,8},{32,48},{40,56},{48,32},{56,40},{64,80... | collective-permute-start | bytes 147464 | tf_op jit(solution)/shard_map/ppermute | solution.py:589
  14.7 3.5 %collective-permute-start.4 = (bf16[64,128]{1,0:T(8,128)(2,1)S(1)}, bf16[64,128]{1,0:T(8,128)(2,1)S(1)}, u32[]{:S(2)}, u32[]{:S(2)}) collective-permute-start(bf16[64,128]{1,0:T(8,128)(2,1)S(1)} %collective-permute-done.1.refs_0_.refs_13_), channel_id=1, source_target_pairs={{0,2},{2,4},{3,1},{4,6},{5,3},{7,5},{8,10},{10,12},{11,9},{12,14},... | collective-permute-start | bytes 49160 | tf_op jit(solution)/shard_map/ppermute | solution.py:590
  18.2 1.2 %shard_map.147 = (f32[64,16,128]{2,1,0:T(8,128)S(1)}, f32[2,64,16,128]{3,2,1,0:T(8,128)S(1)}, f32[64,16,128]{2,1,0:T(8,128)S(1)}, f32[64,16,128]{2,1,0:T(8,128)S(1)}) custom-call(f32[64,16,128]{2,1,0:T(8,128)S(1)} %get-tuple-element.39.refs_0_.refs_3_, f32[2,64,16,128]{3,2,1,0:T(8,128)S(1)} %get-tuple-element.40.refs_1_, ...), custom_call_target="tpu_custom_call" | custom-call | tf_op jit(solution)/shard_map/pallas_call | solution.py:387
  19.4 1.0 %collective-permute-done.4.refs_14_ = bf16[64,128]{1,0:T(8,128)(2,1)S(1)} collective-permute-done((bf16[64,128]{1,0:T(8,128)(2,1)S(1)}, bf16[64,128]{1,0:T(8,128)(2,1)S(1)}, u32[]{:S(2)}, u32[]{:S(2)}) %collective-permute-start.4) | collective-permute-done | bytes 16416 | tf_op jit(solution)/shard_map/ppermute | solution.py:590
  20.3 0.0 collective-permute-done.2.refs_10_
  20.3 0.0 collective-permute-done.3.refs_11_
  20.3 1.1 %shard_map.150 = (f32[64,16,128]{2,1,0:T(8,128)S(1)}, f32[2,64,16,128]{3,2,1,0:T(8,128)S(1)}, f32[64,16,128]{2,1,0:T(8,128)S(1)}, f32[64,128]{1,0:T(8,128)S(1)},...) custom-call(f32[64,16,128]{2,1,0:T(8,128)S(1)} %get-tuple-element.44., ...), custom_call_target="tpu_custom_call" | custom-call | tf_op jit(solution)/shard_map/pallas_call | solution.py:575
  21.5 0.1 collective-permute-start.5
  21.6 1.1 %collective-permute-start.6 = (bf16[64,128]{1,0:T(8,128)(2,1)S(1)}, bf16[64,128]{1,0:T(8,128)(2,1)S(1)}, u32[]{:S(2)}, u32[]{:S(2)}) collective-permute-start(bf16[64,128]{1,0:T(8,128)(2,1)S(1)} %get-tuple-element.66), channel_id=1, source_target_pairs={{0,1},{1,0},{2,3},{3,2},{4,5},{5,4},{6,7},{7,6},{8,9},{9,8},{10,11... | collective-permute-start | bytes 49160 | tf_op jit(solution)/shard_map/ppermute | solution.py:586
  22.7 0.3 collective-permute-done.5.received.refs_9_
  23.0 0.1 shard_map.153
  23.0 1.9 %collective-permute-start.8 = (s16[224,128]{1,0:T(8,128)(2,1)S(1)}, s16[224,128]{1,0:T(8,128)(2,1)S(1)}, u32[]{:S(2)}, u32[]{:S(2)}) collective-permute-start(s16[224,128]{1,0:T(8,128)(2,1)S(1)} %shard_map.153), channel_id=1, source_target_pairs={{16,32},{24,40},{32,16},{40,24},{48,64},{56,72},{64,48},{72,56},{8... | collective-permute-start | bytes 172040 | tf_op jit(solution)/shard_map/ppermute | solution.py:587
  25.0 0.4 %collective-permute-done.6.refs_0_.refs_13_ = bf16[64,128]{1,0:T(8,128)(2,1)S(1)} collective-permute-done((bf16[64,128]{1,0:T(8,128)(2,1)S(1)}, bf16[64,128]{1,0:T(8,128)(2,1)S(1)}, u32[]{:S(2)}, u32[]{:S(2)}) %collective-permute-start.6) | collective-permute-done | bytes 16416 | tf_op jit(solution)/shard_map/ppermute | solution.py:586
  25.4 0.1 shard_map.152
  25.5 3.1 %collective-permute-start.7 = (s16[192,128]{1,0:T(8,128)(2,1)S(1)}, s16[192,128]{1,0:T(8,128)(2,1)S(1)}, u32[]{:S(2)}, u32[]{:S(2)}) collective-permute-start(s16[192,128]{1,0:T(8,128)(2,1)S(1)} %shard_map.152), channel_id=1, source_target_pairs={{0,16},{8,24},{16,0},{24,8},{32,48},{40,56},{48,32},{56,40},{64,80... | collective-permute-start | bytes 147464 | tf_op jit(solution)/shard_map/ppermute | solution.py:589
  28.6 3.5 %collective-permute-start.9 = (bf16[64,128]{1,0:T(8,128)(2,1)S(1)}, bf16[64,128]{1,0:T(8,128)(2,1)S(1)}, u32[]{:S(2)}, u32[]{:S(2)}) collective-permute-start(bf16[64,128]{1,0:T(8,128)(2,1)S(1)} %collective-permute-done.6.refs_0_.refs_13_), channel_id=1, source_target_pairs={{0,2},{2,4},{3,1},{4,6},{5,3},{7,5},{8,10},{10,12},{11,9},{12,14},... | collective-permute-start | bytes 49160 | tf_op jit(solution)/shard_map/ppermute | solution.py:590
  32.1 1.4 %shard_map.151 = (f32[64,16,128]{2,1,0:T(8,128)S(1)}, f32[2,64,16,128]{3,2,1,0:T(8,128)S(1)}, f32[1024,128]{1,0:T(8,128)S(1)}) custom-call(f32[64,16,128]{2,1,0:T(8,128)S(1)} %get-tuple-element.56.refs_0_.refs_3_, f32[2,64,16,128]{3,2,1,0:T(8,128)S(1)} %get-tuple-element.57.refs_1_, f32[64,16,128]{2,1,0:T(8,128)S(1)} %get-tuple-element.58.refs_2_, ...), custom_call_target="tpu_custom_call" | custom-call | tf_op jit(solution)/shard_map/pallas_call | solution.py:387
  33.5 0.7 %collective-permute-done.9.refs_14_ = bf16[64,128]{1,0:T(8,128)(2,1)S(1)} collective-permute-done((bf16[64,128]{1,0:T(8,128)(2,1)S(1)}, bf16[64,128]{1,0:T(8,128)(2,1)S(1)}, u32[]{:S(2)}, u32[]{:S(2)}) %collective-permute-start.9) | collective-permute-done | bytes 16416 | tf_op jit(solution)/shard_map/ppermute | solution.py:590
  34.2 0.0 collective-permute-done.7.refs_10_
  34.2 0.0 collective-permute-done.8.refs_11_
  34.2 1.6 %shard_map.154 = (f32[64,16,128]{2,1,0:T(8,128)}, f32[2,64,16,128]{3,2,1,0:T(8,128)}, f32[960,128]{1,0:T(8,128)}, f32[64,128]{1,0:T(8,128)}, f32[2,64,128]{2,1,0:T(8,128)}) custom-call(f32[64,16,128]{2,1,0:T(8,128)S(1)} %get-tuple-element.60.refs_0_, f32[2,64,16,128]{3,2,1,0:T(8,128)S(1)} %get-tuple-element.61.refs_1_, ...), custom_call_target="tpu_custom_call" | custom-call | tf_op jit(solution)/shard_map/pallas_call | solution.py:575
Async XLA Ops:
  5.5 2.1 %collective-permute-start = (f32[352,128]{1,0:T(8,128)S(1)}, f32[352,128]{1,0:T(8,128)S(1)}, u32[]{:S(2)}, u32[]{:S(2)}) collective-permute-start(f32[352,128]{1,0:T(8,128)S(1)} %get-tuple-element.50), channel_id=1, source_target_pairs={{0,8},{8,0},{16,24},{24,16},{32,40},{40,32},{48,56},{56,48},{64,72... | collective-permute-start | bytes 540680 | tf_op jit(solution)/shard_map/ppermute | solution.py:585
  5.6 4.5 %collective-permute-start.1 = (bf16[64,128]{1,0:T(8,128)(2,1)S(1)}, bf16[64,128]{1,0:T(8,128)(2,1)S(1)}, u32[]{:S(2)}, u32[]{:S(2)}) collective-permute-start(bf16[64,128]{1,0:T(8,128)(2,1)S(1)} %get-tuple-element.52), channel_id=1, source_target_pairs={{0,1},{1,0},{2,3},{3,2},{4,5},{5,4},{6,7},{7,6},{8,9},{9,8},{10,11... | collective-permute-start | bytes 49160 | tf_op jit(solution)/shard_map/ppermute | solution.py:586
  7.6 12.7 %collective-permute-start.3 = (s16[224,128]{1,0:T(8,128)(2,1)S(1)}, s16[224,128]{1,0:T(8,128)(2,1)S(1)}, u32[]{:S(2)}, u32[]{:S(2)}) collective-permute-start(s16[224,128]{1,0:T(8,128)(2,1)S(1)} %shard_map.149), channel_id=1, source_target_pairs={{16,32},{24,40},{32,16},{40,24},{48,64},{56,72},{64,48},{72,56},{8... | collective-permute-start | bytes 172040 | tf_op jit(solution)/shard_map/ppermute | solution.py:587
  10.2 10.2 %collective-permute-start.2 = (s16[192,128]{1,0:T(8,128)(2,1)S(1)}, s16[192,128]{1,0:T(8,128)(2,1)S(1)}, u32[]{:S(2)}, u32[]{:S(2)}) collective-permute-start(s16[192,128]{1,0:T(8,128)(2,1)S(1)} %shard_map.148), channel_id=1, source_target_pairs={{0,16},{8,24},{16,0},{24,8},{32,48},{40,56},{48,32},{56,40},{64,80... | collective-permute-start | bytes 147464 | tf_op jit(solution)/shard_map/ppermute | solution.py:589
  14.7 5.6 %collective-permute-start.4 = (bf16[64,128]{1,0:T(8,128)(2,1)S(1)}, bf16[64,128]{1,0:T(8,128)(2,1)S(1)}, u32[]{:S(2)}, u32[]{:S(2)}) collective-permute-start(bf16[64,128]{1,0:T(8,128)(2,1)S(1)} %collective-permute-done.1.refs_0_.refs_13_), channel_id=1, source_target_pairs={{0,2},{2,4},{3,1},{4,6},{5,3},{7,5},{8,10},{10,12},{11,9},{12,14},... | collective-permute-start | bytes 49160 | tf_op jit(solution)/shard_map/ppermute | solution.py:590
  21.5 1.5 %collective-permute-start.5 = (f32[352,128]{1,0:T(8,128)S(1)}, f32[352,128]{1,0:T(8,128)S(1)}, u32[]{:S(2)}, u32[]{:S(2)}) collective-permute-start(f32[352,128]{1,0:T(8,128)S(1)} %get-tuple-element.64), channel_id=1, source_target_pairs={{0,8},{8,0},{16,24},{24,16},{32,40},{40,32},{48,56},{56,48},{64,72... | collective-permute-start | bytes 540680 | tf_op jit(solution)/shard_map/ppermute | solution.py:585
  21.6 3.8 %collective-permute-start.6 = (bf16[64,128]{1,0:T(8,128)(2,1)S(1)}, bf16[64,128]{1,0:T(8,128)(2,1)S(1)}, u32[]{:S(2)}, u32[]{:S(2)}) collective-permute-start(bf16[64,128]{1,0:T(8,128)(2,1)S(1)} %get-tuple-element.66), channel_id=1, source_target_pairs={{0,1},{1,0},{2,3},{3,2},{4,5},{5,4},{6,7},{7,6},{8,9},{9,8},{10,11... | collective-permute-start | bytes 49160 | tf_op jit(solution)/shard_map/ppermute | solution.py:586
  23.0 11.2 %collective-permute-start.8 = (s16[224,128]{1,0:T(8,128)(2,1)S(1)}, s16[224,128]{1,0:T(8,128)(2,1)S(1)}, u32[]{:S(2)}, u32[]{:S(2)}) collective-permute-start(s16[224,128]{1,0:T(8,128)(2,1)S(1)} %shard_map.153), channel_id=1, source_target_pairs={{16,32},{24,40},{32,16},{40,24},{48,64},{56,72},{64,48},{72,56},{8... | collective-permute-start | bytes 172040 | tf_op jit(solution)/shard_map/ppermute | solution.py:587
  25.5 8.8 %collective-permute-start.7 = (s16[192,128]{1,0:T(8,128)(2,1)S(1)}, s16[192,128]{1,0:T(8,128)(2,1)S(1)}, u32[]{:S(2)}, u32[]{:S(2)}) collective-permute-start(s16[192,128]{1,0:T(8,128)(2,1)S(1)} %shard_map.152), channel_id=1, source_target_pairs={{0,16},{8,24},{16,0},{24,8},{32,48},{40,56},{48,32},{56,40},{64,80... | collective-permute-start | bytes 147464 | tf_op jit(solution)/shard_map/ppermute | solution.py:589
  28.6 5.6 %collective-permute-start.9 = (bf16[64,128]{1,0:T(8,128)(2,1)S(1)}, bf16[64,128]{1,0:T(8,128)(2,1)S(1)}, u32[]{:S(2)}, u32[]{:S(2)}) collective-permute-start(bf16[64,128]{1,0:T(8,128)(2,1)S(1)} %collective-permute-done.6.refs_0_.refs_13_), channel_id=1, source_target_pairs={{0,2},{2,4},{3,1},{4,6},{5,3},{7,5},{8,10},{10,12},{11,9},{12,14},... | collective-permute-start | bytes 49160 | tf_op jit(solution)/shard_map/ppermute | solution.py:590

commit v6 on v5

--- a/solution.py
+++ b/solution.py
@@ -17,7 +17,7 @@
 CHUNK = 8
 CHUNK_COLUMNS = 1024
 SPLIT = 2
-SPARE = 32
+SPARE = 16
 MIB = 2**20
 FIRST_LIMIT = 12 * MIB
 

time: 36.1 us -> 36 us (level)
  no operation moved by 1% of the time
where the time goes in v6:
time: 36 us; the launch traced here: 35.8 us
  starting transfers between devices  22.2 us (62%)
  Pallas kernels  10.4 us (29%)
  waiting for transfers between devices  2.43 us (7%)
  between operations  0.75 us (2%)
    ppermute x2, starting transfers between devices, exchange(): near = lax.ppermute(near, GX, swap_pairs(GX, 2, 0))  7.55 us
    ppermute x2, starting transfers between devices, exchange(): depth_far = lax.ppermute(depth_near, GZ, onward_pairs(GZ))  6.94 us
    pallas_call x1, Pallas kernels, first_call(): pl.pallas_call(first_kernel, in_specs=[pl.BlockSpec(memory_space=pltpu.HB...  4.82 us
    ppermute x2, starting transfers between devices, exchange(): lax.ppermute(relay_call(False, received, own), GX, swap_pairs(GX, 2, 2))  4.36 us
    ppermute x2, starting transfers between devices, exchange(): depth_near = lax.ppermute(edges_sent, GZ, swap_pairs(GZ, 1, 0))  3.11 us
    pallas_call x2, Pallas kernels, step_call(): pl.pallas_call(functools.partial(step_kernel, last), out_shape=out_shape,...  2.8 us
    pallas_call x2, Pallas kernels, inner_call(): pl.pallas_call(functools.partial(inner_kernel, last), out_shape=[jax.Shap...  2.58 us
    ppermute x2, waiting for transfers between devices, exchange(): depth_far = lax.ppermute(depth_near, GZ, onward_pairs(GZ))  1.69 us
  transfers between devices with their start and end apart: 10, of which 4 were waited for; matrix products, arithmetic and copies ran while one was open for 0% of the time, Pallas kernels for 8%

profile of v6, /device:TPU:76, one launch (start us, length us, event | category | flops | bytes accessed | tf_op | source)
XLA Modules:
  0.0 35.8 jit_solution(13025053404185392912)
XLA Ops:
  0.6 4.8 %shard_map.146 = (f32[352,128]{1,0:T(8,128)S(1)}, f32[2,192,128]{2,1,0:T(8,128)S(1)}, f32[2,320,128]{2,1,0:T(8,128)S(1)}, bf16[2,320,64]{2,1,0:T(8,128)(2,1)S(1)...) custom-call(f32[64,16,128]{2,1,0:T(8,128)} %refs_0_.1, ...), custom_call_target="tpu_custom_call" | custom-call | tf_op jit(solution)/shard_map/pallas_call | solution.py:232
  5.5 0.1 collective-permute-start
  5.6 2.0 %collective-permute-start.1 = (bf16[64,128]{1,0:T(8,128)(2,1)S(1)}, bf16[64,128]{1,0:T(8,128)(2,1)S(1)}, u32[]{:S(2)}, u32[]{:S(2)}) collective-permute-start(bf16[64,128]{1,0:T(8,128)(2,1)S(1)} %get-tuple-element.52), channel_id=1, source_target_pairs={{0,1},{1,0},{2,3},{3,2},{4,5},{5,4},{6,7},{7,6},{8,9},{9,8},{10,11... | collective-permute-start | bytes 49160 | tf_op jit(solution)/shard_map/ppermute | solution.py:586
  7.6 0.0 collective-permute-done.received.refs_9_
  7.6 0.1 shard_map.149
  7.6 2.4 %collective-permute-start.3 = (s16[208,128]{1,0:T(8,128)(2,1)S(1)}, s16[208,128]{1,0:T(8,128)(2,1)S(1)}, u32[]{:S(2)}, u32[]{:S(2)}) collective-permute-start(s16[208,128]{1,0:T(8,128)(2,1)S(1)} %shard_map.149), channel_id=1, source_target_pairs={{16,32},{24,40},{32,16},{40,24},{48,64},{56,72},{64,48},{72,56},{8... | collective-permute-start | bytes 159752 | tf_op jit(solution)/shard_map/ppermute | solution.py:587
  10.1 0.0 collective-permute-done.1.refs_0_.refs_13_
  10.1 0.1 shard_map.148
  10.2 4.5 %collective-permute-start.2 = (s16[192,128]{1,0:T(8,128)(2,1)S(1)}, s16[192,128]{1,0:T(8,128)(2,1)S(1)}, u32[]{:S(2)}, u32[]{:S(2)}) collective-permute-start(s16[192,128]{1,0:T(8,128)(2,1)S(1)} %shard_map.148), channel_id=1, source_target_pairs={{0,16},{8,24},{16,0},{24,8},{32,48},{40,56},{48,32},{56,40},{64,80... | collective-permute-start | bytes 147464 | tf_op jit(solution)/shard_map/ppermute | solution.py:589
  14.7 3.5 %collective-permute-start.4 = (bf16[64,128]{1,0:T(8,128)(2,1)S(1)}, bf16[64,128]{1,0:T(8,128)(2,1)S(1)}, u32[]{:S(2)}, u32[]{:S(2)}) collective-permute-start(bf16[64,128]{1,0:T(8,128)(2,1)S(1)} %collective-permute-done.1.refs_0_.refs_13_), channel_id=1, source_target_pairs={{0,2},{2,4},{3,1},{4,6},{5,3},{7,5},{8,10},{10,12},{11,9},{12,14},... | collective-permute-start | bytes 49160 | tf_op jit(solution)/shard_map/ppermute | solution.py:590
  18.2 1.2 %shard_map.147 = (f32[64,16,128]{2,1,0:T(8,128)S(1)}, f32[2,64,16,128]{3,2,1,0:T(8,128)S(1)}, f32[64,16,128]{2,1,0:T(8,128)S(1)}, f32[64,16,128]{2,1,0:T(8,128)S(1)}) custom-call(f32[64,16,128]{2,1,0:T(8,128)S(1)} %get-tuple-element.39.refs_0_.refs_3_, f32[2,64,16,128]{3,2,1,0:T(8,128)S(1)} %get-tuple-element.40.refs_1_, ...), custom_call_target="tpu_custom_call" | custom-call | tf_op jit(solution)/shard_map/pallas_call | solution.py:387
  19.4 1.0 %collective-permute-done.4.refs_14_ = bf16[64,128]{1,0:T(8,128)(2,1)S(1)} collective-permute-done((bf16[64,128]{1,0:T(8,128)(2,1)S(1)}, bf16[64,128]{1,0:T(8,128)(2,1)S(1)}, u32[]{:S(2)}, u32[]{:S(2)}) %collective-permute-start.4) | collective-permute-done | bytes 16416 | tf_op jit(solution)/shard_map/ppermute | solution.py:590
  20.3 0.0 collective-permute-done.2.refs_10_
  20.3 0.0 collective-permute-done.3.refs_11_
  20.3 1.2 %shard_map.150 = (f32[64,16,128]{2,1,0:T(8,128)S(1)}, f32[2,64,16,128]{3,2,1,0:T(8,128)S(1)}, f32[64,16,128]{2,1,0:T(8,128)S(1)}, f32[64,128]{1,0:T(8,128)S(1)},...) custom-call(f32[64,16,128]{2,1,0:T(8,128)S(1)} %get-tuple-element.44., ...), custom_call_target="tpu_custom_call" | custom-call | tf_op jit(solution)/shard_map/pallas_call | solution.py:575
  21.5 0.1 collective-permute-start.5
  21.6 1.1 %collective-permute-start.6 = (bf16[64,128]{1,0:T(8,128)(2,1)S(1)}, bf16[64,128]{1,0:T(8,128)(2,1)S(1)}, u32[]{:S(2)}, u32[]{:S(2)}) collective-permute-start(bf16[64,128]{1,0:T(8,128)(2,1)S(1)} %get-tuple-element.66), channel_id=1, source_target_pairs={{0,1},{1,0},{2,3},{3,2},{4,5},{5,4},{6,7},{7,6},{8,9},{9,8},{10,11... | collective-permute-start | bytes 49160 | tf_op jit(solution)/shard_map/ppermute | solution.py:586
  22.7 0.3 collective-permute-done.5.received.refs_9_
  23.0 0.1 shard_map.153
  23.1 1.9 %collective-permute-start.8 = (s16[208,128]{1,0:T(8,128)(2,1)S(1)}, s16[208,128]{1,0:T(8,128)(2,1)S(1)}, u32[]{:S(2)}, u32[]{:S(2)}) collective-permute-start(s16[208,128]{1,0:T(8,128)(2,1)S(1)} %shard_map.153), channel_id=1, source_target_pairs={{16,32},{24,40},{32,16},{40,24},{48,64},{56,72},{64,48},{72,56},{8... | collective-permute-start | bytes 159752 | tf_op jit(solution)/shard_map/ppermute | solution.py:587
  25.0 0.4 %collective-permute-done.6.refs_0_.refs_13_ = bf16[64,128]{1,0:T(8,128)(2,1)S(1)} collective-permute-done((bf16[64,128]{1,0:T(8,128)(2,1)S(1)}, bf16[64,128]{1,0:T(8,128)(2,1)S(1)}, u32[]{:S(2)}, u32[]{:S(2)}) %collective-permute-start.6) | collective-permute-done | bytes 16416 | tf_op jit(solution)/shard_map/ppermute | solution.py:586
  25.4 0.1 shard_map.152
  25.5 3.0 %collective-permute-start.7 = (s16[192,128]{1,0:T(8,128)(2,1)S(1)}, s16[192,128]{1,0:T(8,128)(2,1)S(1)}, u32[]{:S(2)}, u32[]{:S(2)}) collective-permute-start(s16[192,128]{1,0:T(8,128)(2,1)S(1)} %shard_map.152), channel_id=1, source_target_pairs={{0,16},{8,24},{16,0},{24,8},{32,48},{40,56},{48,32},{56,40},{64,80... | collective-permute-start | bytes 147464 | tf_op jit(solution)/shard_map/ppermute | solution.py:589
  28.5 3.5 %collective-permute-start.9 = (bf16[64,128]{1,0:T(8,128)(2,1)S(1)}, bf16[64,128]{1,0:T(8,128)(2,1)S(1)}, u32[]{:S(2)}, u32[]{:S(2)}) collective-permute-start(bf16[64,128]{1,0:T(8,128)(2,1)S(1)} %collective-permute-done.6.refs_0_.refs_13_), channel_id=1, source_target_pairs={{0,2},{2,4},{3,1},{4,6},{5,3},{7,5},{8,10},{10,12},{11,9},{12,14},... | collective-permute-start | bytes 49160 | tf_op jit(solution)/shard_map/ppermute | solution.py:590
  32.0 1.4 %shard_map.151 = (f32[64,16,128]{2,1,0:T(8,128)S(1)}, f32[2,64,16,128]{3,2,1,0:T(8,128)S(1)}, f32[1024,128]{1,0:T(8,128)S(1)}) custom-call(f32[64,16,128]{2,1,0:T(8,128)S(1)} %get-tuple-element.56.refs_0_.refs_3_, f32[2,64,16,128]{3,2,1,0:T(8,128)S(1)} %get-tuple-element.57.refs_1_, f32[64,16,128]{2,1,0:T(8,128)S(1)} %get-tuple-element.58.refs_2_, ...), custom_call_target="tpu_custom_call" | custom-call | tf_op jit(solution)/shard_map/pallas_call | solution.py:387
  33.4 0.7 %collective-permute-done.9.refs_14_ = bf16[64,128]{1,0:T(8,128)(2,1)S(1)} collective-permute-done((bf16[64,128]{1,0:T(8,128)(2,1)S(1)}, bf16[64,128]{1,0:T(8,128)(2,1)S(1)}, u32[]{:S(2)}, u32[]{:S(2)}) %collective-permute-start.9) | collective-permute-done | bytes 16416 | tf_op jit(solution)/shard_map/ppermute | solution.py:590
  34.1 0.0 collective-permute-done.7.refs_10_
  34.1 0.0 collective-permute-done.8.refs_11_
  34.1 1.6 %shard_map.154 = (f32[64,16,128]{2,1,0:T(8,128)}, f32[2,64,16,128]{3,2,1,0:T(8,128)}, f32[960,128]{1,0:T(8,128)}, f32[64,128]{1,0:T(8,128)}, f32[2,64,128]{2,1,0:T(8,128)}) custom-call(f32[64,16,128]{2,1,0:T(8,128)S(1)} %get-tuple-element.60.refs_0_, f32[2,64,16,128]{3,2,1,0:T(8,128)S(1)} %get-tuple-element.61.refs_1_, ...), custom_call_target="tpu_custom_call" | custom-call | tf_op jit(solution)/shard_map/pallas_call | solution.py:575
Async XLA Ops:
  5.5 2.1 %collective-permute-start = (f32[352,128]{1,0:T(8,128)S(1)}, f32[352,128]{1,0:T(8,128)S(1)}, u32[]{:S(2)}, u32[]{:S(2)}) collective-permute-start(f32[352,128]{1,0:T(8,128)S(1)} %get-tuple-element.50), channel_id=1, source_target_pairs={{0,8},{8,0},{16,24},{24,16},{32,40},{40,32},{48,56},{56,48},{64,72... | collective-permute-start | bytes 540680 | tf_op jit(solution)/shard_map/ppermute | solution.py:585
  5.6 4.5 %collective-permute-start.1 = (bf16[64,128]{1,0:T(8,128)(2,1)S(1)}, bf16[64,128]{1,0:T(8,128)(2,1)S(1)}, u32[]{:S(2)}, u32[]{:S(2)}) collective-permute-start(bf16[64,128]{1,0:T(8,128)(2,1)S(1)} %get-tuple-element.52), channel_id=1, source_target_pairs={{0,1},{1,0},{2,3},{3,2},{4,5},{5,4},{6,7},{7,6},{8,9},{9,8},{10,11... | collective-permute-start | bytes 49160 | tf_op jit(solution)/shard_map/ppermute | solution.py:586
  7.6 12.7 %collective-permute-start.3 = (s16[208,128]{1,0:T(8,128)(2,1)S(1)}, s16[208,128]{1,0:T(8,128)(2,1)S(1)}, u32[]{:S(2)}, u32[]{:S(2)}) collective-permute-start(s16[208,128]{1,0:T(8,128)(2,1)S(1)} %shard_map.149), channel_id=1, source_target_pairs={{16,32},{24,40},{32,16},{40,24},{48,64},{56,72},{64,48},{72,56},{8... | collective-permute-start | bytes 159752 | tf_op jit(solution)/shard_map/ppermute | solution.py:587
  10.2 10.2 %collective-permute-start.2 = (s16[192,128]{1,0:T(8,128)(2,1)S(1)}, s16[192,128]{1,0:T(8,128)(2,1)S(1)}, u32[]{:S(2)}, u32[]{:S(2)}) collective-permute-start(s16[192,128]{1,0:T(8,128)(2,1)S(1)} %shard_map.148), channel_id=1, source_target_pairs={{0,16},{8,24},{16,0},{24,8},{32,48},{40,56},{48,32},{56,40},{64,80... | collective-permute-start | bytes 147464 | tf_op jit(solution)/shard_map/ppermute | solution.py:589
  14.7 5.6 %collective-permute-start.4 = (bf16[64,128]{1,0:T(8,128)(2,1)S(1)}, bf16[64,128]{1,0:T(8,128)(2,1)S(1)}, u32[]{:S(2)}, u32[]{:S(2)}) collective-permute-start(bf16[64,128]{1,0:T(8,128)(2,1)S(1)} %collective-permute-done.1.refs_0_.refs_13_), channel_id=1, source_target_pairs={{0,2},{2,4},{3,1},{4,6},{5,3},{7,5},{8,10},{10,12},{11,9},{12,14},... | collective-permute-start | bytes 49160 | tf_op jit(solution)/shard_map/ppermute | solution.py:590
  21.5 1.5 %collective-permute-start.5 = (f32[352,128]{1,0:T(8,128)S(1)}, f32[352,128]{1,0:T(8,128)S(1)}, u32[]{:S(2)}, u32[]{:S(2)}) collective-permute-start(f32[352,128]{1,0:T(8,128)S(1)} %get-tuple-element.64), channel_id=1, source_target_pairs={{0,8},{8,0},{16,24},{24,16},{32,40},{40,32},{48,56},{56,48},{64,72... | collective-permute-start | bytes 540680 | tf_op jit(solution)/shard_map/ppermute | solution.py:585
  21.6 3.8 %collective-permute-start.6 = (bf16[64,128]{1,0:T(8,128)(2,1)S(1)}, bf16[64,128]{1,0:T(8,128)(2,1)S(1)}, u32[]{:S(2)}, u32[]{:S(2)}) collective-permute-start(bf16[64,128]{1,0:T(8,128)(2,1)S(1)} %get-tuple-element.66), channel_id=1, source_target_pairs={{0,1},{1,0},{2,3},{3,2},{4,5},{5,4},{6,7},{7,6},{8,9},{9,8},{10,11... | collective-permute-start | bytes 49160 | tf_op jit(solution)/shard_map/ppermute | solution.py:586
  23.1 11.1 %collective-permute-start.8 = (s16[208,128]{1,0:T(8,128)(2,1)S(1)}, s16[208,128]{1,0:T(8,128)(2,1)S(1)}, u32[]{:S(2)}, u32[]{:S(2)}) collective-permute-start(s16[208,128]{1,0:T(8,128)(2,1)S(1)} %shard_map.153), channel_id=1, source_target_pairs={{16,32},{24,40},{32,16},{40,24},{48,64},{56,72},{64,48},{72,56},{8... | collective-permute-start | bytes 159752 | tf_op jit(solution)/shard_map/ppermute | solution.py:587
  25.5 8.6 %collective-permute-start.7 = (s16[192,128]{1,0:T(8,128)(2,1)S(1)}, s16[192,128]{1,0:T(8,128)(2,1)S(1)}, u32[]{:S(2)}, u32[]{:S(2)}) collective-permute-start(s16[192,128]{1,0:T(8,128)(2,1)S(1)} %shard_map.152), channel_id=1, source_target_pairs={{0,16},{8,24},{16,0},{24,8},{32,48},{40,56},{48,32},{56,40},{64,80... | collective-permute-start | bytes 147464 | tf_op jit(solution)/shard_map/ppermute | solution.py:589
  28.5 5.6 %collective-permute-start.9 = (bf16[64,128]{1,0:T(8,128)(2,1)S(1)}, bf16[64,128]{1,0:T(8,128)(2,1)S(1)}, u32[]{:S(2)}, u32[]{:S(2)}) collective-permute-start(bf16[64,128]{1,0:T(8,128)(2,1)S(1)} %collective-permute-done.6.refs_0_.refs_13_), channel_id=1, source_target_pairs={{0,2},{2,4},{3,1},{4,6},{5,3},{7,5},{8,10},{10,12},{11,9},{12,14},... | collective-permute-start | bytes 49160 | tf_op jit(solution)/shard_map/ppermute | solution.py:590

commit v7 on v6

--- a/solution.py
+++ b/solution.py
@@ -468,17 +468,12 @@
         if last and (at + CHUNK) % (nodes // 2) == 0:
             half = pl.ds(at + CHUNK - nodes // 2, nodes // 2)
             send(shear.at[half], results[1].at[1, half])
-        if not last:
-            stress_new[0, cells] = stress[0, cells]
-            faces_new[cells] = faces[cells]
 
     first_row, last_row = stress[0, 0] + added_left, stress[0, nodes - 1] + added_right
     if last:
         tips[0], tips[1] = first_row, last_row
         send(tips.at[0], results[1].at[0, 0])
         send(tips.at[1], results[1].at[0, nodes - 1])
-    else:
-        stress_new[0, 0], stress_new[0, nodes - 1] = first_row, last_row
 
     row = lax.broadcasted_iota(jnp.int32, (nodes, width), 0)
     lower, upper = slice(fault, fault + 1), slice(fault + 1, fault + 2)
@@ -503,6 +498,7 @@
         send(state_new, results[3])
         send(bounds, results[4])
     else:
+        stress_new[0, 0], stress_new[0, nodes - 1] = first_row, last_row
         faces_new.reshape(nodes * ny, width)[pl.ds(fault, nodes, stride=ny), :] = clipped
 
     flat = velocity_new.reshape(nodes * ny, width)
@@ -575,6 +571,7 @@
     return pl.pallas_call(
         functools.partial(step_kernel, last),
         out_shape=out_shape,
+        input_output_aliases={} if last else {1: 1, 2: 2},
         out_specs=[pl.BlockSpec(memory_space=space)] * len(out_shape),
         scratch_shapes=scratch,
         compiler_params=pltpu.CompilerParams(vmem_limit_bytes=16 * MIB),

time: 36 us -> 36 us (level)
  no operation moved by 1% of the time
where the time goes in v7:
time: 36 us; the launch traced here: 35.8 us
  starting transfers between devices  22.2 us (62%)
  Pallas kernels  10.5 us (29%)
  waiting for transfers between devices  2.43 us (7%)
  between operations  0.75 us (2%)
    ppermute x2, starting transfers between devices, exchange(): near = lax.ppermute(near, GX, swap_pairs(GX, 2, 0))  7.55 us
    ppermute x2, starting transfers between devices, exchange(): depth_far = lax.ppermute(depth_near, GZ, onward_pairs(GZ))  6.94 us
    pallas_call x1, Pallas kernels, first_call(): pl.pallas_call(first_kernel, in_specs=[pl.BlockSpec(memory_space=pltpu.HB...  4.82 us
    ppermute x2, starting transfers between devices, exchange(): lax.ppermute(relay_call(False, received, own), GX, swap_pairs(GX, 2, 2))  4.36 us
    ppermute x2, starting transfers between devices, exchange(): depth_near = lax.ppermute(edges_sent, GZ, swap_pairs(GZ, 1, 0))  3.11 us
    pallas_call x2, Pallas kernels, step_call(): pl.pallas_call(functools.partial(step_kernel, last), out_shape=out_shape,...  2.86 us
    pallas_call x2, Pallas kernels, inner_call(): pl.pallas_call(functools.partial(inner_kernel, last), out_shape=[jax.Shap...  2.58 us
    ppermute x2, waiting for transfers between devices, exchange(): depth_far = lax.ppermute(depth_near, GZ, onward_pairs(GZ))  1.68 us
  transfers between devices with their start and end apart: 10, of which 4 were waited for; matrix products, arithmetic and copies ran while one was open for 0% of the time, Pallas kernels for 8%

profile of v7, /device:TPU:76, one launch (start us, length us, event | category | flops | bytes accessed | tf_op | source)
XLA Modules:
  0.0 35.8 jit_solution(18266364620247483776)
XLA Ops:
  0.6 4.8 %shard_map.146 = (f32[352,128]{1,0:T(8,128)S(1)}, f32[2,192,128]{2,1,0:T(8,128)S(1)}, f32[2,320,128]{2,1,0:T(8,128)S(1)}, bf16[2,320,64]{2,1,0:T(8,128)(2,1)S(1)...) custom-call(f32[64,16,128]{2,1,0:T(8,128)} %refs_0_.1, ...), custom_call_target="tpu_custom_call" | custom-call | tf_op jit(solution)/shard_map/pallas_call | solution.py:232
  5.5 0.1 collective-permute-start
  5.6 2.0 %collective-permute-start.1 = (bf16[64,128]{1,0:T(8,128)(2,1)S(1)}, bf16[64,128]{1,0:T(8,128)(2,1)S(1)}, u32[]{:S(2)}, u32[]{:S(2)}) collective-permute-start(bf16[64,128]{1,0:T(8,128)(2,1)S(1)} %get-tuple-element.52), channel_id=1, source_target_pairs={{0,1},{1,0},{2,3},{3,2},{4,5},{5,4},{6,7},{7,6},{8,9},{9,8},{10,11... | collective-permute-start | bytes 49160 | tf_op jit(solution)/shard_map/ppermute | solution.py:583
  7.6 0.0 collective-permute-done.received.refs_9_
  7.6 0.1 shard_map.149
  7.6 2.4 %collective-permute-start.3 = (s16[208,128]{1,0:T(8,128)(2,1)S(1)}, s16[208,128]{1,0:T(8,128)(2,1)S(1)}, u32[]{:S(2)}, u32[]{:S(2)}) collective-permute-start(s16[208,128]{1,0:T(8,128)(2,1)S(1)} %shard_map.149), channel_id=1, source_target_pairs={{16,32},{24,40},{32,16},{40,24},{48,64},{56,72},{64,48},{72,56},{8... | collective-permute-start | bytes 159752 | tf_op jit(solution)/shard_map/ppermute | solution.py:584
  10.1 0.0 collective-permute-done.1.refs_0_.refs_13_
  10.1 0.1 shard_map.148
  10.2 4.5 %collective-permute-start.2 = (s16[192,128]{1,0:T(8,128)(2,1)S(1)}, s16[192,128]{1,0:T(8,128)(2,1)S(1)}, u32[]{:S(2)}, u32[]{:S(2)}) collective-permute-start(s16[192,128]{1,0:T(8,128)(2,1)S(1)} %shard_map.148), channel_id=1, source_target_pairs={{0,16},{8,24},{16,0},{24,8},{32,48},{40,56},{48,32},{56,40},{64,80... | collective-permute-start | bytes 147464 | tf_op jit(solution)/shard_map/ppermute | solution.py:586
  14.7 3.5 %collective-permute-start.4 = (bf16[64,128]{1,0:T(8,128)(2,1)S(1)}, bf16[64,128]{1,0:T(8,128)(2,1)S(1)}, u32[]{:S(2)}, u32[]{:S(2)}) collective-permute-start(bf16[64,128]{1,0:T(8,128)(2,1)S(1)} %collective-permute-done.1.refs_0_.refs_13_), channel_id=1, source_target_pairs={{0,2},{2,4},{3,1},{4,6},{5,3},{7,5},{8,10},{10,12},{11,9},{12,14},... | collective-permute-start | bytes 49160 | tf_op jit(solution)/shard_map/ppermute | solution.py:587
  18.2 1.2 %shard_map.147 = (f32[64,16,128]{2,1,0:T(8,128)S(1)}, f32[2,64,16,128]{3,2,1,0:T(8,128)S(1)}, f32[64,16,128]{2,1,0:T(8,128)S(1)}, f32[64,16,128]{2,1,0:T(8,128)S(1)}) custom-call(f32[64,16,128]{2,1,0:T(8,128)S(1)} %get-tuple-element.39.refs_0_.refs_3_, f32[2,64,16,128]{3,2,1,0:T(8,128)S(1)} %get-tuple-element.40.refs_1_, ...), custom_call_target="tpu_custom_call" | custom-call | tf_op jit(solution)/shard_map/pallas_call | solution.py:387
  19.4 1.0 %collective-permute-done.4.refs_14_ = bf16[64,128]{1,0:T(8,128)(2,1)S(1)} collective-permute-done((bf16[64,128]{1,0:T(8,128)(2,1)S(1)}, bf16[64,128]{1,0:T(8,128)(2,1)S(1)}, u32[]{:S(2)}, u32[]{:S(2)}) %collective-permute-start.4) | collective-permute-done | bytes 16416 | tf_op jit(solution)/shard_map/ppermute | solution.py:587
  20.3 0.0 collective-permute-done.2.refs_10_
  20.3 0.0 collective-permute-done.3.refs_11_
  20.3 1.2 %shard_map.150 = (f32[64,16,128]{2,1,0:T(8,128)S(1)}, f32[2,64,16,128]{3,2,1,0:T(8,128)S(1)}, f32[64,16,128]{2,1,0:T(8,128)S(1)}, f32[64,128]{1,0:T(8,128)S(1)},...) custom-call(f32[64,16,128]{2,1,0:T(8,128)S(1)} %get-tuple-element.44, ...), custom_call_target="tpu_custom_call", output_to_operand_aliasing={{1}: (1, {}), {2}: (2, {})} | custom-call | tf_op jit(solution)/shard_map/pallas_call | solution.py:571
  21.6 0.1 collective-permute-start.5
  21.7 1.1 %collective-permute-start.6 = (bf16[64,128]{1,0:T(8,128)(2,1)S(1)}, bf16[64,128]{1,0:T(8,128)(2,1)S(1)}, u32[]{:S(2)}, u32[]{:S(2)}) collective-permute-start(bf16[64,128]{1,0:T(8,128)(2,1)S(1)} %get-tuple-element.66), channel_id=1, source_target_pairs={{0,1},{1,0},{2,3},{3,2},{4,5},{5,4},{6,7},{7,6},{8,9},{9,8},{10,11... | collective-permute-start | bytes 49160 | tf_op jit(solution)/shard_map/ppermute | solution.py:583
  22.8 0.3 collective-permute-done.5.received.refs_9_
  23.1 0.1 shard_map.153
  23.1 1.9 %collective-permute-start.8 = (s16[208,128]{1,0:T(8,128)(2,1)S(1)}, s16[208,128]{1,0:T(8,128)(2,1)S(1)}, u32[]{:S(2)}, u32[]{:S(2)}) collective-permute-start(s16[208,128]{1,0:T(8,128)(2,1)S(1)} %shard_map.153), channel_id=1, source_target_pairs={{16,32},{24,40},{32,16},{40,24},{48,64},{56,72},{64,48},{72,56},{8... | collective-permute-start | bytes 159752 | tf_op jit(solution)/shard_map/ppermute | solution.py:584
  25.1 0.4 %collective-permute-done.6.refs_0_.refs_13_ = bf16[64,128]{1,0:T(8,128)(2,1)S(1)} collective-permute-done((bf16[64,128]{1,0:T(8,128)(2,1)S(1)}, bf16[64,128]{1,0:T(8,128)(2,1)S(1)}, u32[]{:S(2)}, u32[]{:S(2)}) %collective-permute-start.6) | collective-permute-done | bytes 16416 | tf_op jit(solution)/shard_map/ppermute | solution.py:583
  25.5 0.1 shard_map.152
  25.5 3.0 %collective-permute-start.7 = (s16[192,128]{1,0:T(8,128)(2,1)S(1)}, s16[192,128]{1,0:T(8,128)(2,1)S(1)}, u32[]{:S(2)}, u32[]{:S(2)}) collective-permute-start(s16[192,128]{1,0:T(8,128)(2,1)S(1)} %shard_map.152), channel_id=1, source_target_pairs={{0,16},{8,24},{16,0},{24,8},{32,48},{40,56},{48,32},{56,40},{64,80... | collective-permute-start | bytes 147464 | tf_op jit(solution)/shard_map/ppermute | solution.py:586
  28.6 3.5 %collective-permute-start.9 = (bf16[64,128]{1,0:T(8,128)(2,1)S(1)}, bf16[64,128]{1,0:T(8,128)(2,1)S(1)}, u32[]{:S(2)}, u32[]{:S(2)}) collective-permute-start(bf16[64,128]{1,0:T(8,128)(2,1)S(1)} %collective-permute-done.6.refs_0_.refs_13_), channel_id=1, source_target_pairs={{0,2},{2,4},{3,1},{4,6},{5,3},{7,5},{8,10},{10,12},{11,9},{12,14},... | collective-permute-start | bytes 49160 | tf_op jit(solution)/shard_map/ppermute | solution.py:587
  32.0 1.4 %shard_map.151 = (f32[64,16,128]{2,1,0:T(8,128)S(1)}, f32[2,64,16,128]{3,2,1,0:T(8,128)S(1)}, f32[1024,128]{1,0:T(8,128)S(1)}) custom-call(f32[64,16,128]{2,1,0:T(8,128)S(1)} %get-tuple-element.56.refs_0_.refs_3_, f32[2,64,16,128]{3,2,1,0:T(8,128)S(1)} %get-tuple-element.57.refs_1_, f32[64,16,128]{2,1,0:T(8,128)S(1)} %get-tuple-element.58.refs_2_, ...), custom_call_target="tpu_custom_call" | custom-call | tf_op jit(solution)/shard_map/pallas_call | solution.py:387
  33.5 0.7 %collective-permute-done.9.refs_14_ = bf16[64,128]{1,0:T(8,128)(2,1)S(1)} collective-permute-done((bf16[64,128]{1,0:T(8,128)(2,1)S(1)}, bf16[64,128]{1,0:T(8,128)(2,1)S(1)}, u32[]{:S(2)}, u32[]{:S(2)}) %collective-permute-start.9) | collective-permute-done | bytes 16416 | tf_op jit(solution)/shard_map/ppermute | solution.py:587
  34.2 0.0 collective-permute-done.7.refs_10_
  34.2 0.0 collective-permute-done.8.refs_11_
  34.2 1.6 %shard_map.154 = (f32[64,16,128]{2,1,0:T(8,128)}, f32[2,64,16,128]{3,2,1,0:T(8,128)}, f32[960,128]{1,0:T(8,128)}, f32[64,128]{1,0:T(8,128)}, f32[2,64,128]{2,1,0:T(8,128)}) custom-call(f32[64,16,128]{2,1,0:T(8,128)S(1)} %get-tuple-element.60.refs_0_, f32[2,64,16,128]{3,2,1,0:T(8,128)S(1)} %get-tuple-element.61.refs_1_, ...), custom_call_target="tpu_custom_call" | custom-call | tf_op jit(solution)/shard_map/pallas_call | solution.py:571
Async XLA Ops:
  5.5 2.1 %collective-permute-start = (f32[352,128]{1,0:T(8,128)S(1)}, f32[352,128]{1,0:T(8,128)S(1)}, u32[]{:S(2)}, u32[]{:S(2)}) collective-permute-start(f32[352,128]{1,0:T(8,128)S(1)} %get-tuple-element.50), channel_id=1, source_target_pairs={{0,8},{8,0},{16,24},{24,16},{32,40},{40,32},{48,56},{56,48},{64,72... | collective-permute-start | bytes 540680 | tf_op jit(solution)/shard_map/ppermute | solution.py:582
  5.6 4.5 %collective-permute-start.1 = (bf16[64,128]{1,0:T(8,128)(2,1)S(1)}, bf16[64,128]{1,0:T(8,128)(2,1)S(1)}, u32[]{:S(2)}, u32[]{:S(2)}) collective-permute-start(bf16[64,128]{1,0:T(8,128)(2,1)S(1)} %get-tuple-element.52), channel_id=1, source_target_pairs={{0,1},{1,0},{2,3},{3,2},{4,5},{5,4},{6,7},{7,6},{8,9},{9,8},{10,11... | collective-permute-start | bytes 49160 | tf_op jit(solution)/shard_map/ppermute | solution.py:583
  7.6 12.7 %collective-permute-start.3 = (s16[208,128]{1,0:T(8,128)(2,1)S(1)}, s16[208,128]{1,0:T(8,128)(2,1)S(1)}, u32[]{:S(2)}, u32[]{:S(2)}) collective-permute-start(s16[208,128]{1,0:T(8,128)(2,1)S(1)} %shard_map.149), channel_id=1, source_target_pairs={{16,32},{24,40},{32,16},{40,24},{48,64},{56,72},{64,48},{72,56},{8... | collective-permute-start | bytes 159752 | tf_op jit(solution)/shard_map/ppermute | solution.py:584
  10.2 10.2 %collective-permute-start.2 = (s16[192,128]{1,0:T(8,128)(2,1)S(1)}, s16[192,128]{1,0:T(8,128)(2,1)S(1)}, u32[]{:S(2)}, u32[]{:S(2)}) collective-permute-start(s16[192,128]{1,0:T(8,128)(2,1)S(1)} %shard_map.148), channel_id=1, source_target_pairs={{0,16},{8,24},{16,0},{24,8},{32,48},{40,56},{48,32},{56,40},{64,80... | collective-permute-start | bytes 147464 | tf_op jit(solution)/shard_map/ppermute | solution.py:586
  14.7 5.6 %collective-permute-start.4 = (bf16[64,128]{1,0:T(8,128)(2,1)S(1)}, bf16[64,128]{1,0:T(8,128)(2,1)S(1)}, u32[]{:S(2)}, u32[]{:S(2)}) collective-permute-start(bf16[64,128]{1,0:T(8,128)(2,1)S(1)} %collective-permute-done.1.refs_0_.refs_13_), channel_id=1, source_target_pairs={{0,2},{2,4},{3,1},{4,6},{5,3},{7,5},{8,10},{10,12},{11,9},{12,14},... | collective-permute-start | bytes 49160 | tf_op jit(solution)/shard_map/ppermute | solution.py:587
  21.6 1.5 %collective-permute-start.5 = (f32[352,128]{1,0:T(8,128)S(1)}, f32[352,128]{1,0:T(8,128)S(1)}, u32[]{:S(2)}, u32[]{:S(2)}) collective-permute-start(f32[352,128]{1,0:T(8,128)S(1)} %get-tuple-element.64), channel_id=1, source_target_pairs={{0,8},{8,0},{16,24},{24,16},{32,40},{40,32},{48,56},{56,48},{64,72... | collective-permute-start | bytes 540680 | tf_op jit(solution)/shard_map/ppermute | solution.py:582
  21.7 3.8 %collective-permute-start.6 = (bf16[64,128]{1,0:T(8,128)(2,1)S(1)}, bf16[64,128]{1,0:T(8,128)(2,1)S(1)}, u32[]{:S(2)}, u32[]{:S(2)}) collective-permute-start(bf16[64,128]{1,0:T(8,128)(2,1)S(1)} %get-tuple-element.66), channel_id=1, source_target_pairs={{0,1},{1,0},{2,3},{3,2},{4,5},{5,4},{6,7},{7,6},{8,9},{9,8},{10,11... | collective-permute-start | bytes 49160 | tf_op jit(solution)/shard_map/ppermute | solution.py:583
  23.1 11.1 %collective-permute-start.8 = (s16[208,128]{1,0:T(8,128)(2,1)S(1)}, s16[208,128]{1,0:T(8,128)(2,1)S(1)}, u32[]{:S(2)}, u32[]{:S(2)}) collective-permute-start(s16[208,128]{1,0:T(8,128)(2,1)S(1)} %shard_map.153), channel_id=1, source_target_pairs={{16,32},{24,40},{32,16},{40,24},{48,64},{56,72},{64,48},{72,56},{8... | collective-permute-start | bytes 159752 | tf_op jit(solution)/shard_map/ppermute | solution.py:584
  25.5 8.6 %collective-permute-start.7 = (s16[192,128]{1,0:T(8,128)(2,1)S(1)}, s16[192,128]{1,0:T(8,128)(2,1)S(1)}, u32[]{:S(2)}, u32[]{:S(2)}) collective-permute-start(s16[192,128]{1,0:T(8,128)(2,1)S(1)} %shard_map.152), channel_id=1, source_target_pairs={{0,16},{8,24},{16,0},{24,8},{32,48},{40,56},{48,32},{56,40},{64,80... | collective-permute-start | bytes 147464 | tf_op jit(solution)/shard_map/ppermute | solution.py:586
  28.6 5.6 %collective-permute-start.9 = (bf16[64,128]{1,0:T(8,128)(2,1)S(1)}, bf16[64,128]{1,0:T(8,128)(2,1)S(1)}, u32[]{:S(2)}, u32[]{:S(2)}) collective-permute-start(bf16[64,128]{1,0:T(8,128)(2,1)S(1)} %collective-permute-done.6.refs_0_.refs_13_), channel_id=1, source_target_pairs={{0,2},{2,4},{3,1},{4,6},{5,3},{7,5},{8,10},{10,12},{11,9},{12,14},... | collective-permute-start | bytes 49160 | tf_op jit(solution)/shard_map/ppermute | solution.py:587
